TPU v7x, 512 devices: a whole 4x8x8 slice. The times are simulated.
512 devices in a mesh: inline: 32 (over y, z_hi, core), freq: 16 (over x, z_lo).
Axes of the slice: x: 4, y: 8, z: 8 (z_hi: 2, z_lo: 4; z = z_hi * 4 + z_lo), core: 2. Of those that a mesh axis runs over, the one named last changes fastest.
Arguments:
- traces_in: float32 [2048, 128, 128], P('freq', 'inline'), may hold values from -6 to 6
- reweights: float32 [2, 1024, 128, 128], P(None, 'freq', 'inline'), may hold values from 0.1 to 10
- live_mask: int32 [128, 128], P('inline'), may hold values 0 or 1
Outputs:
- denoised: float32 [2048, 128, 128], P('freq', 'inline')
All inputs are finite; a program needn't handle non-finite values. No bound on the sum of `live_mask` on one device may be relied on, other than what follows from the above.
Results may differ from a plain program's by a relative error of at most 0.0003.
Values sent between devices are 32-bit elements; how exact they have to be, the bound alone decides.
No kernel may reach another device: no remote copies, remote signals or barrier semaphores. Data moves between devices by JAX's collectives and lax.ppermute only.
A program may use at most 64 MiB of HBM per device.

v0:
```python
import math

import jax
import jax.numpy as jnp
from jax import lax
from jax.sharding import PartitionSpec as P

NT = 2048
NF = 1024
FILT = 4
WI = 4
WX = 32
ITERS = 2


highest = lax.Precision.HIGHEST


def padded_2(cells, sides, width):
    for axis, dim in sides:
        count = lax.axis_size(axis)
        ends = count - 1
        head = lax.slice_in_dim(cells, 0, width, axis=dim)
        tail = lax.slice_in_dim(cells, cells.shape[dim] - width, cells.shape[dim], axis=dim)
        cells = jnp.concatenate(
            [
                lax.ppermute(tail, axis, [(i, (i + 1) % count) for i in range(ends)]),
                cells,
                lax.ppermute(head, axis, [((i + 1) % count, i) for i in range(ends)]),
            ],
            axis=dim,
        )
    return cells


def cholesky_solve(normal_matrix, target):
    system_size = len(target)
    trace_sum = sum((normal_matrix[column][column] for column in range(system_size)))
    ridge_value = 0.05 * trace_sum / system_size + 1e-05
    factor = {}
    for column in range(system_size):
        diagonal_term = normal_matrix[column][column] + ridge_value
        for inner_index in range(column):
            diagonal_term = (
                diagonal_term - factor[column, inner_index] * factor[column, inner_index]
            )
        pivot_value = jnp.sqrt(diagonal_term)
        factor[column, column] = pivot_value
        for below_row in range(column + 1, system_size):
            entry_value = normal_matrix[below_row][column]
            for inner_index in range(column):
                entry_value = (
                    entry_value - factor[below_row, inner_index] * factor[column, inner_index]
                )
            factor[below_row, column] = entry_value / pivot_value
    forward_values = []
    for column in range(system_size):
        entry_value = target[column]
        for inner_index in range(column):
            entry_value = entry_value - factor[column, inner_index] * forward_values[inner_index]
        forward_values.append(entry_value / factor[column, column])
    solution_list = [None] * system_size
    for column in reversed(range(system_size)):
        entry_value = forward_values[column]
        for inner_index in range(column + 1, system_size):
            entry_value = entry_value - factor[inner_index, column] * solution_list[inner_index]
        solution_list[column] = entry_value / factor[column, column]
    return solution_list


def filter_step(padded, weights_now, live_weight):
    freq_count = padded.shape[0]
    inline_rows = padded.shape[2] - 2 * FILT
    crosslines = padded.shape[3]
    real_part = padded[:, 0]
    imag_part = padded[:, 1]

    def shifted(values, offset):
        return values[:, FILT + offset : FILT + offset + inline_rows]

    def tiled(values):
        return values.reshape(freq_count, inline_rows // WI, WI, crosslines // WX, WX)

    def window_sum(values):
        return jnp.sum(tiled(values), axis=(2, 4))

    weighted = weights_now * live_weight[None]
    target_real = shifted(real_part, 0)
    target_imag = shifted(imag_part, 0)
    predicted_real = jnp.zeros(tiled(target_real).shape, jnp.float32)
    predicted_imag = jnp.zeros(tiled(target_real).shape, jnp.float32)
    for direction in (-1, 1):
        lag_real = [shifted(real_part, direction * lag_step) for lag_step in range(1, FILT + 1)]
        lag_imag = [shifted(imag_part, direction * lag_step) for lag_step in range(1, FILT + 1)]
        cross_real = {}
        cross_imag = {}
        for first in range(FILT):
            for second in range(first, FILT):
                cross_real[first, second] = window_sum(
                    weighted
                    * (lag_real[first] * lag_real[second] + lag_imag[first] * lag_imag[second])
                )
                if second > first:
                    cross_imag[first, second] = window_sum(
                        weighted
                        * (lag_real[first] * lag_imag[second] - lag_imag[first] * lag_real[second])
                    )
        zero_block = jnp.zeros_like(cross_real[0, 0])

        def real_entry(first, second):
            return cross_real[min(first, second), max(first, second)]

        def imag_entry(first, second):
            if first == second:
                return zero_block
            if first < second:
                return cross_imag[first, second]
            return -cross_imag[second, first]

        normal_matrix = [[None] * (2 * FILT) for _ in range(2 * FILT)]
        for first in range(FILT):
            for second in range(FILT):
                normal_matrix[first][second] = real_entry(first, second)
                normal_matrix[FILT + first][FILT + second] = real_entry(first, second)
                normal_matrix[first][FILT + second] = -imag_entry(first, second)
                normal_matrix[FILT + first][second] = imag_entry(first, second)
        target = [None] * (2 * FILT)
        for first in range(FILT):
            target[first] = window_sum(
                weighted * (lag_real[first] * target_real + lag_imag[first] * target_imag)
            )
            target[FILT + first] = window_sum(
                weighted * (lag_real[first] * target_imag - lag_imag[first] * target_real)
            )
        solution_list = cholesky_solve(normal_matrix, target)
        for lag_index in range(FILT):
            coef_real = solution_list[lag_index][:, :, None, :, None]
            coef_imag = solution_list[FILT + lag_index][:, :, None, :, None]
            block_real = tiled(lag_real[lag_index])
            block_imag = tiled(lag_imag[lag_index])
            predicted_real = predicted_real + (coef_real * block_real - coef_imag * block_imag)
            predicted_imag = predicted_imag + (coef_real * block_imag + coef_imag * block_real)
    scale_live = 0.5 * live_weight[None]
    new_real = predicted_real.reshape(freq_count, inline_rows, crosslines) * scale_live
    new_imag = predicted_imag.reshape(freq_count, inline_rows, crosslines) * scale_live
    return jnp.stack([new_real, new_imag], axis=1)


def forward_twiddle(freq_count, time_start, time_count):
    freq_index = lax.iota(jnp.int32, freq_count)
    time_index = time_start + lax.iota(jnp.int32, time_count)
    phases = freq_index[:, None] * time_index[None, :] % NT
    angles = phases.astype(jnp.float32) * (2.0 * math.pi / NT)
    return jnp.stack([jnp.cos(angles), -jnp.sin(angles)], axis=1).reshape(
        2 * freq_count, time_count
    )


def inverse_twiddle(time_start, time_count):
    time_index = time_start + lax.iota(jnp.int32, time_count)
    freq_index = lax.iota(jnp.int32, NF)
    phases = time_index[:, None] * freq_index[None, :] % NT
    angles = phases.astype(jnp.float32) * (2.0 * math.pi / NT)
    scaling = jnp.where(freq_index == 0, 1.0, 2.0).astype(jnp.float32) / NT
    return jnp.stack([jnp.cos(angles) * scaling, -jnp.sin(angles) * scaling], axis=2).reshape(
        time_count, 2 * NF
    )


def local(traces_in, reweights, live_mask):
    time_rows, inline_rows, crosslines = traces_in.shape
    freq_rows = reweights.shape[1]
    traces = inline_rows * crosslines
    live_weight = live_mask.astype(jnp.float32)
    signal = (traces_in * live_weight[None]).reshape(time_rows, traces)
    time_start = lax.axis_index("freq") * time_rows
    twiddle = forward_twiddle(lax.axis_size("freq") * freq_rows, time_start, time_rows)
    product = jnp.dot(twiddle, signal, precision=highest, preferred_element_type=jnp.float32)
    spectra = lax.psum_scatter(
        product.reshape(lax.axis_size("freq") * freq_rows, 2 * traces),
        "freq",
        scatter_dimension=0,
        tiled=True,
    ).reshape(freq_rows, 2, traces)
    current = spectra.reshape(freq_rows, 2, inline_rows, crosslines)
    for iteration in range(ITERS):
        padded = padded_2(current, (("inline", 2),), FILT)
        current = filter_step(padded, reweights[iteration], live_weight)
    spread_bins = lax.all_to_all(
        current.reshape(freq_rows, 2, traces), "freq", split_axis=2, concat_axis=0, tiled=True
    )
    stacked_bins = spread_bins.reshape(2 * NF, spread_bins.shape[2])
    time_block = math.gcd(NT, 256)

    def rebuild_block(block_index):
        twiddle = inverse_twiddle(block_index * time_block, time_block)
        return jnp.dot(twiddle, stacked_bins, precision=highest, preferred_element_type=jnp.float32)

    rebuilt = lax.map(rebuild_block, jnp.arange(NT // time_block, dtype=jnp.int32)).reshape(
        NT, stacked_bins.shape[1]
    )
    time_local = lax.all_to_all(rebuilt, "freq", split_axis=0, concat_axis=1, tiled=True)
    return time_local.reshape(time_rows, inline_rows, crosslines)


def solution(mesh):
    in_specs = (P("freq", "inline", None), P(None, "freq", "inline", None), P("inline", None))
    out_specs = P("freq", "inline", None)
    return jax.shard_map(local, mesh=mesh, in_specs=in_specs, out_specs=out_specs, check_vma=False)
```

profile of v0, /device:TPU:41, one launch (start us, length us, event | category | flops | bytes accessed | tf_op | source)
XLA Modules:
  0.0 349.9 jit_solution(6488272190068525484)
XLA Ops:
  7.2 2.1 fusion.15
  10.3 5.0 %fusion.12 = f32[2048,512]{1,0:T(8,128)} fusion(f32[2048,128]{1,0:T(8,128)S(1)} %bitcast.473, f32[16,8,4,128]{3,2,1,0:T(4,128)S(1)} %bitcast.479), kind=kOutput, calls=%fused_computation.34 | convolution fusion | flops 1610612736 | bytes 5505024 | tf_op jit(solution)/shard_map/dot_general | solution.py:178
  15.2 5.2 %reshape.6291 = f32[1024,1024]{1,0:T(8,128)} reshape(f32[2048,512]{1,0:T(8,128)} %fusion.12) | data formatting | bytes 8388608 | tf_op jit(solution)/shard_map/reshape | solution.py:180
  20.5 107.2 %reduce-scatter.2.cloned.1.call-done = f32[64,1024]{1,0:T(8,128)} async-done(((f32[1024,1024]{1,0:T(8,128)}), f32[64,1024]{1,0:T(8,128)}) %reduce-scatter.2.cloned.1.call-update) | async-done | bytes 262160 | tf_op jit(solution)/shard_map/reduce_scatter | solution.py:179
  128.8 10.3 %collective-permute-start = (f32[64,2,4,128]{3,2,1,0:T(4,128)S(1)}, f32[64,2,4,128]{3,2,1,0:T(4,128)S(1)}, u32[]{:S(2)}, u32[]{:S(2)}) collective-permute-start(f32[64,2,4,128]{3,2,1,0:T(4,128)S(1)} %reshape_reshape.3), channel_id=1, source_target_pairs={{0,16},{16,32},{32,48},{48,64},{64,80},{80,96},{96,112},{112,128},... | collective-permute-start | bytes 786440 | tf_op jit(solution)/shard_map/ppermute | solution.py:27
  139.2 2.1 collective-permute-start.1
  141.3 2.6 collective-permute-done
  143.9 8.1 %collective-permute-done.1 = f32[64,2,4,128]{3,2,1,0:T(4,128)S(1)} collective-permute-done((f32[64,2,4,128]{3,2,1,0:T(4,128)S(1)}, f32[64,2,4,128]{3,2,1,0:T(4,128)S(1)}, u32[]{:S(2)}, u32[]{:S(2)}) %collective-permute-start.1) | collective-permute-done | bytes 262176 | tf_op jit(solution)/shard_map/ppermute | solution.py:29
  172.0 1.9 collective-permute-start.2
  173.9 2.6 collective-permute-start.3
  176.5 1.7 collective-permute-done.2
  178.2 10.9 %collective-permute-done.3 = f32[64,2,4,128]{3,2,0,1:T(4,128)S(1)} collective-permute-done((f32[64,2,4,128]{3,2,0,1:T(4,128)S(1)}, f32[64,2,4,128]{3,2,0,1:T(4,128)S(1)}, u32[]{:S(2)}, u32[]{:S(2)}) %collective-permute-start.3) | collective-permute-done | bytes 262176 | tf_op jit(solution)/shard_map/ppermute | solution.py:29
  207.6 5.3 %all-to-all-start = ((f32[16,1,4096]{2,1,0:T(1,128)}), f32[16,1,4096]{2,1,0:T(1,128)S(1)}, u32[]{:S(2)}, u32[]{:S(2)}) async-start(f32[16,1,4096]{2,1,0:T(1,128)} %reshape.6294), calls=%async_computation.1 | async-start | bytes 524288 | tf_op jit(solution)/shard_map/all_to_all | solution.py:189
  212.9 9.0 %all-to-all-done = f32[16,1,4096]{2,1,0:T(1,128)S(1)} async-done(((f32[16,1,4096]{2,1,0:T(1,128)}), f32[16,1,4096]{2,1,0:T(1,128)S(1)}, u32[]{:S(2)}, u32[]{:S(2)}) %all-to-all-start) | async-done | bytes 262176 | tf_op jit(solution)/shard_map/all_to_all | solution.py:189
  224.7 103.8 %while.12 = (s32[]{:T(128)}, f32[8,256,32]{1,0,2:T(8,128)S(1)}, s32[8]{0:T(128)S(1)}, f32[2048,32]{1,0:T(8,128)S(1)}, s32[]{:T(128)}, /*index=5*/s32[1]{0:T(128)}, s32[]{:T(128)}) while((s32[]{:T(128)}, f32[8,256,32]{1,0,2:T(8,128)S(1)}, s32[8]{0:T(128)S(1)}, f32[2048,32]{1,0:T(8,128)S(1)}, s32[]{:T(128)}, /*index=5*/s32[1]{0:T(128)}, ...), condition=%wide.region_194.195_spmd, body=%wide.region_193.194_spmd.sunk | while | flops 206310656 | bytes 17213548 | solution.py:199
  226.0 4.3 %cosine_multiply_fusion.2 = (f32[256,1024,1]{1,0,2:T(8,128)S(1)}, f32[256,1024,1]{1,0,2:T(8,128)S(1)}) fusion(f32[1024]{0:T(1024)S(1)} %select_multiply_fusion.2, s32[256]{0:T(256)S(1)} %iota_add_fusion.3), kind=kLoop, calls=%fused_computation.9.clone.1 | loop fusion | flops 4456448 | bytes 2102272 | tf_op jit(solution)/shard_map/while/body/eval_jaxpr/mul | solution.py:165
  230.5 2.4 copy.696
  232.9 2.7 reshape.6297
  235.6 1.9 convolution_bitcast_fusion.2
  239.0 4.3 %cosine_multiply_fusion.2 = (f32[256,1024,1]{1,0,2:T(8,128)S(1)}, f32[256,1024,1]{1,0,2:T(8,128)S(1)}) fusion(f32[1024]{0:T(1024)S(1)} %select_multiply_fusion.2, s32[256]{0:T(256)S(1)} %iota_add_fusion.3), kind=kLoop, calls=%fused_computation.9.clone.1 | loop fusion | flops 4456448 | bytes 2102272 | tf_op jit(solution)/shard_map/while/body/eval_jaxpr/mul | solution.py:165
  243.5 2.4 copy.696
  245.9 2.7 reshape.6297
  248.6 1.9 convolution_bitcast_fusion.2
  252.0 4.3 %cosine_multiply_fusion.2 = (f32[256,1024,1]{1,0,2:T(8,128)S(1)}, f32[256,1024,1]{1,0,2:T(8,128)S(1)}) fusion(f32[1024]{0:T(1024)S(1)} %select_multiply_fusion.2, s32[256]{0:T(256)S(1)} %iota_add_fusion.3), kind=kLoop, calls=%fused_computation.9.clone.1 | loop fusion | flops 4456448 | bytes 2102272 | tf_op jit(solution)/shard_map/while/body/eval_jaxpr/mul | solution.py:165
  256.5 2.4 copy.696
  258.9 2.7 reshape.6297
  261.6 1.9 convolution_bitcast_fusion.2
  264.9 4.3 %cosine_multiply_fusion.2 = (f32[256,1024,1]{1,0,2:T(8,128)S(1)}, f32[256,1024,1]{1,0,2:T(8,128)S(1)}) fusion(f32[1024]{0:T(1024)S(1)} %select_multiply_fusion.2, s32[256]{0:T(256)S(1)} %iota_add_fusion.3), kind=kLoop, calls=%fused_computation.9.clone.1 | loop fusion | flops 4456448 | bytes 2102272 | tf_op jit(solution)/shard_map/while/body/eval_jaxpr/mul | solution.py:165
  269.5 2.4 copy.696
  271.8 2.7 reshape.6297
  274.5 1.9 convolution_bitcast_fusion.2
  277.9 4.3 %cosine_multiply_fusion.2 = (f32[256,1024,1]{1,0,2:T(8,128)S(1)}, f32[256,1024,1]{1,0,2:T(8,128)S(1)}) fusion(f32[1024]{0:T(1024)S(1)} %select_multiply_fusion.2, s32[256]{0:T(256)S(1)} %iota_add_fusion.3), kind=kLoop, calls=%fused_computation.9.clone.1 | loop fusion | flops 4456448 | bytes 2102272 | tf_op jit(solution)/shard_map/while/body/eval_jaxpr/mul | solution.py:165
  282.5 2.4 copy.696
  284.8 2.7 reshape.6297
  287.5 1.9 convolution_bitcast_fusion.2
  290.9 4.3 %cosine_multiply_fusion.2 = (f32[256,1024,1]{1,0,2:T(8,128)S(1)}, f32[256,1024,1]{1,0,2:T(8,128)S(1)}) fusion(f32[1024]{0:T(1024)S(1)} %select_multiply_fusion.2, s32[256]{0:T(256)S(1)} %iota_add_fusion.3), kind=kLoop, calls=%fused_computation.9.clone.1 | loop fusion | flops 4456448 | bytes 2102272 | tf_op jit(solution)/shard_map/while/body/eval_jaxpr/mul | solution.py:165
  295.4 2.4 copy.696
  297.8 2.7 reshape.6297
  300.5 1.9 convolution_bitcast_fusion.2
  303.9 4.3 %cosine_multiply_fusion.2 = (f32[256,1024,1]{1,0,2:T(8,128)S(1)}, f32[256,1024,1]{1,0,2:T(8,128)S(1)}) fusion(f32[1024]{0:T(1024)S(1)} %select_multiply_fusion.2, s32[256]{0:T(256)S(1)} %iota_add_fusion.3), kind=kLoop, calls=%fused_computation.9.clone.1 | loop fusion | flops 4456448 | bytes 2102272 | tf_op jit(solution)/shard_map/while/body/eval_jaxpr/mul | solution.py:165
  308.4 2.4 copy.696
  310.8 2.7 reshape.6297
  313.5 1.9 convolution_bitcast_fusion.2
  316.9 4.3 %cosine_multiply_fusion.2 = (f32[256,1024,1]{1,0,2:T(8,128)S(1)}, f32[256,1024,1]{1,0,2:T(8,128)S(1)}) fusion(f32[1024]{0:T(1024)S(1)} %select_multiply_fusion.2, s32[256]{0:T(256)S(1)} %iota_add_fusion.3), kind=kLoop, calls=%fused_computation.9.clone.1 | loop fusion | flops 4456448 | bytes 2102272 | tf_op jit(solution)/shard_map/while/body/eval_jaxpr/mul | solution.py:165
  321.4 2.4 copy.696
  323.8 2.7 reshape.6297
  326.5 1.9 convolution_bitcast_fusion.2
  328.7 13.1 %all_to_all.31 = f32[16,128,32]{1,2,0:T(8,128)S(1)} all-to-all(f32[16,128,32]{1,2,0:T(8,128)S(1)} %copy.490), channel_id=1, replica_groups=mesh['inline'=32,'freq'=16] {'freq'}, dimensions={0} | all-to-all | bytes 524288 | tf_op jit(solution)/shard_map/all_to_all | solution.py:202
  (359 shorter events, 51.8 us)
Async XLA Ops:
  6.5 121.2 %reduce-scatter.2.cloned.1.call-start = ((), (), s32[]{:S(2)}) async-start(), calls=%async_computation.3 | async-start | bytes 4456448 | tf_op jit(solution)/shard_map/reduce_scatter | solution.py:179
  9.3 1.0 copy-start.1
  20.5 120.8 %copy-start.4 = (s32[4,128]{1,0:T(4,128)S(1)}, s32[4,128]{1,0:T(4,128)}, u32[]{:S(2)}) copy-start(s32[4,128]{1,0:T(4,128)} %param.7) | copy-start | bytes 6148
  128.8 23.5 %copy-start = (f32[2,64,4,128]{3,2,1,0:T(4,128)S(1)}, f32[2,64,4,128]{3,2,1,0:T(4,128)}, u32[]{:S(2)}) copy-start(f32[2,64,4,128]{3,2,1,0:T(4,128)} %param.6) | copy-start | bytes 786436
  128.8 15.1 %collective-permute-start = (f32[64,2,4,128]{3,2,1,0:T(4,128)S(1)}, f32[64,2,4,128]{3,2,1,0:T(4,128)S(1)}, u32[]{:S(2)}, u32[]{:S(2)}) collective-permute-start(f32[64,2,4,128]{3,2,1,0:T(4,128)S(1)} %reshape_reshape.3), channel_id=1, source_target_pairs={{0,16},{16,32},{32,48},{48,64},{64,80},{80,96},{96,112},{112,128},... | collective-permute-start | bytes 786440 | tf_op jit(solution)/shard_map/ppermute | solution.py:27
  139.2 12.8 %collective-permute-start.1 = (f32[64,2,4,128]{3,2,1,0:T(4,128)S(1)}, f32[64,2,4,128]{3,2,1,0:T(4,128)S(1)}, u32[]{:S(2)}, u32[]{:S(2)}) collective-permute-start(f32[64,2,4,128]{3,2,1,0:T(4,128)S(1)} %reshape_reshape.3), channel_id=1, source_target_pairs={{16,0},{32,16},{48,32},{64,48},{80,64},{96,80},{112,96},{128,112},... | collective-permute-start | bytes 786440 | tf_op jit(solution)/shard_map/ppermute | solution.py:29
  162.6 5.3 %copy-start.3 = (f32[64,128]{1,0:T(8,128)S(1)}, f32[64,128]{1,0:T(8,128)}, u32[]{:S(2)}) copy-start(f32[64,128]{1,0:T(8,128)} %get-tuple-element.368) | copy-start | bytes 98308
  162.7 5.8 %copy-start.2 = (f32[64,128]{1,0:T(8,128)S(1)}, f32[64,128]{1,0:T(8,128)}, u32[]{:S(2)}) copy-start(f32[64,128]{1,0:T(8,128)} %get-tuple-element.146) | copy-start | bytes 98308
  172.0 6.3 %collective-permute-start.2 = (f32[64,2,4,128]{3,2,0,1:T(4,128)S(1)}, f32[64,2,4,128]{3,2,0,1:T(4,128)S(1)}, u32[]{:S(2)}, u32[]{:S(2)}) collective-permute-start(f32[64,2,4,128]{3,2,0,1:T(4,128)S(1)} %pad_maximum_fusion.5), channel_id=1, source_target_pairs={{0,16},{16,32},{32,48},{48,64},{64,80},{80,96},{96,112},{112,128},... | collective-permute-start | bytes 786440 | tf_op jit(solution)/shard_map/ppermute | solution.py:27
  173.9 15.2 %collective-permute-start.3 = (f32[64,2,4,128]{3,2,0,1:T(4,128)S(1)}, f32[64,2,4,128]{3,2,0,1:T(4,128)S(1)}, u32[]{:S(2)}, u32[]{:S(2)}) collective-permute-start(f32[64,2,4,128]{3,2,0,1:T(4,128)S(1)} %pad_maximum_fusion.5), channel_id=1, source_target_pairs={{16,0},{32,16},{48,32},{64,48},{80,64},{96,80},{112,96},{128,112},... | collective-permute-start | bytes 786440 | tf_op jit(solution)/shard_map/ppermute | solution.py:29
  207.6 14.3 %all-to-all-start = ((f32[16,1,4096]{2,1,0:T(1,128)}), f32[16,1,4096]{2,1,0:T(1,128)S(1)}, u32[]{:S(2)}, u32[]{:S(2)}) async-start(f32[16,1,4096]{2,1,0:T(1,128)} %reshape.6294), calls=%async_computation.1 | async-start | bytes 524288 | tf_op jit(solution)/shard_map/all_to_all | solution.py:189
Sparse Core Ops, SparseCore 0:
  20.6 107.0 reduce-scatter.1
where the time goes:
time: 355 us; the launch traced here: 350 us
  waiting for transfers between devices  139 us (39%)
  local copies, waits for them, and re-layouts  72.6 us (20%)
  other arithmetic  61.1 us (17%)
  starting transfers between devices  22.3 us (6%)
  matrix products  20.2 us (6%)
  between operations  15.3 us (4%)
  blocking collectives  13.1 us (4%)
  loops' own time  5.73 us (2%)
    reduce_scatter x1, waiting for transfers between devices, local(): lax.psum_scatter(product.reshape(lax.axis_size('freq') * freq_rows, 2 * t...  107 us
    mul x8, other arithmetic, inverse_twiddle(): jnp.cos(angles) * scaling  34.2 us
    reshape x8, local copies, waits for them, and re-layouts, inverse_twiddle(): jnp.stack([jnp.cos(angles) * scaling, -jnp.sin(angles) * scaling], axis=2)  21.5 us
    ppermute x2, waiting for transfers between devices, padded_2(): lax.ppermute(head, axis, [((i + 1) % count, i) for i in range(ends)])  19 us
    another operation x8, local copies, waits for them, and re-layouts, inverse_twiddle(): jnp.stack([jnp.cos(angles) * scaling, -jnp.sin(angles) * scaling], axis=2)  18.9 us
    reduce_sum x92, other arithmetic, window_sum(): return jnp.sum(tiled(values), axis=(2, 4))  16.2 us
    dot_general x8, matrix products, rebuild_block(): jnp.dot(twiddle, stacked_bins, precision=highest, preferred_element_type=...  15.3 us
    all_to_all x1, blocking collectives, local(): lax.all_to_all(rebuilt, 'freq', split_axis=0, concat_axis=1, tiled=True)  13.1 us
  transfers between devices with their start and end apart: 6, of which 6 were waited for; matrix products, arithmetic and copies ran while one was open for 0% of the time, Pallas kernels for 0%

commit v1 on v0

v1 whole, which is shorter than its diff:
```python
import math

import jax
import jax.numpy as jnp
import numpy as np
from jax import lax
from jax.experimental import pallas as pl
from jax.experimental.pallas import tpu as pltpu
from jax.sharding import PartitionSpec as P

NT = 2048
FILT = 4
ITERS = 2
RADIX = 16
SPAN = 128
BINS = 64
WINDOWS = 4
WX = 32
LANES = 128
f32, bf16 = jnp.float32, jnp.bfloat16


def local_bin(m, e):
    side, step = divmod(e, 4)
    residue = m if side == 0 else (8 if m == 0 else RADIX - m)
    return 16 * step + residue


def bin_order():
    return [local_bin(m, e) for m in range(8) for e in range(8)]


def split_table(table):
    high = table.astype(np.float32).astype(bf16)
    low = (table - high.astype(np.float64)).astype(np.float32).astype(bf16)
    return high, low


def transform_tables():
    forward = np.zeros((8, 2 * SPAN, 2 * SPAN))
    inverse = np.zeros((8, 2 * SPAN, 2 * SPAN))
    r = np.arange(SPAN)
    for m in range(8):
        for g in range(RADIX):
            for e in range(8):
                f = BINS * g + local_bin(m, e)
                angle = 2.0 * np.pi * ((f * r) % NT) / NT
                c, s = np.cos(angle), np.sin(angle)
                col = g * 8 + e
                if m == 0:
                    part = slice(0, SPAN) if e < 4 else slice(SPAN, 2 * SPAN)
                    forward[m, part, col] = c
                    forward[m, part, SPAN + col] = -s
                else:
                    sign = 1.0 if e < 4 else -1.0
                    forward[m, :SPAN, col] = c
                    forward[m, SPAN:, col] = sign * s
                    forward[m, :SPAN, SPAN + col] = -s
                    forward[m, SPAN:, SPAN + col] = sign * c
                scale = (1.0 if f == 0 else 2.0) / NT * (1.0 if m == 0 else 0.5)
                inverse[m, col] = forward[m, :, col] * scale
                inverse[m, SPAN + col] = forward[m, :, SPAN + col] * scale
    return split_table(forward), split_table(inverse)


def spread_table():
    table = np.zeros((BINS, LANES), np.float32)
    for place, b in enumerate(bin_order()):
        table[b, place] = 1.0
        table[b, BINS + place] = 1.0
    return table.astype(bf16)


def cadd(a, b):
    im = a[1] if b[1] is None else (b[1] if a[1] is None else a[1] + b[1])
    return a[0] + b[0], im


def csub(a, b):
    im = a[1] if b[1] is None else (-b[1] if a[1] is None else a[1] - b[1])
    return a[0] - b[0], im


def conj(a):
    return a[0], None if a[1] is None else -a[1]


def turn(a, step, size):
    step = step % size
    if step == 0:
        return a
    if 4 * step == size:
        return (jnp.zeros_like(a[0]) if a[1] is None else -a[1]), a[0]
    if 4 * step == 3 * size:
        return (jnp.zeros_like(a[0]) if a[1] is None else a[1]), -a[0]
    c, s = math.cos(2 * math.pi * step / size), math.sin(2 * math.pi * step / size)
    if a[1] is None:
        return a[0] * c, a[0] * s
    return a[0] * c - a[1] * s, a[0] * s + a[1] * c


def real_transform(values):
    n = len(values)
    if n == 1:
        return [(values[0], None)]
    if n == 2:
        return [(values[0] + values[1], None), (values[0] - values[1], None)]
    even, odd = real_transform(values[::2]), real_transform(values[1::2])
    out = [None] * (n // 2 + 1)
    for p in range(n // 4 + 1):
        turned = turn(odd[p], -p, n)
        out[p] = cadd(even[p], turned)
        out[n // 2 - p] = conj(csub(even[p], turned))
    out[0] = (out[0][0], None)
    out[n // 2] = (out[n // 2][0], None)
    return out


def real_inverse(bins):
    n = 2 * (len(bins) - 1)
    if n == 2:
        return [bins[0][0] + bins[1][0], bins[0][0] - bins[1][0]]
    quarter = n // 4
    first, second = [], []
    for p in range(quarter + 1):
        other = conj(bins[n // 2 - p])
        total, rest = cadd(bins[p], other), turn(csub(bins[p], other), p, n)
        if p in (0, quarter):
            total, rest = (total[0], None), (rest[0], None)
        first.append(total)
        second.append(rest)
    out = [None] * n
    out[::2], out[1::2] = real_inverse(first), real_inverse(second)
    return out


def split_dot(lhs, high, low):
    rows = lhs.shape[0]
    top = lhs.astype(bf16)
    rest = (lhs - top.astype(f32)).astype(bf16)
    both = jnp.dot(jnp.concatenate([top, rest], axis=0), high, preferred_element_type=f32)
    return both[:rows] + both[rows:] + jnp.dot(top, low, preferred_element_type=f32)


def swap_blocks(arrays, lane):
    arrays = list(arrays)
    for d in (1, 2, 4):
        upper = (lane & (8 * d)) != 0
        for i in range(8):
            if i & d:
                continue
            a, b = arrays[i], arrays[i + d]
            arrays[i] = jnp.where(upper, pltpu.roll(b, 8 * d, 1), a)
            arrays[i + d] = jnp.where(upper, b, pltpu.roll(a, LANES - 8 * d, 1))
    return arrays


def send_kernel(traces, live, out):
    alive = live[...].astype(f32)
    for i in range(FILT):
        rows = traces[pl.ds(i, SPAN, stride=FILT), :] * alive[i : i + 1]
        out[i] = rows.T


def forward_kernel(blocks, high, low, out):
    lane = lax.broadcasted_iota(jnp.int32, (WX, LANES), 1)
    left = lane < BINS
    bins = real_transform([blocks[j] for j in range(RADIX)])
    real, imag = [], []
    for m in range(8):
        pair = [bins[0][0], bins[8][0]] if m == 0 else list(bins[m])
        product = split_dot(jnp.concatenate(pair, axis=1), high[m], low[m])
        real.append(product[:, :LANES])
        imag.append(product[:, LANES:])
    real, imag = swap_blocks(real, lane), swap_blocks(imag, lane)
    for g in range(8):
        out[g] = jnp.where(left, real[g], pltpu.roll(imag[g], BINS, 1))
        out[8 + g] = jnp.where(left, pltpu.roll(real[g], BINS, 1), imag[g])


def inverse_kernel(blocks, high, low, out):
    lane = lax.broadcasted_iota(jnp.int32, (WX, LANES), 1)
    left = lane < BINS
    real, imag = [], []
    for g in range(8):
        first, second = blocks[g], blocks[8 + g]
        real.append(jnp.where(left, first, pltpu.roll(second, BINS, 1)))
        imag.append(jnp.where(left, pltpu.roll(first, BINS, 1), second))
    real, imag = swap_blocks(real, lane), swap_blocks(imag, lane)
    bins = [None] * 9
    for m in range(8):
        product = split_dot(jnp.concatenate([real[m], imag[m]], axis=1), high[m], low[m])
        first, second = product[:, :LANES], product[:, LANES:]
        if m == 0:
            bins[0], bins[8] = (first, None), (second, None)
        else:
            bins[m] = (first, second)
    for j, values in enumerate(real_inverse(bins)):
        out[j] = values


def receive_kernel(blocks, out):
    for i in range(FILT):
        out[pl.ds(i, SPAN, stride=FILT), :] = blocks[i].T


def solve(matrix, target):
    n = FILT
    trace = matrix[0][0][0]
    for k in range(1, n):
        trace = trace + matrix[k][k][0]
    ridge = (0.05 * 2.0 / (2 * n)) * trace + 1e-05

    def cmul(a, b):
        return a[0] * b[0] - a[1] * b[1], a[0] * b[1] + a[1] * b[0]

    diag = [matrix[k][k][0] + ridge for k in range(n)]
    upper = {(k, l): matrix[k][l] for k in range(n) for l in range(k + 1, n)}
    rhs = list(target)
    inv = [None] * n
    for k in range(n):
        inv[k] = 1.0 / diag[k]
        for i in range(k + 1, n):
            re, im = upper[k, i]
            factor = (re * inv[k], -im * inv[k])
            diag[i] = diag[i] - (re * factor[0] - im * factor[1])
            for l in range(i + 1, n):
                t = cmul(factor, upper[k, l])
                upper[i, l] = (upper[i, l][0] - t[0], upper[i, l][1] - t[1])
            t = cmul(factor, rhs[k])
            rhs[i] = (rhs[i][0] - t[0], rhs[i][1] - t[1])
    found = [None] * n
    for k in reversed(range(n)):
        re, im = rhs[k]
        for l in range(k + 1, n):
            t = cmul(upper[k, l], found[l])
            re, im = re - t[0], im - t[1]
        found[k] = (re * inv[k], im * inv[k])
    return found


PAIRS = [(k, l) for k in range(FILT) for l in range(k, FILT)]
OFF = [(k, l) for k, l in PAIRS if k < l]
SUMS = len(PAIRS) + len(OFF) + 2 * FILT


def filter_kernel(before, block, after, weights, live, spread, out, omega, turned, sums, coefs):
    alive = live[...].astype(f32)
    table = spread[...]
    for i in range(FILT):
        rows = weights[pl.ds(i, BINS, stride=FILT), :] * alive[i : i + 1]
        top = rows.astype(bf16)
        rest = (rows - top.astype(f32)).astype(bf16)
        over = (((0,), (0,)), ((), ()))
        omega[i] = lax.dot_general(top, table, over, preferred_element_type=f32) + lax.dot_general(
            rest, table, over, preferred_element_type=f32
        )
    parts = (before, block, after)
    for part in range(3):
        for c in range(4 * FILT):
            turned[part, c] = pltpu.roll(parts[part][c], BINS, 1)

    def row_of(row):
        return divmod(row + FILT, FILT)

    def load(row, w, lines):
        part, i = row_of(row)
        return parts[part][i * WINDOWS + w, lines, :]

    def load_turned(row, w, lines):
        part, i = row_of(row)
        return turned[part, i * WINDOWS + w, lines, :]

    def gather(w, carry):
        for way, d in enumerate((-1, 1)):
            acc = [None] * SUMS

            def add(place, value):
                acc[place] = value if acc[place] is None else acc[place] + value

            for sub in range(WX // 8):
                lines = pl.ds(sub * 8, 8)
                wide = pl.ds(pl.multiple_of(w * WX + sub * 8, 8), 8)
                rows, turns = {}, {}
                for i in range(FILT):
                    for k in range(FILT + 1):
                        row = i + d * k
                        if row not in rows:
                            rows[row] = load(row, w, lines)
                            turns[row] = load_turned(row, w, lines)
                for i in range(FILT):
                    om = omega[i, wide, :]
                    place = 0
                    weighted = [om * rows[i + d * (k + 1)] for k in range(FILT)]
                    for k, l in PAIRS:
                        add(place, weighted[k] * rows[i + d * (l + 1)])
                        place += 1
                    for k, l in OFF:
                        add(place, weighted[k] * turns[i + d * (l + 1)])
                        place += 1
                    for k in range(FILT):
                        add(place, weighted[k] * rows[i])
                        add(place + 1, weighted[k] * turns[i])
                        place += 2
            for place in range(SUMS):
                start = pl.multiple_of((w * 2 + way) * 8, 8)
                sums[place, pl.ds(start, 8), :] = acc[place]
        return carry

    lax.fori_loop(0, WINDOWS, gather, 0)

    lane = lax.broadcasted_iota(jnp.int32, (8, LANES), 1)
    sign = jnp.where(lane < BINS, 1.0, -1.0).astype(f32)

    def total(place):
        value = sums[place, pl.ds(0, 8, stride=8), :]
        for s in range(1, 8):
            value = value + sums[place, pl.ds(s, 8, stride=8), :]
        return value

    def real_sum(place):
        value = total(place)
        return value + pltpu.roll(value, BINS, 1)

    def imag_sum(place):
        value = total(place)
        return (value - pltpu.roll(value, BINS, 1)) * sign

    matrix = [[None] * FILT for _ in range(FILT)]
    for place, (k, l) in enumerate(PAIRS):
        matrix[k][l] = (real_sum(place), None)
    for place, (k, l) in enumerate(OFF):
        matrix[k][l] = (matrix[k][l][0], imag_sum(len(PAIRS) + place))
    base = len(PAIRS) + len(OFF)
    target = [(real_sum(base + 2 * k), imag_sum(base + 2 * k + 1)) for k in range(FILT)]
    for k, (re, im) in enumerate(solve(matrix, target)):
        coefs[2 * k] = re
        coefs[2 * k + 1] = -im * sign

    def predict(w, carry):
        for sub in range(WX // 8):
            lines = pl.ds(sub * 8, 8)
            wide = pl.ds(pl.multiple_of(w * WX + sub * 8, 8), 8)
            acc = [None] * FILT
            for way, d in enumerate((-1, 1)):
                for k in range(FILT):
                    one = coefs[2 * k, pl.ds(w * 2 + way, 1), :]
                    two = coefs[2 * k + 1, pl.ds(w * 2 + way, 1), :]
                    for i in range(FILT):
                        row = i + d * (k + 1)
                        value = one * load(row, w, lines) + two * load_turned(row, w, lines)
                        acc[i] = value if acc[i] is None else acc[i] + value
            for i in range(FILT):
                half = jnp.where(omega[i, wide, :] > 0.0, 0.5, 0.0)
                out[i * WINDOWS + w, lines, :] = acc[i] * half
        return carry

    lax.fori_loop(0, WINDOWS, predict, 0)


def kernel_call(body, shape, scratch=(), name=None):
    return pl.pallas_call(
        body,
        out_shape=jax.ShapeDtypeStruct(shape, f32),
        scratch_shapes=list(scratch),
        compiler_params=pltpu.CompilerParams(vmem_limit_bytes=40 * 1024 * 1024),
        name=name,
    )


CHUNKS = (RADIX, WX, LANES)


def send_call(traces, live):
    rows = traces.reshape(SPAN * FILT, LANES)
    return kernel_call(send_kernel, (FILT, LANES, SPAN), name="send")(rows, live).reshape(CHUNKS)


def forward_call(blocks, high, low):
    return kernel_call(forward_kernel, CHUNKS, name="forward")(blocks, high, low)


def inverse_call(blocks, high, low):
    return kernel_call(inverse_kernel, CHUNKS, name="inverse")(blocks, high, low)


def filter_call(before, block, after, weights, live, spread):
    scratch = [
        pltpu.VMEM((FILT, LANES, LANES), f32),
        pltpu.VMEM((3,) + CHUNKS, f32),
        pltpu.VMEM((SUMS, 64, LANES), f32),
        pltpu.VMEM((2 * FILT, 8, LANES), f32),
    ]
    rows = weights.reshape(BINS * FILT, LANES)
    return kernel_call(filter_kernel, CHUNKS, scratch, name="filter")(
        before, block, after, rows, live, spread
    )


def receive_call(blocks):
    rows = blocks.reshape(FILT, LANES, SPAN)
    return kernel_call(receive_kernel, (SPAN * FILT, LANES), name="receive")(rows).reshape(
        SPAN, FILT, LANES
    )


def local(tables, traces_in, reweights, live_mask):
    (fh, fl), (ih, il), spread = tables
    fh, fl, ih, il, spread = (jnp.asarray(t) for t in (fh, fl, ih, il, spread))

    def exchange(blocks):
        return lax.all_to_all(blocks, "freq", 0, 0, tiled=True)

    count = lax.axis_size("inline")
    up = [(i, i + 1) for i in range(count - 1)]
    down = [(i + 1, i) for i in range(count - 1)]
    sent = send_call(traces_in, live_mask)
    current = exchange(forward_call(exchange(sent), fh, fl))
    for n in range(ITERS):
        before = lax.ppermute(current, "inline", up)
        after = lax.ppermute(current, "inline", down)
        current = filter_call(before, current, after, reweights[n], live_mask, spread)
    return receive_call(exchange(inverse_call(exchange(current), ih, il)))


def solution(mesh):
    tables = (*transform_tables(), spread_table())

    def run(traces_in, reweights, live_mask):
        return local(tables, traces_in, reweights, live_mask)

    in_specs = (P("freq", "inline", None), P(None, "freq", "inline", None), P("inline", None))
    out_specs = P("freq", "inline", None)
    return jax.shard_map(run, mesh=mesh, in_specs=in_specs, out_specs=out_specs, check_vma=False)
```

time: 355 us -> 113 us (0.32)
  the two profiles are of different devices: /device:TPU:41 before, /device:TPU:8 now
where the time goes in v1:
time: 113 us
  blocking collectives  66.9 us (59%)
  waiting for transfers between devices  24 us (21%)
  starting transfers between devices  12.5 us (11%)
  Pallas kernels  6.17 us (5%)
  local copies, waits for them, and re-layouts  2.99 us (3%)
    all_to_all x4, blocking collectives, exchange(): return lax.all_to_all(blocks, 'freq', 0, 0, tiled=True)  66.9 us
    ppermute x2, waiting for transfers between devices, local(): before = lax.ppermute(current, 'inline', up)  20 us
    ppermute x2, starting transfers between devices, local(): after = lax.ppermute(current, 'inline', down)  8.21 us
    ppermute x2, starting transfers between devices, local(): before = lax.ppermute(current, 'inline', up)  4.33 us
    ppermute x2, waiting for transfers between devices, local(): after = lax.ppermute(current, 'inline', down)  4 us
    pallas_call x2, Pallas kernels, filter_call(): kernel_call(filter_kernel, CHUNKS, scratch, name='filter')  3.71 us
    unnamed x18, local copies, waits for them, and re-layouts  2.98 us
  transfers between devices with their start and end apart: 4, of which 4 were waited for; matrix products, arithmetic and copies ran while one was open for 0% of the time, Pallas kernels for 0%

profile of v1, /device:TPU:8, one launch (start us, length us, event | category | flops | bytes accessed | tf_op | source)
XLA Modules:
  0.0 112.8 jit_solution(158174936418454088)
XLA Ops:
  0.0 0.0 copy-start.2
  0.0 0.0 copy-start.4
  0.0 1.0 copy-done.4
  1.0 0.0 copy-start.6
  1.0 0.7 copy-done.6
  1.7 0.1 send.1
  1.9 20.5 %all_to_all.20.blocks = f32[16,32,128]{2,1,0:T(8,128)S(1)} all-to-all(f32[16,32,128]{2,1,0:T(8,128)S(1)} %bitcast.7), channel_id=1, replica_groups=mesh['inline'=32,'freq'=16] {'freq'}, dimensions={0} | all-to-all | bytes 524288 | tf_op jit(solution)/shard_map/all_to_all | solution.py:412
  22.4 0.0 copy-done.2
  22.4 0.0 copy-start.3
  22.4 1.2 %copy-done.3 = bf16[8,256,256]{2,1,0:T(8,128)(2,1)S(1)} copy-done((bf16[8,256,256]{2,1,0:T(8,128)(2,1)S(1)}, bf16[8,256,256]{2,1,0:T(8,128)(2,1)}, u32[]{:S(2)}) %copy-start.3) | copy-done | bytes 1048600
  23.6 0.8 forward.1
  24.4 0.0 copy-start.8
  24.4 13.6 %all_to_all.21.block = f32[16,32,128]{2,1,0:T(8,128)S(1)} all-to-all(f32[16,32,128]{2,1,0:T(8,128)S(1)} %forward.1), channel_id=1, replica_groups=mesh['inline'=32,'freq'=16] {'freq'}, dimensions={0} | all-to-all | bytes 524288 | tf_op jit(solution)/shard_map/all_to_all | solution.py:412
  38.0 0.0 copy-start.5
  38.0 6.2 %collective-permute-start.1 = (f32[16,32,128]{2,1,0:T(8,128)S(1)}, f32[16,32,128]{2,1,0:T(8,128)S(1)}, u32[]{:S(2)}, u32[]{:S(2)}) collective-permute-start(f32[16,32,128]{2,1,0:T(8,128)S(1)} %all_to_all.21.block), channel_id=1, source_target_pairs={{16,0},{32,16},{48,32},{64,48},{80,64},{96,80},{112,96},{128,112},... | collective-permute-start | bytes 786440 | tf_op jit(solution)/shard_map/ppermute | solution.py:421
  44.2 1.9 %collective-permute-start = (f32[16,32,128]{2,1,0:T(8,128)S(1)}, f32[16,32,128]{2,1,0:T(8,128)S(1)}, u32[]{:S(2)}, u32[]{:S(2)}) collective-permute-start(f32[16,32,128]{2,1,0:T(8,128)S(1)} %all_to_all.21.block), channel_id=1, source_target_pairs={{0,16},{16,32},{32,48},{48,64},{64,80},{80,96},{96,112},{112,128},... | collective-permute-start | bytes 786440 | tf_op jit(solution)/shard_map/ppermute | solution.py:420
  46.1 0.0 copy-done.8
  46.2 0.0 copy-start.7
  46.2 2.5 %collective-permute-done.1.after = f32[16,32,128]{2,1,0:T(8,128)S(1)} collective-permute-done((f32[16,32,128]{2,1,0:T(8,128)S(1)}, f32[16,32,128]{2,1,0:T(8,128)S(1)}, u32[]{:S(2)}, u32[]{:S(2)}) %collective-permute-start.1) | collective-permute-done | bytes 262176 | tf_op jit(solution)/shard_map/ppermute | solution.py:421
  48.7 9.3 %collective-permute-done.before = f32[16,32,128]{2,1,0:T(8,128)S(1)} collective-permute-done((f32[16,32,128]{2,1,0:T(8,128)S(1)}, f32[16,32,128]{2,1,0:T(8,128)S(1)}, u32[]{:S(2)}, u32[]{:S(2)}) %collective-permute-start) | collective-permute-done | bytes 262176 | tf_op jit(solution)/shard_map/ppermute | solution.py:420
  58.0 0.0 copy-done.5
  58.0 0.0 copy-done.7
  58.0 0.0 copy-start.1
  58.0 1.9 %filter.2.block = f32[16,32,128]{2,1,0:T(8,128)S(1)} custom-call(f32[16,32,128]{2,1,0:T(8,128)S(1)} %collective-permute-done.before, f32[16,32,128]{2,1,0:T(8,128)S(1)} %all_to_all.21.block, f32[16,32,128]{2,1,0:T(8,128)S(1)} %collective-permute-done.1.after, f32[256,128]{1,0:T(8,128)S(1)} %bitcast.9, s32[4,128]{1,0:T(4,128)S(1)} %copy-done.7, ...), custom_call_target="tpu_custom_call" | custom-call | tf_op jit(solution)/shard_map/filter/pallas_call | solution.py:395
  59.9 0.0 copy-start
  59.9 2.1 %collective-permute-start.3 = (f32[16,32,128]{2,1,0:T(8,128)S(1)}, f32[16,32,128]{2,1,0:T(8,128)S(1)}, u32[]{:S(2)}, u32[]{:S(2)}) collective-permute-start(f32[16,32,128]{2,1,0:T(8,128)S(1)} %filter.2.block), channel_id=1, source_target_pairs={{16,0},{32,16},{48,32},{64,48},{80,64},{96,80},{112,96},{128,112},... | collective-permute-start | bytes 786440 | tf_op jit(solution)/shard_map/ppermute | solution.py:421
  61.9 2.4 %collective-permute-start.2 = (f32[16,32,128]{2,1,0:T(8,128)S(1)}, f32[16,32,128]{2,1,0:T(8,128)S(1)}, u32[]{:S(2)}, u32[]{:S(2)}) collective-permute-start(f32[16,32,128]{2,1,0:T(8,128)S(1)} %filter.2.block), channel_id=1, source_target_pairs={{0,16},{16,32},{32,48},{48,64},{64,80},{80,96},{96,112},{112,128},... | collective-permute-start | bytes 786440 | tf_op jit(solution)/shard_map/ppermute | solution.py:420
  64.4 1.5 %collective-permute-done.3.after = f32[16,32,128]{2,1,0:T(8,128)S(1)} collective-permute-done((f32[16,32,128]{2,1,0:T(8,128)S(1)}, f32[16,32,128]{2,1,0:T(8,128)S(1)}, u32[]{:S(2)}, u32[]{:S(2)}) %collective-permute-start.3) | collective-permute-done | bytes 262176 | tf_op jit(solution)/shard_map/ppermute | solution.py:421
  65.8 10.7 %collective-permute-done.2.before = f32[16,32,128]{2,1,0:T(8,128)S(1)} collective-permute-done((f32[16,32,128]{2,1,0:T(8,128)S(1)}, f32[16,32,128]{2,1,0:T(8,128)S(1)}, u32[]{:S(2)}, u32[]{:S(2)}) %collective-permute-start.2) | collective-permute-done | bytes 262176 | tf_op jit(solution)/shard_map/ppermute | solution.py:420
  76.5 1.9 %filter.3 = f32[16,32,128]{2,1,0:T(8,128)S(1)} custom-call(f32[16,32,128]{2,1,0:T(8,128)S(1)} %collective-permute-done.2.before, f32[16,32,128]{2,1,0:T(8,128)S(1)} %filter.2.block, f32[16,32,128]{2,1,0:T(8,128)S(1)} %collective-permute-done.3.after, f32[256,128]{1,0:T(8,128)S(1)} %bitcast.8, s32[4,128]{1,0:T(4,128)S(1)} %copy-done.7, ...), custom_call_target="tpu_custom_call" | custom-call | tf_op jit(solution)/shard_map/filter/pallas_call | solution.py:395
  78.4 18.7 %all_to_all.22.blocks = f32[16,32,128]{2,1,0:T(8,128)S(1)} all-to-all(f32[16,32,128]{2,1,0:T(8,128)S(1)} %filter.3), channel_id=1, replica_groups=mesh['inline'=32,'freq'=16] {'freq'}, dimensions={0} | all-to-all | bytes 524288 | tf_op jit(solution)/shard_map/all_to_all | solution.py:412
  97.1 0.0 copy-done.1
  97.1 0.0 copy-done
  97.1 0.7 inverse.1
  97.8 14.1 %all_to_all.23 = f32[16,32,128]{2,1,0:T(8,128)S(1)} all-to-all(f32[16,32,128]{2,1,0:T(8,128)S(1)} %inverse.1), channel_id=1, replica_groups=mesh['inline'=32,'freq'=16] {'freq'}, dimensions={0} | all-to-all | bytes 524288 | tf_op jit(solution)/shard_map/all_to_all | solution.py:412
  111.9 0.8 receive.1
  (1 shorter events, 0.0 us)
Async XLA Ops:
  0.0 22.4 %copy-start.2 = (bf16[8,256,256]{2,1,0:T(8,128)(2,1)S(1)}, bf16[8,256,256]{2,1,0:T(8,128)(2,1)}, u32[]{:S(2)}) copy-start(bf16[8,256,256]{2,1,0:T(8,128)(2,1)} %constant.11.clone.low) | copy-start | bytes 3145732
  0.0 1.0 copy-start.4
  1.0 0.7 copy-start.6
  22.4 1.2 %copy-start.3 = (bf16[8,256,256]{2,1,0:T(8,128)(2,1)S(1)}, bf16[8,256,256]{2,1,0:T(8,128)(2,1)}, u32[]{:S(2)}) copy-start(bf16[8,256,256]{2,1,0:T(8,128)(2,1)} %constant.10.clone.high) | copy-start | bytes 3145732
  24.4 21.8 %copy-start.8 = (f32[2,64,4,128]{3,2,1,0:T(4,128)S(1)}, f32[2,64,4,128]{3,2,1,0:T(4,128)}, u32[]{:S(2)}) copy-start(f32[2,64,4,128]{3,2,1,0:T(4,128)} %param.9) | copy-start | bytes 786436
  38.0 20.0 %copy-start.5 = (bf16[64,128]{1,0:T(8,128)(2,1)S(1)}, bf16[64,128]{1,0:T(8,128)(2,1)}, u32[]{:S(2)}) copy-start(bf16[64,128]{1,0:T(8,128)(2,1)} %constant.14.clone.spread) | copy-start | bytes 49156
  38.0 10.7 %collective-permute-start.1 = (f32[16,32,128]{2,1,0:T(8,128)S(1)}, f32[16,32,128]{2,1,0:T(8,128)S(1)}, u32[]{:S(2)}, u32[]{:S(2)}) collective-permute-start(f32[16,32,128]{2,1,0:T(8,128)S(1)} %all_to_all.21.block), channel_id=1, source_target_pairs={{16,0},{32,16},{48,32},{64,48},{80,64},{96,80},{112,96},{128,112},... | collective-permute-start | bytes 786440 | tf_op jit(solution)/shard_map/ppermute | solution.py:421
  44.2 13.8 %collective-permute-start = (f32[16,32,128]{2,1,0:T(8,128)S(1)}, f32[16,32,128]{2,1,0:T(8,128)S(1)}, u32[]{:S(2)}, u32[]{:S(2)}) collective-permute-start(f32[16,32,128]{2,1,0:T(8,128)S(1)} %all_to_all.21.block), channel_id=1, source_target_pairs={{0,16},{16,32},{32,48},{48,64},{64,80},{80,96},{96,112},{112,128},... | collective-permute-start | bytes 786440 | tf_op jit(solution)/shard_map/ppermute | solution.py:420
  46.2 11.9 %copy-start.7 = (s32[4,128]{1,0:T(4,128)S(1)}, s32[4,128]{1,0:T(4,128)}, u32[]{:S(2)}) copy-start(s32[4,128]{1,0:T(4,128)} %live.5) | copy-start | bytes 6148
  58.0 39.1 %copy-start.1 = (bf16[8,256,256]{2,1,0:T(8,128)(2,1)S(1)}, bf16[8,256,256]{2,1,0:T(8,128)(2,1)}, u32[]{:S(2)}) copy-start(bf16[8,256,256]{2,1,0:T(8,128)(2,1)} %constant.12.clone.high) | copy-start | bytes 3145732
  59.9 37.2 %copy-start = (bf16[8,256,256]{2,1,0:T(8,128)(2,1)S(1)}, bf16[8,256,256]{2,1,0:T(8,128)(2,1)}, u32[]{:S(2)}) copy-start(bf16[8,256,256]{2,1,0:T(8,128)(2,1)} %constant.13.clone.low) | copy-start | bytes 3145732
  59.9 5.9 %collective-permute-start.3 = (f32[16,32,128]{2,1,0:T(8,128)S(1)}, f32[16,32,128]{2,1,0:T(8,128)S(1)}, u32[]{:S(2)}, u32[]{:S(2)}) collective-permute-start(f32[16,32,128]{2,1,0:T(8,128)S(1)} %filter.2.block), channel_id=1, source_target_pairs={{16,0},{32,16},{48,32},{64,48},{80,64},{96,80},{112,96},{128,112},... | collective-permute-start | bytes 786440 | tf_op jit(solution)/shard_map/ppermute | solution.py:421
  61.9 14.6 %collective-permute-start.2 = (f32[16,32,128]{2,1,0:T(8,128)S(1)}, f32[16,32,128]{2,1,0:T(8,128)S(1)}, u32[]{:S(2)}, u32[]{:S(2)}) collective-permute-start(f32[16,32,128]{2,1,0:T(8,128)S(1)} %filter.2.block), channel_id=1, source_target_pairs={{0,16},{16,32},{32,48},{48,64},{64,80},{80,96},{96,112},{112,128},... | collective-permute-start | bytes 786440 | tf_op jit(solution)/shard_map/ppermute | solution.py:420

commit v2 on v1

v2 whole, which is shorter than its diff:
```python
import functools
import math

import jax
import jax.numpy as jnp
import numpy as np
from jax import lax
from jax.experimental import pallas as pl
from jax.experimental.pallas import tpu as pltpu
from jax.sharding import PartitionSpec as P

NT = 2048
FILT = 4
ITERS = 2
RADIX = 16
SPAN = 128
BINS = 64
WINDOWS = 4
WX = 32
ROWS = 16
UNITS = 8
LANES = 128
f32, bf16 = jnp.float32, jnp.bfloat16


def low_bin(m, s, b):
    residue = m if s == 0 else (8 if m == 0 else RADIX - m)
    return 16 * b + residue


INNER = [(s, b) for s in range(2) for b in range(2)]
HALF = BINS // 2


def split_table(table):
    high = table.astype(np.float32).astype(bf16)
    low = (table - high.astype(np.float64)).astype(np.float32).astype(bf16)
    return high, low


def transform_tables():
    forward = np.zeros((8, 2 * SPAN, 2 * SPAN))
    inverse = np.zeros((8, 2 * SPAN, 2 * SPAN))
    r = np.arange(SPAN)
    for m in range(8):
        for part in range(2 * RADIX):
            zh, g = divmod(part, RADIX)
            for place, (s, b) in enumerate(INNER):
                f = BINS * g + HALF * zh + low_bin(m, s, b)
                angle = 2.0 * np.pi * ((f * r) % NT) / NT
                c, sn = np.cos(angle), np.sin(angle)
                col = part * 4 + place
                if m == 0:
                    span = slice(s * SPAN, (s + 1) * SPAN)
                    forward[m, span, col] = c
                    forward[m, span, SPAN + col] = -sn
                else:
                    sign = 1.0 if s == 0 else -1.0
                    forward[m, :SPAN, col] = c
                    forward[m, SPAN:, col] = sign * sn
                    forward[m, :SPAN, SPAN + col] = -sn
                    forward[m, SPAN:, SPAN + col] = sign * c
                scale = (1.0 if f == 0 else 2.0) / NT * (1.0 if m == 0 else 0.5)
                inverse[m, col] = forward[m, :, col] * scale
                inverse[m, SPAN + col] = forward[m, :, SPAN + col] * scale
    return split_table(forward), split_table(inverse)


def spread_table():
    table = np.zeros((HALF, LANES), np.float32)
    for m in range(8):
        for place, (s, b) in enumerate(INNER):
            for quarter in range(4):
                table[low_bin(m, s, b), quarter * HALF + m * 4 + place] = 1.0
    return table.astype(bf16)


def cadd(a, b):
    im = a[1] if b[1] is None else (b[1] if a[1] is None else a[1] + b[1])
    return a[0] + b[0], im


def csub(a, b):
    im = a[1] if b[1] is None else (-b[1] if a[1] is None else a[1] - b[1])
    return a[0] - b[0], im


def conj(a):
    return a[0], None if a[1] is None else -a[1]


def turn(a, step, size):
    step = step % size
    if step == 0:
        return a
    if 4 * step == size:
        return (jnp.zeros_like(a[0]) if a[1] is None else -a[1]), a[0]
    if 4 * step == 3 * size:
        return (jnp.zeros_like(a[0]) if a[1] is None else a[1]), -a[0]
    c, s = math.cos(2 * math.pi * step / size), math.sin(2 * math.pi * step / size)
    if a[1] is None:
        return a[0] * c, a[0] * s
    return a[0] * c - a[1] * s, a[0] * s + a[1] * c


def real_transform(values):
    n = len(values)
    if n == 1:
        return [(values[0], None)]
    if n == 2:
        return [(values[0] + values[1], None), (values[0] - values[1], None)]
    even, odd = real_transform(values[::2]), real_transform(values[1::2])
    out = [None] * (n // 2 + 1)
    for p in range(n // 4 + 1):
        turned = turn(odd[p], -p, n)
        out[p] = cadd(even[p], turned)
        out[n // 2 - p] = conj(csub(even[p], turned))
    out[0] = (out[0][0], None)
    out[n // 2] = (out[n // 2][0], None)
    return out


def real_inverse(bins):
    n = 2 * (len(bins) - 1)
    if n == 2:
        return [bins[0][0] + bins[1][0], bins[0][0] - bins[1][0]]
    quarter = n // 4
    first, second = [], []
    for p in range(quarter + 1):
        other = conj(bins[n // 2 - p])
        total, rest = cadd(bins[p], other), turn(csub(bins[p], other), p, n)
        if p in (0, quarter):
            total, rest = (total[0], None), (rest[0], None)
        first.append(total)
        second.append(rest)
    out = [None] * n
    out[::2], out[1::2] = real_inverse(first), real_inverse(second)
    return out


def split_dot(lhs, high, low):
    rows = lhs.shape[0]
    top = lhs.astype(bf16)
    rest = (lhs - top.astype(f32)).astype(bf16)
    both = jnp.dot(jnp.concatenate([top, rest], axis=0), high, preferred_element_type=f32)
    return both[:rows] + both[rows:] + jnp.dot(top, low, preferred_element_type=f32)


def swap_blocks(arrays, lane, width):
    arrays = list(arrays)
    n = len(arrays)
    d = 1
    while d < n:
        upper = (lane & (width * d)) != 0
        for i in range(n):
            if i & d:
                continue
            a, b = arrays[i], arrays[i + d]
            arrays[i] = jnp.where(upper, pltpu.roll(b, width * d, 1), a)
            arrays[i + d] = jnp.where(upper, b, pltpu.roll(a, LANES - width * d, 1))
        d *= 2
    return arrays


def lanes_of(rows):
    return lax.broadcasted_iota(jnp.int32, (rows, LANES), 1)


def send_kernel(traces, live, weights, out, give):
    alive = live[...].astype(f32)
    for i in range(FILT):
        rows = traces[pl.ds(i, SPAN, stride=FILT), :] * alive[i : i + 1]
        turned = rows.T
        for w in range(WINDOWS):
            out[w * FILT + i] = turned[w * WX : (w + 1) * WX]
    other = (1 - lax.axis_index("zh")) * (HALF * FILT)
    pair = jnp.concatenate([alive, alive], axis=0)
    for n in range(ITERS):
        for k in range(HALF * FILT // 8):
            start = pl.multiple_of(n * BINS * FILT + other + 8 * k, 8)
            give[n, pl.ds(8 * k, 8), :] = weights[pl.ds(start, 8), :] * pair


def forward_kernel(blocks, high, low, out):
    lane = lanes_of(WX)
    bins = real_transform([blocks[j] for j in range(RADIX)])
    real, imag = [], []
    for m in range(8):
        pair = [bins[0][0], bins[8][0]] if m == 0 else list(bins[m])
        product = split_dot(jnp.concatenate(pair, axis=1), high[m], low[m])
        real.append(product[:, :LANES])
        imag.append(product[:, LANES:])
    real, imag = swap_blocks(real, lane, 4), swap_blocks(imag, lane, 4)
    for k in range(8):
        pieces = [real[k][:16], real[k][16:], imag[k][:16], imag[k][16:]]
        for top, tile in enumerate(swap_blocks(pieces, lanes_of(16), HALF)):
            out[top * 8 + k] = tile


def inverse_kernel(blocks, high, low, out):
    lane = lanes_of(WX)
    real, imag = [], []
    for k in range(8):
        pieces = swap_blocks([blocks[top * 8 + k] for top in range(4)], lanes_of(16), HALF)
        real.append(jnp.concatenate(pieces[:2], axis=0))
        imag.append(jnp.concatenate(pieces[2:], axis=0))
    real, imag = swap_blocks(real, lane, 4), swap_blocks(imag, lane, 4)
    bins = [None] * 9
    for m in range(8):
        product = split_dot(jnp.concatenate([real[m], imag[m]], axis=1), high[m], low[m])
        first, second = product[:, :LANES], product[:, LANES:]
        if m == 0:
            bins[0], bins[8] = (first, None), (second, None)
        else:
            bins[m] = (first, second)
    for j, values in enumerate(real_inverse(bins)):
        out[j] = values


def receive_kernel(blocks, out):
    for i in range(FILT):
        rows = jnp.concatenate([blocks[w * FILT + i] for w in range(WINDOWS)], axis=0)
        out[pl.ds(i, SPAN, stride=FILT), :] = rows.T


def solve(matrix, target):
    n = FILT
    trace = matrix[0][0][0]
    for k in range(1, n):
        trace = trace + matrix[k][k][0]
    ridge = (0.05 * 2.0 / (2 * n)) * trace + 1e-05

    def cmul(a, b):
        return a[0] * b[0] - a[1] * b[1], a[0] * b[1] + a[1] * b[0]

    diag = [matrix[k][k][0] + ridge for k in range(n)]
    upper = {(k, l): matrix[k][l] for k in range(n) for l in range(k + 1, n)}
    rhs = list(target)
    inv = [None] * n
    for k in range(n):
        inv[k] = 1.0 / diag[k]
        for i in range(k + 1, n):
            re, im = upper[k, i]
            factor = (re * inv[k], -im * inv[k])
            diag[i] = diag[i] - (re * factor[0] - im * factor[1])
            for l in range(i + 1, n):
                t = cmul(factor, upper[k, l])
                upper[i, l] = (upper[i, l][0] - t[0], upper[i, l][1] - t[1])
            t = cmul(factor, rhs[k])
            rhs[i] = (rhs[i][0] - t[0], rhs[i][1] - t[1])
    found = [None] * n
    for k in reversed(range(n)):
        re, im = rhs[k]
        for l in range(k + 1, n):
            t = cmul(upper[k, l], found[l])
            re, im = re - t[0], im - t[1]
        found[k] = (re * inv[k], im * inv[k])
    return found


PAIRS = [(k, l) for k in range(FILT) for l in range(k, FILT)]
OFF = [(k, l) for k, l in PAIRS if k < l]
SUMS = len(PAIRS) + len(OFF) + 2 * FILT


def filter_kernel(n, block, partner, edge, weights, live, got, spread, *refs):
    out, edge_out = refs[:2] if len(refs) == 8 else (refs[0], None)
    sides, turned_sides, turned, omega, sums, coefs = refs[-6:]
    core, own = lax.axis_index("c"), lax.axis_index("zh")
    alive = live[...].astype(f32)
    table = spread[...]
    over = (((0,), (0,)), ((), ()))
    upper = (lanes_of(ROWS) & HALF) != 0
    for mine in (True, False):
        beta = own if mine else 1 - own
        for i in range(FILT):
            if mine:
                rows = weights[pl.ds(n * BINS * FILT + own * HALF * FILT + i, HALF, stride=FILT), :] * alive[i : i + 1]
            else:
                rows = got[n, pl.ds(i, HALF, stride=FILT), :]
            top = rows.astype(bf16)
            rest = (rows - top.astype(f32)).astype(bf16)
            wide = lax.dot_general(top, table, over, preferred_element_type=f32) + lax.dot_general(
                rest, table, over, preferred_element_type=f32
            )
            for w in range(WINDOWS):
                first, second = wide[w * WX : w * WX + ROWS], wide[w * WX + ROWS : (w + 1) * WX]
                omega[beta * WINDOWS + w, i * ROWS : (i + 1) * ROWS] = jnp.where(upper, second, first)
    for k in range(4 * FILT):
        values = edge[k]
        sides[2 * core, k] = values
        turned_sides[2 * core, k] = pltpu.roll(values, BINS, 1)
        for p in range(2):
            values = partner[p * 4 * FILT + k]
            sides[1 - core + p, k] = values
            turned_sides[1 - core + p, k] = pltpu.roll(values, BINS, 1)
            turned[p * 4 * FILT + k] = pltpu.roll(block[p * 4 * FILT + k], BINS, 1)

    def load(row, unit, lines, plain=True):
        beta, w = unit // WINDOWS, unit % WINDOWS
        part, i = divmod(row + FILT, FILT)
        if part == 1:
            return (block if plain else turned)[unit * FILT + i, lines, :]
        return (sides if plain else turned_sides)[beta + part // 2, w * FILT + i, lines, :]

    def gather(unit, carry):
        for way, d in enumerate((-1, 1)):
            acc = [None] * SUMS

            def add(place, value):
                acc[place] = value if acc[place] is None else acc[place] + value

            for sub in range(ROWS // 8):
                lines = pl.ds(sub * 8, 8)
                rows, turns = {}, {}
                for i in range(FILT):
                    for k in range(FILT + 1):
                        row = i + d * k
                        if row not in rows:
                            rows[row] = load(row, unit, lines)
                            turns[row] = load(row, unit, lines, False)
                for i in range(FILT):
                    om = omega[unit, pl.ds(i * ROWS + sub * 8, 8), :]
                    place = 0
                    weighted = [om * rows[i + d * (k + 1)] for k in range(FILT)]
                    for k, l in PAIRS:
                        add(place, weighted[k] * rows[i + d * (l + 1)])
                        place += 1
                    for k, l in OFF:
                        add(place, weighted[k] * turns[i + d * (l + 1)])
                        place += 1
                    for k in range(FILT):
                        add(place, weighted[k] * rows[i])
                        add(place + 1, weighted[k] * turns[i])
                        place += 2
            for place in range(SUMS):
                start = pl.multiple_of((unit * 2 + way) * 8, 8)
                sums[place, pl.ds(start, 8), :] = acc[place]
        return carry

    lax.fori_loop(0, UNITS, gather, 0)

    sign = jnp.where(lanes_of(2 * UNITS) < BINS, 1.0, -1.0).astype(f32)

    def total(place):
        value = sums[place, pl.ds(0, 2 * UNITS, stride=8), :]
        for s in range(1, 8):
            value = value + sums[place, pl.ds(s, 2 * UNITS, stride=8), :]
        return value

    def both_halves(value):
        return value + pltpu.roll(value, HALF, 1)

    def real_sum(place):
        value = total(place)
        return both_halves(value + pltpu.roll(value, BINS, 1))

    def imag_sum(place):
        value = total(place)
        return both_halves((value - pltpu.roll(value, BINS, 1)) * sign)

    matrix = [[None] * FILT for _ in range(FILT)]
    for place, (k, l) in enumerate(PAIRS):
        matrix[k][l] = (real_sum(place), None)
    for place, (k, l) in enumerate(OFF):
        matrix[k][l] = (matrix[k][l][0], imag_sum(len(PAIRS) + place))
    base = len(PAIRS) + len(OFF)
    target = [(real_sum(base + 2 * k), imag_sum(base + 2 * k + 1)) for k in range(FILT)]
    for k, (re, im) in enumerate(solve(matrix, target)):
        coefs[2 * k] = re
        coefs[2 * k + 1] = -im * sign

    def predict(unit, carry):
        for sub in range(ROWS // 8):
            lines = pl.ds(sub * 8, 8)
            acc = [None] * FILT
            for way, d in enumerate((-1, 1)):
                for k in range(FILT):
                    one = coefs[2 * k, pl.ds(unit * 2 + way, 1), :]
                    two = coefs[2 * k + 1, pl.ds(unit * 2 + way, 1), :]
                    for i in range(FILT):
                        row = i + d * (k + 1)
                        value = one * load(row, unit, lines) + two * load(row, unit, lines, False)
                        acc[i] = value if acc[i] is None else acc[i] + value
            for i in range(FILT):
                half = jnp.where(omega[unit, pl.ds(i * ROWS + sub * 8, 8), :] > 0.0, 0.5, 0.0)
                out[unit * FILT + i, lines, :] = acc[i] * half
        return carry

    lax.fori_loop(0, UNITS, predict, 0)
    if edge_out is not None:
        for k in range(4 * FILT):
            edge_out[k] = out[core * 4 * FILT + k]


def kernel_call(body, shapes, scratch=(), name=None):
    out = [jax.ShapeDtypeStruct(shape, f32) for shape in shapes]
    return pl.pallas_call(
        body,
        out_shape=out if len(out) > 1 else out[0],
        scratch_shapes=list(scratch),
        compiler_params=pltpu.CompilerParams(vmem_limit_bytes=16 * 1024 * 1024),
        name=name,
    )


TRACES = (RADIX, WX, LANES)
TILES = (8 * FILT, ROWS, LANES)
EDGE = (4 * FILT, ROWS, LANES)
GIVE = (ITERS, HALF * FILT, LANES)


def send_call(traces, live, weights):
    rows = traces.reshape(SPAN * FILT, LANES)
    return kernel_call(send_kernel, [TRACES, GIVE], name="send")(rows, live, weights)


def forward_call(blocks, high, low):
    return kernel_call(forward_kernel, [TILES], name="forward")(blocks, high, low)


def inverse_call(blocks, high, low):
    return kernel_call(inverse_kernel, [TRACES], name="inverse")(blocks, high, low)


def filter_call(n, block, partner, edge, weights, live, got, spread):
    scratch = [
        pltpu.VMEM((3,) + EDGE, f32),
        pltpu.VMEM((3,) + EDGE, f32),
        pltpu.VMEM(TILES, f32),
        pltpu.VMEM((UNITS, FILT * ROWS, LANES), f32),
        pltpu.VMEM((SUMS, 16 * UNITS, LANES), f32),
        pltpu.VMEM((2 * FILT, 2 * UNITS, LANES), f32),
    ]
    shapes = [TILES, EDGE] if n + 1 < ITERS else [TILES]
    body = functools.partial(filter_kernel, n)
    return kernel_call(body, shapes, scratch, name="filter")(
        block, partner, edge, weights, live, got, spread
    )


def receive_call(blocks):
    return kernel_call(receive_kernel, [(SPAN * FILT, LANES)], name="receive")(blocks).reshape(
        SPAN, FILT, LANES
    )


def local(tables, traces_in, reweights, live_mask):
    (fh, fl), (ih, il), spread = tables
    fh, fl, ih, il, spread = (jnp.asarray(t) for t in (fh, fl, ih, il, spread))

    def exchange(blocks, axes):
        return lax.all_to_all(blocks, axes, 0, 0, tiled=True)

    swap = [(0, 1), (1, 0)]
    ys = lax.axis_size("y")
    shift = [(2 * y + 1, 2 * y + 2) for y in range(ys - 1)] + [(2 * y + 2, 2 * y + 1) for y in range(ys - 1)]
    weights = reweights.reshape(ITERS * BINS * FILT, LANES)
    sent, give = send_call(traces_in, live_mask, weights)
    got = lax.ppermute(give, "zh", swap)
    spectra = forward_call(exchange(sent, ("x", "zl")), fh, fl)
    spectra, got = lax.optimization_barrier((spectra, got))
    block = exchange(spectra, ("zh", "x", "zl"))
    edge = lax.dynamic_index_in_dim(block.reshape((2,) + EDGE), lax.axis_index("c"), 0, False)
    for n in range(ITERS):
        partner = lax.ppermute(block, "c", swap)
        beyond = lax.ppermute(edge, ("y", "c"), shift)
        found = filter_call(n, block, partner, beyond, weights, live_mask, got, spread)
        block, edge = found if n + 1 < ITERS else (found, None)
    back = exchange(block, ("zh", "x", "zl"))
    return receive_call(exchange(inverse_call(back, ih, il), ("x", "zl")))


def solution(mesh):
    tables = (*transform_tables(), spread_table())

    def run(traces_in, reweights, live_mask):
        return local(tables, traces_in, reweights, live_mask)

    inner = jax.sharding.Mesh(mesh.devices.reshape(-1, 2, 2, 4, 4), ("y", "zh", "c", "x", "zl"))
    inline, freq = ("y", "zh", "c"), ("x", "zl")
    in_specs = (P(freq, inline, None), P(None, freq, inline, None), P(inline, None))
    out_specs = P(freq, inline, None)
    return jax.shard_map(run, mesh=inner, in_specs=in_specs, out_specs=out_specs, check_vma=False)
```

time: 113 us -> 108 us (0.956)
  the two profiles are of different devices: /device:TPU:8 before, /device:TPU:24 now
where the time goes in v2:
time: 108 us; the launch traced here: 107 us
  blocking collectives  55.9 us (52%)
  starting transfers between devices  28.2 us (26%)
  waiting for transfers between devices  11.7 us (11%)
  Pallas kernels  7.47 us (7%)
  local copies, waits for them, and re-layouts  3.85 us (4%)
    all_to_all x3, blocking collectives, exchange(): return lax.all_to_all(blocks, axes, 0, 0, tiled=True)  55.9 us
    all_to_all x1, starting transfers between devices, exchange(): return lax.all_to_all(blocks, axes, 0, 0, tiled=True)  9.83 us
    ppermute x1, starting transfers between devices, local(): got = lax.ppermute(give, 'zh', swap)  8.22 us
    ppermute x2, waiting for transfers between devices, local(): beyond = lax.ppermute(edge, ('y', 'c'), shift)  8.18 us
    ppermute x2, starting transfers between devices, local(): partner = lax.ppermute(block, 'c', swap)  5.78 us
    ppermute x2, starting transfers between devices, local(): beyond = lax.ppermute(edge, ('y', 'c'), shift)  4.38 us
    pallas_call x2, Pallas kernels, filter_call(): kernel_call(body, shapes, scratch, name='filter')  4.15 us
    unnamed x18, local copies, waits for them, and re-layouts  3.83 us
  transfers between devices with their start and end apart: 6, of which 4 were waited for; matrix products, arithmetic and copies ran while one was open for 0% of the time, Pallas kernels for 1%

profile of v2, /device:TPU:24, one launch (start us, length us, event | category | flops | bytes accessed | tf_op | source)
XLA Modules:
  0.0 107.3 jit_solution(1464546730971694208)
XLA Ops:
  0.0 0.0 copy-start.8
  0.0 0.7 copy-done.8
  0.7 0.0 copy-start
  0.7 0.9 copy-done
  1.6 0.0 copy-start.6
  1.6 0.9 copy-done.6
  2.6 0.0 copy-start.4
  2.6 0.8 send.1
  3.4 9.8 %all-to-all-start = ((f32[16,32,128]{2,1,0:T(8,128)}), f32[16,32,128]{2,1,0:T(8,128)S(1)}, u32[]{:S(2)}, u32[]{:S(2)}) async-start(f32[16,32,128]{2,1,0:T(8,128)} %get-tuple-element.11), calls=%async_computation | async-start | bytes 524288 | tf_op jit(solution)/shard_map/all_to_all | solution.py:453
  13.3 8.2 %collective-permute-start = (f32[2,128,128]{2,1,0:T(8,128)S(1)}, f32[2,128,128]{2,1,0:T(8,128)S(1)}, u32[]{:S(2)}, u32[]{:S(2)}) collective-permute-start(f32[2,128,128]{2,1,0:T(8,128)S(1)} %get-tuple-element.12), channel_id=1, source_target_pairs={{0,32},{32,0},{1,33},{33,1},{2,34},{34,2},{3,35},{35,3},{4,36},{36... | collective-permute-start | bytes 393224 | tf_op jit(solution)/shard_map/ppermute | solution.py:460
  21.5 2.7 %all-to-all-done.blocks = f32[16,32,128]{2,1,0:T(8,128)S(1)} async-done(((f32[16,32,128]{2,1,0:T(8,128)}), f32[16,32,128]{2,1,0:T(8,128)S(1)}, u32[]{:S(2)}, u32[]{:S(2)}) %all-to-all-start) | async-done | bytes 262176 | tf_op jit(solution)/shard_map/all_to_all | solution.py:453
  24.1 0.0 copy-done.4
  24.1 0.0 copy-start.5
  24.2 1.2 %copy-done.5 = bf16[8,256,256]{2,1,0:T(8,128)(2,1)S(1)} copy-done((bf16[8,256,256]{2,1,0:T(8,128)(2,1)S(1)}, bf16[8,256,256]{2,1,0:T(8,128)(2,1)}, u32[]{:S(2)}) %copy-start.5) | copy-done | bytes 1048600
  25.4 0.8 forward.1
  26.2 0.9 collective-permute-done.got
  27.1 24.3 %all_to_all.20.block = f32[32,16,128]{2,1,0:T(8,128)S(1)} all-to-all(f32[32,16,128]{2,1,0:T(8,128)S(1)} %forward.1), channel_id=1, replica_groups=mesh['y'=8,'zh'=2,'c'=2,'x'=4,'zl'=4] {'zh','x','zl'}, dimensions={0} | all-to-all | bytes 524288 | tf_op jit(solution)/shard_map/all_to_all | solution.py:453
  51.4 0.0 copy-start.1
  51.4 2.0 %collective-permute-start.1 = (f32[32,16,128]{2,1,0:T(8,128)S(1)}, f32[32,16,128]{2,1,0:T(8,128)S(1)}, u32[]{:S(2)}, u32[]{:S(2)}) collective-permute-start(f32[32,16,128]{2,1,0:T(8,128)S(1)} %all_to_all.20.block), channel_id=1, source_target_pairs={{0,16},{16,0},{1,17},{17,1},{2,18},{18,2},{3,19},{19,3},{4,20},{20... | collective-permute-start | bytes 786440 | tf_op jit(solution)/shard_map/ppermute | solution.py:466
  53.4 0.0 copy-start.7
  53.5 2.5 %collective-permute-start.2 = (f32[16,16,128]{2,1,0:T(8,128)S(1)}, f32[16,16,128]{2,1,0:T(8,128)S(1)}, u32[]{:S(2)}, u32[]{:S(2)}) collective-permute-start(f32[16,16,128]{2,1,0:T(8,128)S(1)} %dynamic-slice_bitcast_fusion), channel_id=1, source_target_pairs={{16,64},{80,128},{144,192},{208,256},{272,320},{336,384},{400,448}... | collective-permute-start | bytes 393224 | tf_op jit(solution)/shard_map/ppermute | solution.py:467
  55.9 3.8 %collective-permute-done.2.edge = f32[16,16,128]{2,1,0:T(8,128)S(1)} collective-permute-done((f32[16,16,128]{2,1,0:T(8,128)S(1)}, f32[16,16,128]{2,1,0:T(8,128)S(1)}, u32[]{:S(2)}, u32[]{:S(2)}) %collective-permute-start.2) | collective-permute-done | bytes 131104 | tf_op jit(solution)/shard_map/ppermute | solution.py:467
  59.7 0.0 collective-permute-done.1.partner
  59.7 0.0 copy-done.1
  59.7 0.0 copy-done.7
  59.8 0.0 copy-start.3
  59.8 2.1 %filter.2 = (f32[32,16,128]{2,1,0:T(8,128)S(1)}, f32[16,16,128]{2,1,0:T(8,128)S(1)}) custom-call(f32[32,16,128]{2,1,0:T(8,128)S(1)} %all_to_all.20.block, f32[32,16,128]{2,1,0:T(8,128)S(1)} %collective-permute-done.1.partner, f32[16,16,128]{2,1,0:T(8,128)S(1)} %collective-permute-done.2.edge, f32[512,128]{1,0:T(8,128)S(1)} %bitcast.7, ...), custom_call_target="tpu_custom_call" | custom-call | tf_op jit(solution)/shard_map/filter/pallas_call | solution.py:437
  61.9 0.0 copy-start.2
  61.9 3.7 %collective-permute-start.3 = (f32[32,16,128]{2,1,0:T(8,128)S(1)}, f32[32,16,128]{2,1,0:T(8,128)S(1)}, u32[]{:S(2)}, u32[]{:S(2)}) collective-permute-start(f32[32,16,128]{2,1,0:T(8,128)S(1)} %get-tuple-element.15.block), channel_id=1, source_target_pairs={{0,16},{16,0},{1,17},{17,1},{2,18},{18,2},{3,19},{19,3},{4,20},{20... | collective-permute-start | bytes 786440 | tf_op jit(solution)/shard_map/ppermute | solution.py:466
  65.6 1.9 %collective-permute-start.4 = (f32[16,16,128]{2,1,0:T(8,128)S(1)}, f32[16,16,128]{2,1,0:T(8,128)S(1)}, u32[]{:S(2)}, u32[]{:S(2)}) collective-permute-start(f32[16,16,128]{2,1,0:T(8,128)S(1)} %get-tuple-element.16), channel_id=1, source_target_pairs={{16,64},{80,128},{144,192},{208,256},{272,320},{336,384},{400,448}... | collective-permute-start | bytes 393224 | tf_op jit(solution)/shard_map/ppermute | solution.py:467
  67.5 4.4 %collective-permute-done.4.edge = f32[16,16,128]{2,1,0:T(8,128)S(1)} collective-permute-done((f32[16,16,128]{2,1,0:T(8,128)S(1)}, f32[16,16,128]{2,1,0:T(8,128)S(1)}, u32[]{:S(2)}, u32[]{:S(2)}) %collective-permute-start.4) | collective-permute-done | bytes 131104 | tf_op jit(solution)/shard_map/ppermute | solution.py:467
  71.9 0.0 collective-permute-done.3.partner
  71.9 2.1 %filter.3 = f32[32,16,128]{2,1,0:T(8,128)S(1)} custom-call(f32[32,16,128]{2,1,0:T(8,128)S(1)} %get-tuple-element.15.block, f32[32,16,128]{2,1,0:T(8,128)S(1)} %collective-permute-done.3.partner, f32[16,16,128]{2,1,0:T(8,128)S(1)} %collective-permute-done.4.edge, f32[512,128]{1,0:T(8,128)S(1)} %bitcast.8, s32[4,128]{1,0:T(4,128)S(1)} %copy-done.8, ...), custom_call_target="tpu_custom_call" | custom-call | tf_op jit(solution)/shard_map/filter/pallas_call | solution.py:437
  74.0 17.6 %all_to_all.21.blocks = f32[32,16,128]{2,1,0:T(8,128)S(1)} all-to-all(f32[32,16,128]{2,1,0:T(8,128)S(1)} %filter.3), channel_id=1, replica_groups=mesh['y'=8,'zh'=2,'c'=2,'x'=4,'zl'=4] {'zh','x','zl'}, dimensions={0} | all-to-all | bytes 524288 | tf_op jit(solution)/shard_map/all_to_all | solution.py:453
  91.6 0.0 copy-done.3
  91.6 0.0 copy-done.2
  91.6 0.8 inverse.1
  92.5 14.0 %all_to_all.22.blocks = f32[16,32,128]{2,1,0:T(8,128)S(1)} all-to-all(f32[16,32,128]{2,1,0:T(8,128)S(1)} %inverse.1), channel_id=1, replica_groups=mesh['y'=8,'zh'=2,'c'=2,'x'=4,'zl'=4] {'x','zl'}, dimensions={0} | all-to-all | bytes 524288 | tf_op jit(solution)/shard_map/all_to_all | solution.py:453
  106.5 0.8 receive.1
  (1 shorter events, 0.0 us)
Async XLA Ops:
  0.0 0.7 copy-start.8
  0.7 0.9 copy-start
  1.6 0.9 copy-start.6
  2.6 21.6 %copy-start.4 = (bf16[8,256,256]{2,1,0:T(8,128)(2,1)S(1)}, bf16[8,256,256]{2,1,0:T(8,128)(2,1)}, u32[]{:S(2)}) copy-start(bf16[8,256,256]{2,1,0:T(8,128)(2,1)} %constant.23.clone.low) | copy-start | bytes 3145732
  3.4 20.7 %all-to-all-start = ((f32[16,32,128]{2,1,0:T(8,128)}), f32[16,32,128]{2,1,0:T(8,128)S(1)}, u32[]{:S(2)}, u32[]{:S(2)}) async-start(f32[16,32,128]{2,1,0:T(8,128)} %get-tuple-element.11), calls=%async_computation | async-start | bytes 524288 | tf_op jit(solution)/shard_map/all_to_all | solution.py:453
  13.3 13.9 %collective-permute-start = (f32[2,128,128]{2,1,0:T(8,128)S(1)}, f32[2,128,128]{2,1,0:T(8,128)S(1)}, u32[]{:S(2)}, u32[]{:S(2)}) collective-permute-start(f32[2,128,128]{2,1,0:T(8,128)S(1)} %get-tuple-element.12), channel_id=1, source_target_pairs={{0,32},{32,0},{1,33},{33,1},{2,34},{34,2},{3,35},{35,3},{4,36},{36... | collective-permute-start | bytes 393224 | tf_op jit(solution)/shard_map/ppermute | solution.py:460
  24.1 1.2 %copy-start.5 = (bf16[8,256,256]{2,1,0:T(8,128)(2,1)S(1)}, bf16[8,256,256]{2,1,0:T(8,128)(2,1)}, u32[]{:S(2)}) copy-start(bf16[8,256,256]{2,1,0:T(8,128)(2,1)} %constant.22.clone.high) | copy-start | bytes 3145732
  51.4 8.4 %copy-start.1 = (f32[2,64,4,128]{3,2,1,0:T(4,128)S(1)}, f32[2,64,4,128]{3,2,1,0:T(4,128)}, u32[]{:S(2)}) copy-start(f32[2,64,4,128]{3,2,1,0:T(4,128)} %param.9) | copy-start | bytes 786436
  51.4 8.4 %collective-permute-start.1 = (f32[32,16,128]{2,1,0:T(8,128)S(1)}, f32[32,16,128]{2,1,0:T(8,128)S(1)}, u32[]{:S(2)}, u32[]{:S(2)}) collective-permute-start(f32[32,16,128]{2,1,0:T(8,128)S(1)} %all_to_all.20.block), channel_id=1, source_target_pairs={{0,16},{16,0},{1,17},{17,1},{2,18},{18,2},{3,19},{19,3},{4,20},{20... | collective-permute-start | bytes 786440 | tf_op jit(solution)/shard_map/ppermute | solution.py:466
  53.4 6.3 %copy-start.7 = (bf16[32,128]{1,0:T(8,128)(2,1)S(1)}, bf16[32,128]{1,0:T(8,128)(2,1)}, u32[]{:S(2)}) copy-start(bf16[32,128]{1,0:T(8,128)(2,1)} %constant.26.clone.spread) | copy-start | bytes 24580
  53.5 6.3 %collective-permute-start.2 = (f32[16,16,128]{2,1,0:T(8,128)S(1)}, f32[16,16,128]{2,1,0:T(8,128)S(1)}, u32[]{:S(2)}, u32[]{:S(2)}) collective-permute-start(f32[16,16,128]{2,1,0:T(8,128)S(1)} %dynamic-slice_bitcast_fusion), channel_id=1, source_target_pairs={{16,64},{80,128},{144,192},{208,256},{272,320},{336,384},{400,448}... | collective-permute-start | bytes 393224 | tf_op jit(solution)/shard_map/ppermute | solution.py:467
  59.8 31.9 %copy-start.3 = (bf16[8,256,256]{2,1,0:T(8,128)(2,1)S(1)}, bf16[8,256,256]{2,1,0:T(8,128)(2,1)}, u32[]{:S(2)}) copy-start(bf16[8,256,256]{2,1,0:T(8,128)(2,1)} %constant.24.clone.high) | copy-start | bytes 3145732
  61.9 29.8 %copy-start.2 = (bf16[8,256,256]{2,1,0:T(8,128)(2,1)S(1)}, bf16[8,256,256]{2,1,0:T(8,128)(2,1)}, u32[]{:S(2)}) copy-start(bf16[8,256,256]{2,1,0:T(8,128)(2,1)} %constant.25.clone.low) | copy-start | bytes 3145732
  61.9 10.0 %collective-permute-start.3 = (f32[32,16,128]{2,1,0:T(8,128)S(1)}, f32[32,16,128]{2,1,0:T(8,128)S(1)}, u32[]{:S(2)}, u32[]{:S(2)}) collective-permute-start(f32[32,16,128]{2,1,0:T(8,128)S(1)} %get-tuple-element.15.block), channel_id=1, source_target_pairs={{0,16},{16,0},{1,17},{17,1},{2,18},{18,2},{3,19},{19,3},{4,20},{20... | collective-permute-start | bytes 786440 | tf_op jit(solution)/shard_map/ppermute | solution.py:466
  65.6 6.3 %collective-permute-start.4 = (f32[16,16,128]{2,1,0:T(8,128)S(1)}, f32[16,16,128]{2,1,0:T(8,128)S(1)}, u32[]{:S(2)}, u32[]{:S(2)}) collective-permute-start(f32[16,16,128]{2,1,0:T(8,128)S(1)} %get-tuple-element.16), channel_id=1, source_target_pairs={{16,64},{80,128},{144,192},{208,256},{272,320},{336,384},{400,448}... | collective-permute-start | bytes 393224 | tf_op jit(solution)/shard_map/ppermute | solution.py:467

commit v3 on v2

v3 whole, which is shorter than its diff:
```python
import functools
import math

import jax
import jax.numpy as jnp
import numpy as np
from jax import lax
from jax.experimental import pallas as pl
from jax.experimental.pallas import tpu as pltpu
from jax.sharding import PartitionSpec as P

NT = 2048
FILT = 4
ITERS = 2
RADIX = 16
SPAN = 128
BINS = 64
WINDOWS = 4
WX = 32
ROWS = 16
UNITS = 8
LANES = 128
f32, bf16 = jnp.float32, jnp.bfloat16


def low_bin(m, s, b):
    residue = m if s == 0 else (8 if m == 0 else RADIX - m)
    return 16 * b + residue


INNER = [(s, b) for s in range(2) for b in range(2)]
HALF = BINS // 2


def held_bins(part):
    zh, x, zl = part // 16, part // 4 % 4, part % 4
    z = 4 * zh + zl
    half, source = (0, z - 2) if 2 <= z <= 5 else (1, (z + 2) % 8)
    return half, 4 * x + source


def split_table(table):
    high = table.astype(np.float32).astype(bf16)
    low = (table - high.astype(np.float64)).astype(np.float32).astype(bf16)
    return high, low


def transform_tables():
    forward = np.zeros((2, 2 * SPAN, 2 * SPAN))
    inverse = np.zeros((2, 2 * SPAN, 2 * SPAN))
    r = np.arange(SPAN)
    for part in range(2 * RADIX):
        half, g = held_bins(part)
        for place, (s, b) in enumerate(INNER):
            base = BINS * g + HALF * half + 16 * b
            col = part * 4 + place
            f = base + 8 * s
            angle = 2.0 * np.pi * ((f * r) % NT) / NT
            span = slice(s * SPAN, (s + 1) * SPAN)
            forward[0, span, col] = np.cos(angle)
            forward[0, span, SPAN + col] = -np.sin(angle)
            angle = 2.0 * np.pi * (((base // RADIX + s) * r) % SPAN) / SPAN
            sign = 1.0 if s == 0 else -1.0
            forward[1, :SPAN, col] = np.cos(angle)
            forward[1, SPAN:, col] = sign * np.sin(angle)
            forward[1, :SPAN, SPAN + col] = -np.sin(angle)
            forward[1, SPAN:, SPAN + col] = sign * np.cos(angle)
            scale = (1.0 if f == 0 else 2.0) / NT
            for which, factor in ((0, scale), (1, 1.0 / NT)):
                inverse[which, col] = forward[which, :, col] * factor
                inverse[which, SPAN + col] = forward[which, :, SPAN + col] * factor
    return split_table(forward), split_table(inverse)


def turn_table():
    angle = 2.0 * np.pi * np.arange(8)[:, None] * np.arange(SPAN)[None] / NT
    return np.stack([np.cos(angle), np.sin(angle)]).astype(np.float32)


def spread_table():
    table = np.zeros((HALF, LANES), np.float32)
    for m in range(8):
        for place, (s, b) in enumerate(INNER):
            for quarter in range(4):
                table[low_bin(m, s, b), quarter * HALF + m * 4 + place] = 1.0
    return table.astype(bf16)


def cadd(a, b):
    im = a[1] if b[1] is None else (b[1] if a[1] is None else a[1] + b[1])
    return a[0] + b[0], im


def csub(a, b):
    im = a[1] if b[1] is None else (-b[1] if a[1] is None else a[1] - b[1])
    return a[0] - b[0], im


def conj(a):
    return a[0], None if a[1] is None else -a[1]


def turn(a, step, size):
    step = step % size
    if step == 0:
        return a
    if 4 * step == size:
        return (jnp.zeros_like(a[0]) if a[1] is None else -a[1]), a[0]
    if 4 * step == 3 * size:
        return (jnp.zeros_like(a[0]) if a[1] is None else a[1]), -a[0]
    c, s = math.cos(2 * math.pi * step / size), math.sin(2 * math.pi * step / size)
    if a[1] is None:
        return a[0] * c, a[0] * s
    return a[0] * c - a[1] * s, a[0] * s + a[1] * c


def real_transform(values):
    n = len(values)
    if n == 1:
        return [(values[0], None)]
    if n == 2:
        return [(values[0] + values[1], None), (values[0] - values[1], None)]
    even, odd = real_transform(values[::2]), real_transform(values[1::2])
    out = [None] * (n // 2 + 1)
    for p in range(n // 4 + 1):
        turned = turn(odd[p], -p, n)
        out[p] = cadd(even[p], turned)
        out[n // 2 - p] = conj(csub(even[p], turned))
    out[0] = (out[0][0], None)
    out[n // 2] = (out[n // 2][0], None)
    return out


def real_inverse(bins):
    n = 2 * (len(bins) - 1)
    if n == 2:
        return [bins[0][0] + bins[1][0], bins[0][0] - bins[1][0]]
    quarter = n // 4
    first, second = [], []
    for p in range(quarter + 1):
        other = conj(bins[n // 2 - p])
        total, rest = cadd(bins[p], other), turn(csub(bins[p], other), p, n)
        if p in (0, quarter):
            total, rest = (total[0], None), (rest[0], None)
        first.append(total)
        second.append(rest)
    out = [None] * n
    out[::2], out[1::2] = real_inverse(first), real_inverse(second)
    return out


def split_dot(lhs, high, low):
    rows = lhs.shape[0]
    top = lhs.astype(bf16)
    rest = (lhs - top.astype(f32)).astype(bf16)
    both = jnp.dot(jnp.concatenate([top, rest], axis=0), high, preferred_element_type=f32)
    return both[:rows] + both[rows:] + jnp.dot(top, low, preferred_element_type=f32)


def swap_blocks(arrays, lane, width):
    arrays = list(arrays)
    n = len(arrays)
    d = 1
    while d < n:
        upper = (lane & (width * d)) != 0
        for i in range(n):
            if i & d:
                continue
            a, b = arrays[i], arrays[i + d]
            arrays[i] = jnp.where(upper, pltpu.roll(b, width * d, 1), a)
            arrays[i + d] = jnp.where(upper, b, pltpu.roll(a, LANES - width * d, 1))
        d *= 2
    return arrays


def lanes_of(rows):
    return lax.broadcasted_iota(jnp.int32, (rows, LANES), 1)


def send_kernel(traces, out):
    for i in range(FILT):
        turned = traces[pl.ds(i, SPAN, stride=FILT), :].T
        for w in range(WINDOWS):
            out[w * FILT + i] = turned[w * WX : (w + 1) * WX]


def share_kernel(weights, live, plus, minus):
    alive = live[...].astype(f32)
    pair = jnp.concatenate([alive, alive], axis=0)
    count = HALF * FILT
    own = lax.axis_index("zh") * count
    for n in range(ITERS):
        for target, first in ((plus, own), (minus, count - own)):
            for k in range(0, count, 8):
                start = pl.multiple_of(n * BINS * FILT + first + k, 8)
                target[n, k : k + 8, :] = weights[pl.ds(start, 8), :] * pair


def forward_kernel(blocks, live, high, low, turns, out, alive):
    row = live[pl.ds(lax.axis_index("zl"), 1), :].astype(f32)
    alive[...] = jnp.broadcast_to(row, (LANES, LANES)).T
    mask = alive[pl.ds(pl.multiple_of(lax.axis_index("x") * WX, WX), WX), :]
    lane = lanes_of(WX)
    bins = real_transform([blocks[j] * mask for j in range(RADIX)])
    first = split_dot(jnp.concatenate([bins[0][0], bins[8][0]], axis=1), high[0], low[0])
    rows = []
    for m in range(1, 8):
        (re, im), c, s = bins[m], turns[0, m : m + 1, :], turns[1, m : m + 1, :]
        rows.append(jnp.concatenate([re * c + im * s, im * c - re * s], axis=1))
    others = split_dot(jnp.concatenate(rows, axis=0), high[1], low[1])
    real = [first[:, :LANES]] + [others[WX * m : WX * m + WX, :LANES] for m in range(7)]
    imag = [first[:, LANES:]] + [others[WX * m : WX * m + WX, LANES:] for m in range(7)]
    real, imag = swap_blocks(real, lane, 4), swap_blocks(imag, lane, 4)
    for k in range(8):
        pieces = [real[k][:16], real[k][16:], imag[k][:16], imag[k][16:]]
        for top, tile in enumerate(swap_blocks(pieces, lanes_of(16), HALF)):
            out[top * 8 + k] = tile


def inverse_kernel(blocks, high, low, turns, out):
    lane = lanes_of(WX)
    real, imag = [], []
    for k in range(8):
        pieces = swap_blocks([blocks[top * 8 + k] for top in range(4)], lanes_of(16), HALF)
        real.append(jnp.concatenate(pieces[:2], axis=0))
        imag.append(jnp.concatenate(pieces[2:], axis=0))
    real, imag = swap_blocks(real, lane, 4), swap_blocks(imag, lane, 4)
    first = split_dot(jnp.concatenate([real[0], imag[0]], axis=1), high[0], low[0])
    rows = [jnp.concatenate([real[m], imag[m]], axis=1) for m in range(1, 8)]
    others = split_dot(jnp.concatenate(rows, axis=0), high[1], low[1])
    bins = [(first[:, :LANES], None)] + [None] * 7 + [(first[:, LANES:], None)]
    for m in range(1, 8):
        value = others[WX * (m - 1) : WX * m]
        re, im, c, s = value[:, :LANES], value[:, LANES:], turns[0, m : m + 1, :], turns[1, m : m + 1, :]
        bins[m] = (re * c - im * s, re * s + im * c)
    for j, values in enumerate(real_inverse(bins)):
        out[j] = values


def receive_kernel(blocks, out):
    for i in range(FILT):
        rows = jnp.concatenate([blocks[w * FILT + i] for w in range(WINDOWS)], axis=0)
        out[pl.ds(i, SPAN, stride=FILT), :] = rows.T


def solve(matrix, target):
    n = FILT
    trace = matrix[0][0][0]
    for k in range(1, n):
        trace = trace + matrix[k][k][0]
    ridge = (0.05 * 2.0 / (2 * n)) * trace + 1e-05

    def cmul(a, b):
        return a[0] * b[0] - a[1] * b[1], a[0] * b[1] + a[1] * b[0]

    diag = [matrix[k][k][0] + ridge for k in range(n)]
    upper = {(k, l): matrix[k][l] for k in range(n) for l in range(k + 1, n)}
    rhs = list(target)
    inv = [None] * n
    for k in range(n):
        inv[k] = 1.0 / diag[k]
        for i in range(k + 1, n):
            re, im = upper[k, i]
            factor = (re * inv[k], -im * inv[k])
            diag[i] = diag[i] - (re * factor[0] - im * factor[1])
            for l in range(i + 1, n):
                t = cmul(factor, upper[k, l])
                upper[i, l] = (upper[i, l][0] - t[0], upper[i, l][1] - t[1])
            t = cmul(factor, rhs[k])
            rhs[i] = (rhs[i][0] - t[0], rhs[i][1] - t[1])
    found = [None] * n
    for k in reversed(range(n)):
        re, im = rhs[k]
        for l in range(k + 1, n):
            t = cmul(upper[k, l], found[l])
            re, im = re - t[0], im - t[1]
        found[k] = (re * inv[k], im * inv[k])
    return found


PAIRS = [(k, l) for k in range(FILT) for l in range(k, FILT)]
OFF = [(k, l) for k, l in PAIRS if k < l]
SUMS = len(PAIRS) + len(OFF) + 2 * FILT


def prepare_kernel(plus, minus, spread, omega):
    z = 4 * lax.axis_index("zh") + lax.axis_index("zl")
    inner = jnp.where((z >= 2) & (z <= 5), 0, 1)
    table = spread[...]
    over = (((0,), (0,)), ((), ()))
    upper = (lanes_of(ROWS) & HALF) != 0
    for n in range(ITERS):
        for i in range(FILT):
            for source, beta in ((plus, inner), (minus, 1 - inner)):
                rows = source[n, pl.ds(i, HALF, stride=FILT), :]
                top = rows.astype(bf16)
                rest = (rows - top.astype(f32)).astype(bf16)
                wide = lax.dot_general(top, table, over, preferred_element_type=f32) + lax.dot_general(
                    rest, table, over, preferred_element_type=f32
                )
                for w in range(WINDOWS):
                    first, second = wide[w * WX : w * WX + ROWS], wide[w * WX + ROWS : (w + 1) * WX]
                    omega[n, beta * WINDOWS + w, i * ROWS : (i + 1) * ROWS] = jnp.where(upper, second, first)


def predictions(jobs, omega, turned, sums, coefs, store):
    slots = WINDOWS * len(jobs)
    blocks = []
    for own, side, _, _ in jobs:
        blocks += [ref for ref in (own, side) if all(ref is not other for other in blocks)]
    for place, ref in enumerate(blocks):
        for k in range(4 * FILT):
            turned[place, k] = pltpu.roll(ref[k], BINS, 1)
    places = [[next(p for p, other in enumerate(blocks) if other is ref) for ref in job[:2]] for job in jobs]

    def tile_of(row, w, flip):
        row = row % FILT
        return w * FILT + row + flip * (FILT - 1 - 2 * row)

    def rows_of(job, w, lines):
        own, side, _, flip = jobs[job]
        plain, quarter = [], []
        for row in range(2 * FILT):
            which, tile = row // FILT, tile_of(row, w, flip)
            plain.append((own, side)[which][tile, lines, :])
            quarter.append(turned[places[job][which], tile, lines, :])
        return plain, quarter

    def weight_of(job, i, w, sub):
        _, _, beta, flip = jobs[job]
        start = tile_of(i, 0, flip) * ROWS + sub * 8
        return omega[beta * WINDOWS + w, pl.ds(pl.multiple_of(start, 8), 8), :]

    def gather(w, carry):
        for job in range(len(jobs)):
            acc = [None] * SUMS

            def add(place, value):
                acc[place] = value if acc[place] is None else acc[place] + value

            for sub in range(ROWS // 8):
                rows, turns = rows_of(job, w, pl.ds(sub * 8, 8))
                for i in range(FILT):
                    om = weight_of(job, i, w, sub)
                    weighted = [om * rows[i + k + 1] for k in range(FILT)]
                    place = 0
                    for k, l in PAIRS:
                        add(place, weighted[k] * rows[i + l + 1])
                        place += 1
                    for k, l in OFF:
                        add(place, weighted[k] * turns[i + l + 1])
                        place += 1
                    for k in range(FILT):
                        add(place, weighted[k] * rows[i])
                        add(place + 1, weighted[k] * turns[i])
                        place += 2
            start = pl.multiple_of((job * WINDOWS + w) * 8, 8)
            for place in range(SUMS):
                sums[place, pl.ds(start, 8), :] = acc[place]
        return carry

    lax.fori_loop(0, WINDOWS, gather, 0)

    sign = jnp.where(lanes_of(slots) < BINS, 1.0, -1.0).astype(f32)

    def total(place):
        value = sums[place, pl.ds(0, slots, stride=8), :]
        for s in range(1, 8):
            value = value + sums[place, pl.ds(s, slots, stride=8), :]
        return value

    def both_halves(value):
        return value + pltpu.roll(value, HALF, 1)

    def real_sum(place):
        value = total(place)
        return both_halves(value + pltpu.roll(value, BINS, 1))

    def imag_sum(place):
        value = total(place)
        return both_halves((value - pltpu.roll(value, BINS, 1)) * sign)

    matrix = [[None] * FILT for _ in range(FILT)]
    for place, (k, l) in enumerate(PAIRS):
        matrix[k][l] = (real_sum(place), None)
    for place, (k, l) in enumerate(OFF):
        matrix[k][l] = (matrix[k][l][0], imag_sum(len(PAIRS) + place))
    base = len(PAIRS) + len(OFF)
    target = [(real_sum(base + 2 * k), imag_sum(base + 2 * k + 1)) for k in range(FILT)]
    for k, (re, im) in enumerate(solve(matrix, target)):
        coefs[2 * k] = re
        coefs[2 * k + 1] = -im * sign

    def predict(w, carry):
        for sub in range(ROWS // 8):
            lines = pl.ds(sub * 8, 8)
            for job in range(len(jobs)):
                rows, turns = rows_of(job, w, lines)
                acc = [None] * FILT
                for k in range(FILT):
                    one = coefs[2 * k, pl.ds(job * WINDOWS + w, 1), :]
                    two = coefs[2 * k + 1, pl.ds(job * WINDOWS + w, 1), :]
                    for i in range(FILT):
                        value = one * rows[i + k + 1] + two * turns[i + k + 1]
                        acc[i] = value if acc[i] is None else acc[i] + value
                for i in range(FILT):
                    store(job, tile_of(i, w, jobs[job][3]), lines, acc[i], weight_of(job, i, w, sub))
        return carry

    lax.fori_loop(0, WINDOWS, predict, 0)


def beyond_kernel(n, beyond, edge, omegas, held, *refs):
    core = lax.axis_index("c")

    *outs, turned, sums, coefs = refs
    rest_at, edge_at = (0, 1) if n + 1 < ITERS else (1 - core, core)

    def store(job, tile, lines, value, weight):
        half = jnp.where(weight > 0.0, 0.5, 0.0)
        value = (value + held[1, tile, lines, :]) * half
        outs[0][edge_at, tile, lines, :] = value
        if n + 1 < ITERS:
            outs[1][tile, lines, :] = value

    predictions([(edge, beyond, core, 1 - core)], omegas.at[n], turned, sums, coefs, store)
    for k in range(4 * FILT):
        outs[0][rest_at, k] = held[0, k]


def filter_kernel(n, own, partner, omegas, out, turned, sums, coefs):
    core = lax.axis_index("c")
    rest_at, edge_at = (1 - core, core) if n == 0 else (0, 1)
    rest, edge = own.at[rest_at], own.at[edge_at]
    near, far = (partner.at[core], partner.at[1 - core]) if n == 0 else (partner.at[0], partner.at[1])

    def store(job, tile, lines, value, weight):
        if job == 0:
            out[1, tile, lines, :] = value
        elif job == 1:
            out[0, tile, lines, :] = value
        else:
            out[0, tile, lines, :] = (out[0, tile, lines, :] + value) * jnp.where(weight > 0.0, 0.5, 0.0)

    jobs = [(edge, near, core, core), (rest, near, 1 - core, 1 - core), (rest, far, 1 - core, core)]
    predictions(jobs, omegas.at[n], turned, sums, coefs, store)


def kernel_call(body, shapes, scratch=(), name=None):
    out = [jax.ShapeDtypeStruct(shape, f32) for shape in shapes]
    return pl.pallas_call(
        body,
        out_shape=out if len(out) > 1 else out[0],
        scratch_shapes=list(scratch),
        compiler_params=pltpu.CompilerParams(vmem_limit_bytes=16 * 1024 * 1024),
        name=name,
    )


TRACES = (RADIX, WX, LANES)
TILES = (8 * FILT, ROWS, LANES)
EDGE = (4 * FILT, ROWS, LANES)
GIVE = (ITERS, HALF * FILT, LANES)


def send_call(traces):
    return kernel_call(send_kernel, [TRACES], name="send")(traces.reshape(SPAN * FILT, LANES))


def share_call(weights, live):
    return kernel_call(share_kernel, [GIVE, GIVE], name="share")(weights, live)


def forward_call(blocks, live, *tables):
    scratch = [pltpu.VMEM((LANES, LANES), f32)]
    return kernel_call(forward_kernel, [TILES], scratch, "forward")(blocks, live, *tables)


def inverse_call(blocks, *tables):
    return kernel_call(inverse_kernel, [TRACES], name="inverse")(blocks, *tables)


def prepare_call(plus, minus, spread):
    shape = (ITERS, UNITS, FILT * ROWS, LANES)
    return kernel_call(prepare_kernel, [shape], name="prepare")(plus, minus, spread)


def filter_scratch(blocks, jobs):
    return [
        pltpu.VMEM((blocks,) + EDGE, f32),
        pltpu.VMEM((SUMS, 8 * WINDOWS * jobs, LANES), f32),
        pltpu.VMEM((2 * FILT, WINDOWS * jobs, LANES), f32),
    ]


def beyond_call(n, beyond, edge, omegas, held):
    both = (2,) + EDGE
    body = functools.partial(beyond_kernel, n)
    shapes = [both, EDGE] if n + 1 < ITERS else [both]
    return kernel_call(body, shapes, filter_scratch(2, 1), name="beyond")(beyond, edge, omegas, held)


def filter_call(n, own, partner, omegas):
    body = functools.partial(filter_kernel, n)
    return kernel_call(body, [(2,) + EDGE], filter_scratch(4, 3), name="filter")(own, partner, omegas)


def receive_call(blocks):
    return kernel_call(receive_kernel, [(SPAN * FILT, LANES)], name="receive")(blocks).reshape(
        SPAN, FILT, LANES
    )


def local(tables, traces_in, reweights, live_mask):
    (fh, fl), (ih, il), spread, turns = tables
    fh, fl, ih, il, spread, turns = (jnp.asarray(t) for t in (fh, fl, ih, il, spread, turns))

    def exchange(blocks, axes):
        return lax.all_to_all(blocks, axes, 0, 0, tiled=True)

    swap = [(0, 1), (1, 0)]
    ys = lax.axis_size("y")
    shift = [(2 * y + 1, 2 * y + 2) for y in range(ys - 1)] + [(2 * y + 2, 2 * y + 1) for y in range(ys - 1)]
    weights = reweights.reshape(ITERS * BINS * FILT, LANES)
    sent = send_call(traces_in)
    plus, minus = share_call(weights, live_mask)
    plus = lax.ppermute(plus, ("zh", "zl"), [(z, (z + 2) % 8) for z in range(8)])
    minus = lax.ppermute(minus, ("zh", "zl"), [(z, (z - 2) % 8) for z in range(8)])
    spectra = forward_call(exchange(sent, ("x", "zl")), live_mask, fh, fl, turns)
    spectra, plus, minus = lax.optimization_barrier((spectra, plus, minus))
    block = exchange(spectra, ("zh", "x", "zl"))
    omegas = prepare_call(plus, minus, spread)
    block = block.reshape((2,) + EDGE)
    edge = lax.dynamic_index_in_dim(block, lax.axis_index("c"), 0, False)
    for n in range(ITERS):
        beyond = lax.ppermute(edge, ("y", "c"), shift)
        partner = lax.ppermute(block, "c", swap)
        held = filter_call(n, block, partner, omegas)
        found = beyond_call(n, beyond, edge, omegas, held)
        block, edge = found if n + 1 < ITERS else (found, None)
    back = exchange(block.reshape(TILES), ("zh", "x", "zl"))
    return receive_call(exchange(inverse_call(back, ih, il, turns), ("x", "zl")))


def solution(mesh):
    tables = (*transform_tables(), spread_table(), turn_table())

    def run(traces_in, reweights, live_mask):
        return local(tables, traces_in, reweights, live_mask)

    inner = jax.sharding.Mesh(mesh.devices.reshape(-1, 2, 2, 4, 4), ("y", "zh", "c", "x", "zl"))
    inline, freq = ("y", "zh", "c"), ("x", "zl")
    in_specs = (P(freq, inline, None), P(None, freq, inline, None), P(inline, None))
    out_specs = P(freq, inline, None)
    return jax.shard_map(run, mesh=inner, in_specs=in_specs, out_specs=out_specs, check_vma=False)
```

time: 108 us -> 102 us (0.944)
  blocking collectives: 55.9 us -> 53 us
  local copies, waits for them, and re-layouts: 3.85 us -> 1.01 us
  waiting for transfers between devices: 11.7 us -> 8.86 us
  starting transfers between devices: 28.2 us -> 30.5 us
    ppermute x2, waiting for transfers between devices: 8.18 us -> 4.63 us  [local(): beyond = lax.ppermute(edge, ('y', 'c'), shift)]
    ppermute x1 -> x2, waiting for transfers between devices: 0.91 us -> 4.03 us  [the longest x1 2.1 us: local(): lax.ppermute(plus, ('zh', 'zl'), [(z, (z + 2) % 8) for z in range(8)])]
    all_to_all x3, blocking collectives: 55.9 us -> 53 us  [exchange(): return lax.all_to_all(blocks, axes, 0, 0, tiled=True)]
    unnamed x18, local copies, waits for them, and re-layouts: 3.83 us -> 0.99 us
    all_to_all x1, waiting for transfers between devices: 2.66 us -> 0.19 us  [exchange(): return lax.all_to_all(blocks, axes, 0, 0, tiled=True)]
    ppermute x1 -> x2, starting transfers between devices: 8.22 us -> 10.6 us  [the longest x1 5.87 us: local(): lax.ppermute(minus, ('zh', 'zl'), [(z, (z - 2) % 8) for z in range(8)])]
    pallas_call x5 -> x9, Pallas kernels: 6.64 us -> 7.37 us  [the longest x2 3.02 us: filter_call(): kernel_call(body, [(2,) + EDGE], filter_scratch(4, 3), name='filter')]
  transfers between devices with their start and end apart: 6 -> 7, of which waited for: 4 -> 5; matrix products, arithmetic and copies ran while one was open for 0% -> 0% of each run, Pallas kernels for 1% -> 4%
where the time goes in v3:
time: 102 us
  blocking collectives  53 us (52%)
  starting transfers between devices  30.5 us (30%)
  waiting for transfers between devices  8.86 us (9%)
  Pallas kernels  8.2 us (8%)
    all_to_all x3, blocking collectives, exchange(): return lax.all_to_all(blocks, axes, 0, 0, tiled=True)  53 us
    all_to_all x1, starting transfers between devices, exchange(): return lax.all_to_all(blocks, axes, 0, 0, tiled=True)  9.96 us
    ppermute x1, starting transfers between devices, local(): lax.ppermute(minus, ('zh', 'zl'), [(z, (z - 2) % 8) for z in range(8)])  5.87 us
    ppermute x2, starting transfers between devices, local(): partner = lax.ppermute(block, 'c', swap)  5.52 us
    ppermute x1, starting transfers between devices, local(): lax.ppermute(plus, ('zh', 'zl'), [(z, (z + 2) % 8) for z in range(8)])  4.73 us
    ppermute x2, waiting for transfers between devices, local(): beyond = lax.ppermute(edge, ('y', 'c'), shift)  4.63 us
    ppermute x2, starting transfers between devices, local(): beyond = lax.ppermute(edge, ('y', 'c'), shift)  4.38 us
    pallas_call x2, Pallas kernels, filter_call(): kernel_call(body, [(2,) + EDGE], filter_scratch(4, 3), name='filter')  3.02 us
  transfers between devices with their start and end apart: 7, of which 5 were waited for; matrix products, arithmetic and copies ran while one was open for 0% of the time, Pallas kernels for 4%

profile of v3, /device:TPU:24, one launch (start us, length us, event | category | flops | bytes accessed | tf_op | source)
XLA Modules:
  0.0 101.8 jit_solution(12333429696387984868)
XLA Ops:
  0.0 0.0 copy-start
  0.0 0.9 copy-done
  1.0 0.0 copy-start.8
  1.0 0.0 copy-start.6
  1.0 0.8 send.1
  1.8 0.0 copy-start.1
  1.8 0.0 copy-start.5
  1.8 10.0 %all-to-all-start = ((f32[16,32,128]{2,1,0:T(8,128)}), f32[16,32,128]{2,1,0:T(8,128)S(1)}, u32[]{:S(2)}, u32[]{:S(2)}) async-start(f32[16,32,128]{2,1,0:T(8,128)} %send.1), calls=%async_computation | async-start | bytes 524288 | tf_op jit(solution)/shard_map/all_to_all | solution.py:519
  11.8 0.0 copy-start.4
  11.8 0.0 copy-done.8
  11.8 0.0 copy-done.1
  11.8 4.7 %collective-permute-start = (f32[2,128,128]{2,1,0:T(8,128)S(1)}, f32[2,128,128]{2,1,0:T(8,128)S(1)}, u32[]{:S(2)}, u32[]{:S(2)}) collective-permute-start(f32[2,128,128]{2,1,0:T(8,128)S(1)} %get-tuple-element.12), channel_id=1, source_target_pairs={{0,2},{1,3},{2,32},{3,33},{32,34},{33,35},{34,0},{35,1},{4,6},{5,7... | collective-permute-start | bytes 393224 | tf_op jit(solution)/shard_map/ppermute | solution.py:527
  16.6 5.9 %collective-permute-start.1 = (f32[2,128,128]{2,1,0:T(8,128)S(1)}, f32[2,128,128]{2,1,0:T(8,128)S(1)}, u32[]{:S(2)}, u32[]{:S(2)}) collective-permute-start(f32[2,128,128]{2,1,0:T(8,128)S(1)} %get-tuple-element.13), channel_id=1, source_target_pairs={{0,34},{1,35},{2,0},{3,1},{32,2},{33,3},{34,32},{35,33},{4,38},{5,... | collective-permute-start | bytes 393224 | tf_op jit(solution)/shard_map/ppermute | solution.py:528
  22.5 0.2 all-to-all-done.blocks
  22.6 0.0 copy-done.6
  22.7 0.0 copy-done.5
  22.7 0.0 copy-done.4
  22.7 0.8 forward.1
  23.5 2.1 %collective-permute-done.plus = f32[2,128,128]{2,1,0:T(8,128)S(1)} collective-permute-done((f32[2,128,128]{2,1,0:T(8,128)S(1)}, f32[2,128,128]{2,1,0:T(8,128)S(1)}, u32[]{:S(2)}, u32[]{:S(2)}) %collective-permute-start) | collective-permute-done | bytes 131104 | tf_op jit(solution)/shard_map/ppermute | solution.py:527
  25.6 1.9 %collective-permute-done.1.minus = f32[2,128,128]{2,1,0:T(8,128)S(1)} collective-permute-done((f32[2,128,128]{2,1,0:T(8,128)S(1)}, f32[2,128,128]{2,1,0:T(8,128)S(1)}, u32[]{:S(2)}, u32[]{:S(2)}) %collective-permute-start.1) | collective-permute-done | bytes 131104 | tf_op jit(solution)/shard_map/ppermute | solution.py:528
  27.5 21.5 %all_to_all.20 = f32[32,16,128]{2,1,0:T(8,128)S(1)} all-to-all(f32[32,16,128]{2,1,0:T(8,128)S(1)} %forward.1), channel_id=1, replica_groups=mesh['y'=8,'zh'=2,'c'=2,'x'=4,'zl'=4] {'zh','x','zl'}, dimensions={0} | all-to-all | bytes 524288 | tf_op jit(solution)/shard_map/all_to_all | solution.py:519
  48.9 1.9 %collective-permute-start.3 = (f32[2,16,16,128]{3,2,1,0:T(8,128)S(1)}, f32[2,16,16,128]{3,2,1,0:T(8,128)S(1)}, u32[]{:S(2)}, u32[]{:S(2)}) collective-permute-start(f32[2,16,16,128]{3,2,1,0:T(8,128)S(1)} %bitcast.7), channel_id=1, source_target_pairs={{0,16},{16,0},{1,17},{17,1},{2,18},{18,2},{3,19},{19,3},{4,20},{20... | collective-permute-start | bytes 786440 | tf_op jit(solution)/shard_map/ppermute | solution.py:537
  50.9 0.0 copy-start.7
  50.9 2.5 %collective-permute-start.2 = (f32[16,16,128]{2,1,0:T(8,128)S(1)}, f32[16,16,128]{2,1,0:T(8,128)S(1)}, u32[]{:S(2)}, u32[]{:S(2)}) collective-permute-start(f32[16,16,128]{2,1,0:T(8,128)S(1)} %dynamic-slice_bitcast_fusion.edge), channel_id=1, source_target_pairs={{16,64},{80,128},{144,192},{208,256},{272,320},{336,384},{400,448}... | collective-permute-start | bytes 393224 | tf_op jit(solution)/shard_map/ppermute | solution.py:536
  53.4 0.0 copy-done.7
  53.4 0.5 prepare.1.omegas
  53.9 0.0 collective-permute-done.3.partner
  53.9 1.5 %filter.2.held = f32[2,16,16,128]{3,2,1,0:T(8,128)S(1)} custom-call(f32[2,16,16,128]{3,2,1,0:T(8,128)S(1)} %bitcast.9, f32[2,16,16,128]{3,2,1,0:T(8,128)S(1)} %collective-permute-done.3.partner, f32[2,8,64,128]{3,2,1,0:T(8,128)S(1)} %prepare.1.omegas), custom_call_target="tpu_custom_call" | custom-call | tf_op jit(solution)/shard_map/filter/pallas_call | solution.py:505
  55.4 1.8 %collective-permute-done.2.beyond = f32[16,16,128]{2,1,0:T(8,128)S(1)} collective-permute-done((f32[16,16,128]{2,1,0:T(8,128)S(1)}, f32[16,16,128]{2,1,0:T(8,128)S(1)}, u32[]{:S(2)}, u32[]{:S(2)}) %collective-permute-start.2) | collective-permute-done | bytes 131104 | tf_op jit(solution)/shard_map/ppermute | solution.py:536
  57.2 0.7 beyond.2
  57.9 3.6 %collective-permute-start.5 = (f32[2,16,16,128]{3,2,1,0:T(8,128)S(1)}, f32[2,16,16,128]{3,2,1,0:T(8,128)S(1)}, u32[]{:S(2)}, u32[]{:S(2)}) collective-permute-start(f32[2,16,16,128]{3,2,1,0:T(8,128)S(1)} %get-tuple-element.18.own), channel_id=1, source_target_pairs={{0,16},{16,0},{1,17},{17,1},{2,18},{18,2},{3,19},{19,3},{4,20},{20... | collective-permute-start | bytes 786440 | tf_op jit(solution)/shard_map/ppermute | solution.py:537
  61.6 1.9 %collective-permute-start.4 = (f32[16,16,128]{2,1,0:T(8,128)S(1)}, f32[16,16,128]{2,1,0:T(8,128)S(1)}, u32[]{:S(2)}, u32[]{:S(2)}) collective-permute-start(f32[16,16,128]{2,1,0:T(8,128)S(1)} %get-tuple-element.17.edge), channel_id=1, source_target_pairs={{16,64},{80,128},{144,192},{208,256},{272,320},{336,384},{400,448}... | collective-permute-start | bytes 393224 | tf_op jit(solution)/shard_map/ppermute | solution.py:536
  63.5 0.0 collective-permute-done.5.partner
  63.5 1.5 %filter.3.held = f32[2,16,16,128]{3,2,1,0:T(8,128)S(1)} custom-call(f32[2,16,16,128]{3,2,1,0:T(8,128)S(1)} %get-tuple-element.18.own, f32[2,16,16,128]{3,2,1,0:T(8,128)S(1)} %collective-permute-done.5.partner, f32[2,8,64,128]{3,2,1,0:T(8,128)S(1)} %prepare.1.omegas), custom_call_target="tpu_custom_call" | custom-call | tf_op jit(solution)/shard_map/filter/pallas_call | solution.py:505
  65.0 2.8 %collective-permute-done.4.beyond = f32[16,16,128]{2,1,0:T(8,128)S(1)} collective-permute-done((f32[16,16,128]{2,1,0:T(8,128)S(1)}, f32[16,16,128]{2,1,0:T(8,128)S(1)}, u32[]{:S(2)}, u32[]{:S(2)}) %collective-permute-start.4) | collective-permute-done | bytes 131104 | tf_op jit(solution)/shard_map/ppermute | solution.py:536
  67.9 0.7 beyond.3
  68.6 0.0 copy-start.2
  68.6 0.0 copy-start.3
  68.6 17.5 %all_to_all.21.blocks = f32[32,16,128]{2,1,0:T(8,128)S(1)} all-to-all(f32[32,16,128]{2,1,0:T(8,128)S(1)} %bitcast.10), channel_id=1, replica_groups=mesh['y'=8,'zh'=2,'c'=2,'x'=4,'zl'=4] {'zh','x','zl'}, dimensions={0} | all-to-all | bytes 524288 | tf_op jit(solution)/shard_map/all_to_all | solution.py:519
  86.1 0.0 copy-done.2
  86.1 0.0 copy-done.3
  86.1 0.7 inverse.1
  86.8 14.1 %all_to_all.22.blocks = f32[16,32,128]{2,1,0:T(8,128)S(1)} all-to-all(f32[16,32,128]{2,1,0:T(8,128)S(1)} %inverse.1), channel_id=1, replica_groups=mesh['y'=8,'zh'=2,'c'=2,'x'=4,'zl'=4] {'x','zl'}, dimensions={0} | all-to-all | bytes 524288 | tf_op jit(solution)/shard_map/all_to_all | solution.py:519
  100.9 0.8 receive.1
  (2 shorter events, 0.1 us)
Async XLA Ops:
  0.0 0.9 copy-start
  1.0 10.8 %copy-start.8 = (s32[4,128]{1,0:T(4,128)S(1)}, s32[4,128]{1,0:T(4,128)}, u32[]{:S(2)}) copy-start(s32[4,128]{1,0:T(4,128)} %live.3) | copy-start | bytes 6148
  1.0 21.7 %copy-start.6 = (f32[2,8,128]{2,1,0:T(8,128)S(1)}, f32[2,8,128]{2,1,0:T(8,128)}, u32[]{:S(2)}) copy-start(f32[2,8,128]{2,1,0:T(8,128)} %constant.29.clone.turns) | copy-start | bytes 24580
  1.8 10.0 %copy-start.1 = (f32[2,64,4,128]{3,2,1,0:T(4,128)S(1)}, f32[2,64,4,128]{3,2,1,0:T(4,128)}, u32[]{:S(2)}) copy-start(f32[2,64,4,128]{3,2,1,0:T(4,128)} %param.10) | copy-start | bytes 786436
  1.8 20.9 %copy-start.5 = (bf16[2,256,256]{2,1,0:T(8,128)(2,1)S(1)}, bf16[2,256,256]{2,1,0:T(8,128)(2,1)}, u32[]{:S(2)}) copy-start(bf16[2,256,256]{2,1,0:T(8,128)(2,1)} %constant.25.clone.low) | copy-start | bytes 786436
  1.8 20.9 %all-to-all-start = ((f32[16,32,128]{2,1,0:T(8,128)}), f32[16,32,128]{2,1,0:T(8,128)S(1)}, u32[]{:S(2)}, u32[]{:S(2)}) async-start(f32[16,32,128]{2,1,0:T(8,128)} %send.1), calls=%async_computation | async-start | bytes 524288 | tf_op jit(solution)/shard_map/all_to_all | solution.py:519
  11.8 10.9 %copy-start.4 = (bf16[2,256,256]{2,1,0:T(8,128)(2,1)S(1)}, bf16[2,256,256]{2,1,0:T(8,128)(2,1)}, u32[]{:S(2)}) copy-start(bf16[2,256,256]{2,1,0:T(8,128)(2,1)} %constant.24.clone.high) | copy-start | bytes 786436
  11.8 13.7 %collective-permute-start = (f32[2,128,128]{2,1,0:T(8,128)S(1)}, f32[2,128,128]{2,1,0:T(8,128)S(1)}, u32[]{:S(2)}, u32[]{:S(2)}) collective-permute-start(f32[2,128,128]{2,1,0:T(8,128)S(1)} %get-tuple-element.12), channel_id=1, source_target_pairs={{0,2},{1,3},{2,32},{3,33},{32,34},{33,35},{34,0},{35,1},{4,6},{5,7... | collective-permute-start | bytes 393224 | tf_op jit(solution)/shard_map/ppermute | solution.py:527
  16.6 10.9 %collective-permute-start.1 = (f32[2,128,128]{2,1,0:T(8,128)S(1)}, f32[2,128,128]{2,1,0:T(8,128)S(1)}, u32[]{:S(2)}, u32[]{:S(2)}) collective-permute-start(f32[2,128,128]{2,1,0:T(8,128)S(1)} %get-tuple-element.13), channel_id=1, source_target_pairs={{0,34},{1,35},{2,0},{3,1},{32,2},{33,3},{34,32},{35,33},{4,38},{5,... | collective-permute-start | bytes 393224 | tf_op jit(solution)/shard_map/ppermute | solution.py:528
  48.9 4.9 %collective-permute-start.3 = (f32[2,16,16,128]{3,2,1,0:T(8,128)S(1)}, f32[2,16,16,128]{3,2,1,0:T(8,128)S(1)}, u32[]{:S(2)}, u32[]{:S(2)}) collective-permute-start(f32[2,16,16,128]{3,2,1,0:T(8,128)S(1)} %bitcast.7), channel_id=1, source_target_pairs={{0,16},{16,0},{1,17},{17,1},{2,18},{18,2},{3,19},{19,3},{4,20},{20... | collective-permute-start | bytes 786440 | tf_op jit(solution)/shard_map/ppermute | solution.py:537
  50.9 2.5 %copy-start.7 = (bf16[32,128]{1,0:T(8,128)(2,1)S(1)}, bf16[32,128]{1,0:T(8,128)(2,1)}, u32[]{:S(2)}) copy-start(bf16[32,128]{1,0:T(8,128)(2,1)} %constant.28.clone.spread) | copy-start | bytes 24580
  50.9 6.3 %collective-permute-start.2 = (f32[16,16,128]{2,1,0:T(8,128)S(1)}, f32[16,16,128]{2,1,0:T(8,128)S(1)}, u32[]{:S(2)}, u32[]{:S(2)}) collective-permute-start(f32[16,16,128]{2,1,0:T(8,128)S(1)} %dynamic-slice_bitcast_fusion.edge), channel_id=1, source_target_pairs={{16,64},{80,128},{144,192},{208,256},{272,320},{336,384},{400,448}... | collective-permute-start | bytes 393224 | tf_op jit(solution)/shard_map/ppermute | solution.py:536
  57.9 5.6 %collective-permute-start.5 = (f32[2,16,16,128]{3,2,1,0:T(8,128)S(1)}, f32[2,16,16,128]{3,2,1,0:T(8,128)S(1)}, u32[]{:S(2)}, u32[]{:S(2)}) collective-permute-start(f32[2,16,16,128]{3,2,1,0:T(8,128)S(1)} %get-tuple-element.18.own), channel_id=1, source_target_pairs={{0,16},{16,0},{1,17},{17,1},{2,18},{18,2},{3,19},{19,3},{4,20},{20... | collective-permute-start | bytes 786440 | tf_op jit(solution)/shard_map/ppermute | solution.py:537
  61.6 6.3 %collective-permute-start.4 = (f32[16,16,128]{2,1,0:T(8,128)S(1)}, f32[16,16,128]{2,1,0:T(8,128)S(1)}, u32[]{:S(2)}, u32[]{:S(2)}) collective-permute-start(f32[16,16,128]{2,1,0:T(8,128)S(1)} %get-tuple-element.17.edge), channel_id=1, source_target_pairs={{16,64},{80,128},{144,192},{208,256},{272,320},{336,384},{400,448}... | collective-permute-start | bytes 393224 | tf_op jit(solution)/shard_map/ppermute | solution.py:536
  68.6 17.5 %copy-start.2 = (bf16[2,256,256]{2,1,0:T(8,128)(2,1)S(1)}, bf16[2,256,256]{2,1,0:T(8,128)(2,1)}, u32[]{:S(2)}) copy-start(bf16[2,256,256]{2,1,0:T(8,128)(2,1)} %constant.26.clone.high) | copy-start | bytes 786436
  68.6 17.5 %copy-start.3 = (bf16[2,256,256]{2,1,0:T(8,128)(2,1)S(1)}, bf16[2,256,256]{2,1,0:T(8,128)(2,1)}, u32[]{:S(2)}) copy-start(bf16[2,256,256]{2,1,0:T(8,128)(2,1)} %constant.27.clone.low) | copy-start | bytes 786436

commit v4 on v3

--- a/solution.py
+++ b/solution.py
@@ -33,10 +33,7 @@
 
 
 def held_bins(part):
-    zh, x, zl = part // 16, part // 4 % 4, part % 4
-    z = 4 * zh + zl
-    half, source = (0, z - 2) if 2 <= z <= 5 else (1, (z + 2) % 8)
-    return half, 4 * x + source
+    return divmod(part, RADIX)
 
 
 def split_table(table):
@@ -184,18 +181,6 @@
             out[w * FILT + i] = turned[w * WX : (w + 1) * WX]
 
 
-def share_kernel(weights, live, plus, minus):
-    alive = live[...].astype(f32)
-    pair = jnp.concatenate([alive, alive], axis=0)
-    count = HALF * FILT
-    own = lax.axis_index("zh") * count
-    for n in range(ITERS):
-        for target, first in ((plus, own), (minus, count - own)):
-            for k in range(0, count, 8):
-                start = pl.multiple_of(n * BINS * FILT + first + k, 8)
-                target[n, k : k + 8, :] = weights[pl.ds(start, 8), :] * pair
-
-
 def forward_kernel(blocks, live, high, low, turns, out, alive):
     row = live[pl.ds(lax.axis_index("zl"), 1), :].astype(f32)
     alive[...] = jnp.broadcast_to(row, (LANES, LANES)).T
@@ -283,16 +268,17 @@
 SUMS = len(PAIRS) + len(OFF) + 2 * FILT
 
 
-def prepare_kernel(plus, minus, spread, omega):
-    z = 4 * lax.axis_index("zh") + lax.axis_index("zl")
-    inner = jnp.where((z >= 2) & (z <= 5), 0, 1)
+def prepare_kernel(weights, live, got, spread, omega):
+    own = lax.axis_index("zh")
+    alive = live[...].astype(f32)
     table = spread[...]
     over = (((0,), (0,)), ((), ()))
     upper = (lanes_of(ROWS) & HALF) != 0
     for n in range(ITERS):
         for i in range(FILT):
-            for source, beta in ((plus, inner), (minus, 1 - inner)):
-                rows = source[n, pl.ds(i, HALF, stride=FILT), :]
+            start = n * BINS * FILT + own * HALF * FILT + i
+            mine = weights[pl.ds(start, HALF, stride=FILT), :] * alive[i : i + 1]
+            for rows, beta in ((mine, own), (got[n, pl.ds(i, HALF, stride=FILT), :], 1 - own)):
                 top = rows.astype(bf16)
                 rest = (rows - top.astype(f32)).astype(bf16)
                 wide = lax.dot_general(top, table, over, preferred_element_type=f32) + lax.dot_general(
@@ -410,43 +396,40 @@
     lax.fori_loop(0, WINDOWS, predict, 0)
 
 
-def beyond_kernel(n, beyond, edge, omegas, held, *refs):
+def beyond_kernel(n, beyond, edge, omegas, out, turned, sums, coefs):
     core = lax.axis_index("c")
 
+    def store(job, tile, lines, value, weight):
+        out[tile, lines, :] = value
+
+    predictions([(edge, beyond, core, 1 - core)], omegas.at[n], turned, sums, coefs, store)
+
+
+def filter_kernel(n, part, own, partner, omegas, *refs):
     *outs, turned, sums, coefs = refs
-    rest_at, edge_at = (0, 1) if n + 1 < ITERS else (1 - core, core)
-
-    def store(job, tile, lines, value, weight):
-        half = jnp.where(weight > 0.0, 0.5, 0.0)
-        value = (value + held[1, tile, lines, :]) * half
-        outs[0][edge_at, tile, lines, :] = value
-        if n + 1 < ITERS:
-            outs[1][tile, lines, :] = value
-
-    predictions([(edge, beyond, core, 1 - core)], omegas.at[n], turned, sums, coefs, store)
-    for k in range(4 * FILT):
-        outs[0][rest_at, k] = held[0, k]
-
-
-def filter_kernel(n, own, partner, omegas, out, turned, sums, coefs):
     core = lax.axis_index("c")
     rest_at, edge_at = (1 - core, core) if n == 0 else (0, 1)
     rest, edge = own.at[rest_at], own.at[edge_at]
     near, far = (partner.at[core], partner.at[1 - core]) if n == 0 else (partner.at[0], partner.at[1])
+    new_rest, new_edge = (outs[0].at[0], outs[0].at[1]) if n + 1 < ITERS else (outs[0].at[1 - core], outs[0].at[core])
 
     def store(job, tile, lines, value, weight):
+        half = jnp.where(weight > 0.0, 0.5, 0.0)
         if job == 0:
-            out[1, tile, lines, :] = value
+            value = (value + part[tile, lines, :]) * half
+            new_edge[tile, lines, :] = value
+            if n + 1 < ITERS:
+                outs[1][tile, lines, :] = value
         elif job == 1:
-            out[0, tile, lines, :] = value
+            new_rest[tile, lines, :] = value
         else:
-            out[0, tile, lines, :] = (out[0, tile, lines, :] + value) * jnp.where(weight > 0.0, 0.5, 0.0)
+            new_rest[tile, lines, :] = (new_rest[tile, lines, :] + value) * half
 
     jobs = [(edge, near, core, core), (rest, near, 1 - core, 1 - core), (rest, far, 1 - core, core)]
     predictions(jobs, omegas.at[n], turned, sums, coefs, store)
 
 
-def kernel_call(body, shapes, scratch=(), name=None):
+def kernel_call(body, shapes, scratch=(), name=None, cost=None):
     out = [jax.ShapeDtypeStruct(shape, f32) for shape in shapes]
     return pl.pallas_call(
         body,
@@ -454,6 +437,7 @@
         scratch_shapes=list(scratch),
         compiler_params=pltpu.CompilerParams(vmem_limit_bytes=16 * 1024 * 1024),
         name=name,
+        cost_estimate=cost,
     )
 
 
@@ -467,8 +451,13 @@
     return kernel_call(send_kernel, [TRACES], name="send")(traces.reshape(SPAN * FILT, LANES))
 
 
-def share_call(weights, live):
-    return kernel_call(share_kernel, [GIVE, GIVE], name="share")(weights, live)
+def share(weights, live):
+    start = (1 - lax.axis_index("zh")) * HALF
+    zero = jnp.zeros_like(start)
+    mine = lax.dynamic_slice(
+        weights, (zero, start, zero, zero), (ITERS, HALF, FILT, LANES), allow_negative_indices=False
+    )
+    return jnp.where(live > 0, mine, 0.0).reshape(GIVE)
 
 
 def forward_call(blocks, live, *tables):
@@ -480,9 +469,10 @@
     return kernel_call(inverse_kernel, [TRACES], name="inverse")(blocks, *tables)
 
 
-def prepare_call(plus, minus, spread):
+def prepare_call(weights, live, got, spread):
     shape = (ITERS, UNITS, FILT * ROWS, LANES)
-    return kernel_call(prepare_kernel, [shape], name="prepare")(plus, minus, spread)
+    cost = pl.CostEstimate(flops=16_000_000_000, bytes_accessed=64_000_000, transcendentals=0)
+    return kernel_call(prepare_kernel, [shape], (), "prepare", cost)(weights, live, got, spread)
 
 
 def filter_scratch(blocks, jobs):
@@ -493,16 +483,17 @@
     ]
 
 
-def beyond_call(n, beyond, edge, omegas, held):
+def beyond_call(n, edge, beyond, omegas):
+    body = functools.partial(beyond_kernel, n)
+    cost = pl.CostEstimate(flops=4_000_000_000, bytes_accessed=16_000_000, transcendentals=0)
+    return kernel_call(body, [EDGE], filter_scratch(2, 1), "beyond", cost)(beyond, edge, omegas)
+
+
+def filter_call(n, part, own, partner, omegas):
     both = (2,) + EDGE
-    body = functools.partial(beyond_kernel, n)
     shapes = [both, EDGE] if n + 1 < ITERS else [both]
-    return kernel_call(body, shapes, filter_scratch(2, 1), name="beyond")(beyond, edge, omegas, held)
-
-
-def filter_call(n, own, partner, omegas):
     body = functools.partial(filter_kernel, n)
-    return kernel_call(body, [(2,) + EDGE], filter_scratch(4, 3), name="filter")(own, partner, omegas)
+    return kernel_call(body, shapes, filter_scratch(4, 3), name="filter")(part, own, partner, omegas)
 
 
 def receive_call(blocks):
@@ -523,20 +514,18 @@
     shift = [(2 * y + 1, 2 * y + 2) for y in range(ys - 1)] + [(2 * y + 2, 2 * y + 1) for y in range(ys - 1)]
     weights = reweights.reshape(ITERS * BINS * FILT, LANES)
     sent = send_call(traces_in)
-    plus, minus = share_call(weights, live_mask)
-    plus = lax.ppermute(plus, ("zh", "zl"), [(z, (z + 2) % 8) for z in range(8)])
-    minus = lax.ppermute(minus, ("zh", "zl"), [(z, (z - 2) % 8) for z in range(8)])
-    spectra = forward_call(exchange(sent, ("x", "zl")), live_mask, fh, fl, turns)
-    spectra, plus, minus = lax.optimization_barrier((spectra, plus, minus))
-    block = exchange(spectra, ("zh", "x", "zl"))
-    omegas = prepare_call(plus, minus, spread)
+    got = lax.ppermute(share(reweights, live_mask), "zh", swap)
+    omegas = prepare_call(weights, live_mask, got, spread)
+    core = lax.axis_index("c")
+    sent, omegas, core = lax.optimization_barrier((exchange(sent, ("x", "zl")), omegas, core))
+    block = exchange(forward_call(sent, live_mask, fh, fl, turns), ("zh", "x", "zl"))
     block = block.reshape((2,) + EDGE)
-    edge = lax.dynamic_index_in_dim(block, lax.axis_index("c"), 0, False)
+    edge = lax.dynamic_slice(block, (core, 0, 0, 0), (1,) + EDGE, allow_negative_indices=False).reshape(EDGE)
     for n in range(ITERS):
         beyond = lax.ppermute(edge, ("y", "c"), shift)
         partner = lax.ppermute(block, "c", swap)
-        held = filter_call(n, block, partner, omegas)
-        found = beyond_call(n, beyond, edge, omegas, held)
+        part = beyond_call(n, edge, beyond, omegas)
+        found = filter_call(n, part, block, partner, omegas)
         block, edge = found if n + 1 < ITERS else (found, None)
     back = exchange(block.reshape(TILES), ("zh", "x", "zl"))
     return receive_call(exchange(inverse_call(back, ih, il, turns), ("x", "zl")))

time: 102 us -> 101 us (level)
  blocking collectives: 53 us -> 47.2 us
  other arithmetic: 0 us -> 1.66 us
  starting transfers between devices: 30.5 us -> 32 us
  waiting for transfers between devices: 8.86 us -> 10.2 us
    all_to_all x1, waiting for transfers between devices: 0.19 us -> 9.42 us  [exchange(): return lax.all_to_all(blocks, axes, 0, 0, tiled=True)]
    all_to_all x3, blocking collectives: 53 us -> 47.2 us  [exchange(): return lax.all_to_all(blocks, axes, 0, 0, tiled=True)]
    ppermute x2, waiting for transfers between devices: 4.63 us -> 0.01 us  [local(): beyond = lax.ppermute(edge, ('y', 'c'), shift)]
    ppermute x2, starting transfers between devices: 5.52 us -> 9.97 us  [local(): partner = lax.ppermute(block, 'c', swap)]
    ppermute x2 -> x1, waiting for transfers between devices: 4.03 us -> 0.01 us  [local(): got = lax.ppermute(share(reweights, live_mask), 'zh', swap)]
    all_to_all x1, starting transfers between devices: 9.96 us -> 7.26 us  [exchange(): return lax.all_to_all(blocks, axes, 0, 0, tiled=True)]
    ppermute x2 -> x1, starting transfers between devices: 10.6 us -> 10.9 us  [local(): got = lax.ppermute(share(reweights, live_mask), 'zh', swap)]
    pallas_call x6 -> x5, Pallas kernels: 5.03 us -> 5.01 us  [the longest x2 3.09 us: filter_call(): kernel_call(body, shapes, filter_scratch(4, 3), name='filter')]
  transfers between devices with their start and end apart: 7 -> 6, of which waited for: 5 -> 3; matrix products, arithmetic and copies ran while one was open for 0% -> 0% of each run, Pallas kernels for 4% -> 2%
where the time goes in v4:
time: 101 us; the launch traced here: 100 us
  blocking collectives  47.2 us (47%)
  starting transfers between devices  32 us (32%)
  waiting for transfers between devices  10.2 us (10%)
  Pallas kernels  8.19 us (8%)
  other arithmetic  1.66 us (2%)
    all_to_all x3, blocking collectives, exchange(): return lax.all_to_all(blocks, axes, 0, 0, tiled=True)  47.2 us
    ppermute x1, starting transfers between devices, local(): got = lax.ppermute(share(reweights, live_mask), 'zh', swap)  10.9 us
    ppermute x2, starting transfers between devices, local(): partner = lax.ppermute(block, 'c', swap)  9.97 us
    all_to_all x1, waiting for transfers between devices, exchange(): return lax.all_to_all(blocks, axes, 0, 0, tiled=True)  9.42 us
    all_to_all x1, starting transfers between devices, exchange(): return lax.all_to_all(blocks, axes, 0, 0, tiled=True)  7.26 us
    ppermute x2, starting transfers between devices, local(): beyond = lax.ppermute(edge, ('y', 'c'), shift)  3.84 us
    pallas_call x2, Pallas kernels, filter_call(): kernel_call(body, shapes, filter_scratch(4, 3), name='filter')  3.09 us
  transfers between devices with their start and end apart: 6, of which 3 were waited for; matrix products, arithmetic and copies ran while one was open for 0% of the time, Pallas kernels for 2%

profile of v4, /device:TPU:24, one launch (start us, length us, event | category | flops | bytes accessed | tf_op | source)
XLA Modules:
  0.0 100.2 jit_solution(5907156218580465990)
XLA Ops:
  0.0 0.0 copy-start
  0.0 0.7 broadcast_compare_fusion
  0.7 0.9 dynamic-slice_select_fusion
  1.7 10.9 %collective-permute-start = (f32[2,128,128]{2,1,0:T(8,128)S(1)}, f32[2,128,128]{2,1,0:T(8,128)S(1)}, u32[]{:S(2)}, u32[]{:S(2)}) collective-permute-start(f32[2,128,128]{2,1,0:T(8,128)S(1)} %bitcast.14), channel_id=1, source_target_pairs={{0,32},{32,0},{1,33},{33,1},{2,34},{34,2},{3,35},{35,3},{4,36},{36... | collective-permute-start | bytes 393224 | tf_op jit(solution)/shard_map/ppermute | solution.py:517
  12.6 0.0 copy-done
  12.6 0.8 send.1
  13.4 0.0 copy-start.5
  13.4 0.0 copy-start.8
  13.4 7.3 %all-to-all-start = ((f32[16,32,128]{2,1,0:T(8,128)}), f32[16,32,128]{2,1,0:T(8,128)S(1)}, u32[]{:S(2)}, u32[]{:S(2)}) async-start(f32[16,32,128]{2,1,0:T(8,128)} %send.1), calls=%async_computation | async-start | bytes 524288 | tf_op jit(solution)/shard_map/all_to_all | solution.py:510
  20.7 0.0 copy-start.7
  20.7 0.0 collective-permute-done.got
  20.7 0.0 copy-done.5
  20.8 0.0 copy-done.8
  20.8 0.6 copy-done.7
  21.4 0.0 copy-start.3
  21.4 0.0 copy-start.4
  21.4 0.0 copy-start.6
  21.4 0.5 prepare.1.omegas
  21.9 9.4 %all-to-all-done.blocks = f32[16,32,128]{2,1,0:T(8,128)S(1)} async-done(((f32[16,32,128]{2,1,0:T(8,128)}), f32[16,32,128]{2,1,0:T(8,128)S(1)}, u32[]{:S(2)}, u32[]{:S(2)}) %all-to-all-start) | async-done | bytes 262176 | tf_op jit(solution)/shard_map/all_to_all | solution.py:510
  31.3 0.0 copy-done.3
  31.3 0.0 copy-done.4
  31.3 0.0 copy-done.6
  31.3 0.8 forward.1
  32.1 16.7 %all_to_all.20 = f32[32,16,128]{2,1,0:T(8,128)S(1)} all-to-all(f32[32,16,128]{2,1,0:T(8,128)S(1)} %forward.1), channel_id=1, replica_groups=mesh['y'=8,'zh'=2,'c'=2,'x'=4,'zl'=4] {'zh','x','zl'}, dimensions={0} | all-to-all | bytes 524288 | tf_op jit(solution)/shard_map/all_to_all | solution.py:510
  48.8 1.9 %collective-permute-start.1 = (f32[16,16,128]{2,1,0:T(8,128)S(1)}, f32[16,16,128]{2,1,0:T(8,128)S(1)}, u32[]{:S(2)}, u32[]{:S(2)}) collective-permute-start(f32[16,16,128]{2,1,0:T(8,128)S(1)} %dynamic-slice_bitcast_fusion.edge), channel_id=1, source_target_pairs={{16,64},{80,128},{144,192},{208,256},{272,320},{336,384},{400,448}... | collective-permute-start | bytes 393224 | tf_op jit(solution)/shard_map/ppermute | solution.py:525
  50.7 4.8 %collective-permute-start.2 = (f32[2,16,16,128]{3,2,1,0:T(8,128)S(1)}, f32[2,16,16,128]{3,2,1,0:T(8,128)S(1)}, u32[]{:S(2)}, u32[]{:S(2)}) collective-permute-start(f32[2,16,16,128]{3,2,1,0:T(8,128)S(1)} %bitcast.9), channel_id=1, source_target_pairs={{0,16},{16,0},{1,17},{17,1},{2,18},{18,2},{3,19},{19,3},{4,20},{20... | collective-permute-start | bytes 786440 | tf_op jit(solution)/shard_map/ppermute | solution.py:526
  55.5 0.0 collective-permute-done.1.beyond
  55.6 0.7 beyond.2.part
  56.3 0.4 collective-permute-done.2.partner
  56.7 1.6 %filter.2 = (f32[2,16,16,128]{3,2,1,0:T(8,128)S(1)}, f32[16,16,128]{2,1,0:T(8,128)S(1)}) custom-call(f32[16,16,128]{2,1,0:T(8,128)S(1)} %beyond.2.part, f32[2,16,16,128]{3,2,1,0:T(8,128)S(1)} %bitcast.10, f32[2,16,16,128]{3,2,1,0:T(8,128)S(1)} %collective-permute-done.2.partner, f32[2,8,64,128]{3,2,1,0:T(8,128)S(1)} %prepare.1.omegas), custom_call_target="tpu_custom_call" | custom-call | tf_op jit(solution)/shard_map/filter/pallas_call | solution.py:496
  58.2 1.9 %collective-permute-start.3 = (f32[16,16,128]{2,1,0:T(8,128)S(1)}, f32[16,16,128]{2,1,0:T(8,128)S(1)}, u32[]{:S(2)}, u32[]{:S(2)}) collective-permute-start(f32[16,16,128]{2,1,0:T(8,128)S(1)} %get-tuple-element.13.edge), channel_id=1, source_target_pairs={{16,64},{80,128},{144,192},{208,256},{272,320},{336,384},{400,448}... | collective-permute-start | bytes 393224 | tf_op jit(solution)/shard_map/ppermute | solution.py:525
  60.2 5.2 %collective-permute-start.4 = (f32[2,16,16,128]{3,2,1,0:T(8,128)S(1)}, f32[2,16,16,128]{3,2,1,0:T(8,128)S(1)}, u32[]{:S(2)}, u32[]{:S(2)}) collective-permute-start(f32[2,16,16,128]{3,2,1,0:T(8,128)S(1)} %get-tuple-element.14.own), channel_id=1, source_target_pairs={{0,16},{16,0},{1,17},{17,1},{2,18},{18,2},{3,19},{19,3},{4,20},{20... | collective-permute-start | bytes 786440 | tf_op jit(solution)/shard_map/ppermute | solution.py:526
  65.3 0.0 collective-permute-done.3.beyond
  65.4 0.7 beyond.3.part
  66.1 0.4 collective-permute-done.4.partner
  66.5 1.5 %filter.3 = f32[2,16,16,128]{3,2,1,0:T(8,128)S(1)} custom-call(f32[16,16,128]{2,1,0:T(8,128)S(1)} %beyond.3.part, f32[2,16,16,128]{3,2,1,0:T(8,128)S(1)} %get-tuple-element.14.own, f32[2,16,16,128]{3,2,1,0:T(8,128)S(1)} %collective-permute-done.4.partner, f32[2,8,64,128]{3,2,1,0:T(8,128)S(1)} %prepare.1.omegas), custom_call_target="tpu_custom_call" | custom-call | tf_op jit(solution)/shard_map/filter/pallas_call | solution.py:496
  68.0 0.0 copy-start.1
  68.0 0.0 copy-start.2
  68.1 17.4 %all_to_all.21.blocks = f32[32,16,128]{2,1,0:T(8,128)S(1)} all-to-all(f32[32,16,128]{2,1,0:T(8,128)S(1)} %bitcast.11), channel_id=1, replica_groups=mesh['y'=8,'zh'=2,'c'=2,'x'=4,'zl'=4] {'zh','x','zl'}, dimensions={0} | all-to-all | bytes 524288 | tf_op jit(solution)/shard_map/all_to_all | solution.py:510
  85.4 0.0 copy-done.1
  85.4 0.0 copy-done.2
  85.4 0.7 inverse.1
  86.2 13.2 %all_to_all.22.blocks = f32[16,32,128]{2,1,0:T(8,128)S(1)} all-to-all(f32[16,32,128]{2,1,0:T(8,128)S(1)} %inverse.1), channel_id=1, replica_groups=mesh['y'=8,'zh'=2,'c'=2,'x'=4,'zl'=4] {'x','zl'}, dimensions={0} | all-to-all | bytes 524288 | tf_op jit(solution)/shard_map/all_to_all | solution.py:510
  99.3 0.8 receive.1
  (1 shorter events, 0.0 us)
Async XLA Ops:
  0.0 12.6 %copy-start = (f32[128,4,128]{2,1,0:T(4,128)S(1)}, f32[128,4,128]{2,1,0:T(4,128)}, u32[]{:S(2)}) copy-start(f32[128,4,128]{2,1,0:T(4,128)} %param.9) | copy-start | bytes 786436
  1.7 19.1 %collective-permute-start = (f32[2,128,128]{2,1,0:T(8,128)S(1)}, f32[2,128,128]{2,1,0:T(8,128)S(1)}, u32[]{:S(2)}, u32[]{:S(2)}) collective-permute-start(f32[2,128,128]{2,1,0:T(8,128)S(1)} %bitcast.14), channel_id=1, source_target_pairs={{0,32},{32,0},{1,33},{33,1},{2,34},{34,2},{3,35},{35,3},{4,36},{36... | collective-permute-start | bytes 393224 | tf_op jit(solution)/shard_map/ppermute | solution.py:517
  13.4 7.3 %copy-start.5 = (f32[2,64,4,128]{3,2,1,0:T(4,128)S(1)}, f32[2,64,4,128]{3,2,1,0:T(4,128)}, u32[]{:S(2)}) copy-start(f32[2,64,4,128]{3,2,1,0:T(4,128)} %param.10) | copy-start | bytes 786436
  13.4 7.3 %copy-start.8 = (bf16[32,128]{1,0:T(8,128)(2,1)S(1)}, bf16[32,128]{1,0:T(8,128)(2,1)}, u32[]{:S(2)}) copy-start(bf16[32,128]{1,0:T(8,128)(2,1)} %constant.35.clone.spread) | copy-start | bytes 24580
  13.4 17.9 %all-to-all-start = ((f32[16,32,128]{2,1,0:T(8,128)}), f32[16,32,128]{2,1,0:T(8,128)S(1)}, u32[]{:S(2)}, u32[]{:S(2)}) async-start(f32[16,32,128]{2,1,0:T(8,128)} %send.1), calls=%async_computation | async-start | bytes 524288 | tf_op jit(solution)/shard_map/all_to_all | solution.py:510
  20.7 0.7 copy-start.7
  21.4 9.9 %copy-start.3 = (bf16[2,256,256]{2,1,0:T(8,128)(2,1)S(1)}, bf16[2,256,256]{2,1,0:T(8,128)(2,1)}, u32[]{:S(2)}) copy-start(bf16[2,256,256]{2,1,0:T(8,128)(2,1)} %constant.32.clone.low) | copy-start | bytes 786436
  21.4 9.9 %copy-start.4 = (bf16[2,256,256]{2,1,0:T(8,128)(2,1)S(1)}, bf16[2,256,256]{2,1,0:T(8,128)(2,1)}, u32[]{:S(2)}) copy-start(bf16[2,256,256]{2,1,0:T(8,128)(2,1)} %constant.31.clone.high) | copy-start | bytes 786436
  21.4 9.9 %copy-start.6 = (f32[2,8,128]{2,1,0:T(8,128)S(1)}, f32[2,8,128]{2,1,0:T(8,128)}, u32[]{:S(2)}) copy-start(f32[2,8,128]{2,1,0:T(8,128)} %constant.36.clone.turns) | copy-start | bytes 24580
  48.8 6.7 %collective-permute-start.1 = (f32[16,16,128]{2,1,0:T(8,128)S(1)}, f32[16,16,128]{2,1,0:T(8,128)S(1)}, u32[]{:S(2)}, u32[]{:S(2)}) collective-permute-start(f32[16,16,128]{2,1,0:T(8,128)S(1)} %dynamic-slice_bitcast_fusion.edge), channel_id=1, source_target_pairs={{16,64},{80,128},{144,192},{208,256},{272,320},{336,384},{400,448}... | collective-permute-start | bytes 393224 | tf_op jit(solution)/shard_map/ppermute | solution.py:525
  50.7 5.9 %collective-permute-start.2 = (f32[2,16,16,128]{3,2,1,0:T(8,128)S(1)}, f32[2,16,16,128]{3,2,1,0:T(8,128)S(1)}, u32[]{:S(2)}, u32[]{:S(2)}) collective-permute-start(f32[2,16,16,128]{3,2,1,0:T(8,128)S(1)} %bitcast.9), channel_id=1, source_target_pairs={{0,16},{16,0},{1,17},{17,1},{2,18},{18,2},{3,19},{19,3},{4,20},{20... | collective-permute-start | bytes 786440 | tf_op jit(solution)/shard_map/ppermute | solution.py:526
  58.2 7.1 %collective-permute-start.3 = (f32[16,16,128]{2,1,0:T(8,128)S(1)}, f32[16,16,128]{2,1,0:T(8,128)S(1)}, u32[]{:S(2)}, u32[]{:S(2)}) collective-permute-start(f32[16,16,128]{2,1,0:T(8,128)S(1)} %get-tuple-element.13.edge), channel_id=1, source_target_pairs={{16,64},{80,128},{144,192},{208,256},{272,320},{336,384},{400,448}... | collective-permute-start | bytes 393224 | tf_op jit(solution)/shard_map/ppermute | solution.py:525
  60.2 6.3 %collective-permute-start.4 = (f32[2,16,16,128]{3,2,1,0:T(8,128)S(1)}, f32[2,16,16,128]{3,2,1,0:T(8,128)S(1)}, u32[]{:S(2)}, u32[]{:S(2)}) collective-permute-start(f32[2,16,16,128]{3,2,1,0:T(8,128)S(1)} %get-tuple-element.14.own), channel_id=1, source_target_pairs={{0,16},{16,0},{1,17},{17,1},{2,18},{18,2},{3,19},{19,3},{4,20},{20... | collective-permute-start | bytes 786440 | tf_op jit(solution)/shard_map/ppermute | solution.py:526
  68.0 17.4 %copy-start.1 = (bf16[2,256,256]{2,1,0:T(8,128)(2,1)S(1)}, bf16[2,256,256]{2,1,0:T(8,128)(2,1)}, u32[]{:S(2)}) copy-start(bf16[2,256,256]{2,1,0:T(8,128)(2,1)} %constant.34.clone.low) | copy-start | bytes 786436
  68.0 17.4 %copy-start.2 = (bf16[2,256,256]{2,1,0:T(8,128)(2,1)S(1)}, bf16[2,256,256]{2,1,0:T(8,128)(2,1)}, u32[]{:S(2)}) copy-start(bf16[2,256,256]{2,1,0:T(8,128)(2,1)} %constant.33.clone.high) | copy-start | bytes 786436

commit v5 on v4

--- a/solution.py
+++ b/solution.py
@@ -17,8 +17,6 @@
 BINS = 64
 WINDOWS = 4
 WX = 32
-ROWS = 16
-UNITS = 8
 LANES = 128
 f32, bf16 = jnp.float32, jnp.bfloat16
 
@@ -28,12 +26,8 @@
     return 16 * b + residue
 
 
-INNER = [(s, b) for s in range(2) for b in range(2)]
+INNER = [(a, s, b) for a in range(2) for s in range(2) for b in range(2)]
 HALF = BINS // 2
-
-
-def held_bins(part):
-    return divmod(part, RADIX)
 
 
 def split_table(table):
@@ -46,11 +40,12 @@
     forward = np.zeros((2, 2 * SPAN, 2 * SPAN))
     inverse = np.zeros((2, 2 * SPAN, 2 * SPAN))
     r = np.arange(SPAN)
-    for part in range(2 * RADIX):
-        half, g = held_bins(part)
-        for place, (s, b) in enumerate(INNER):
-            base = BINS * g + HALF * half + 16 * b
-            col = part * 4 + place
+    for spot in range(2 * 8):
+        kappa, part = divmod(spot, 8)
+        zh, zl = divmod(part, 4)
+        for place, (a, s, b) in enumerate(INNER):
+            base = BINS * (4 * (2 * kappa + a) + zl) + HALF * zh + 16 * b
+            col = spot * 8 + place
             f = base + 8 * s
             angle = 2.0 * np.pi * ((f * r) % NT) / NT
             span = slice(s * SPAN, (s + 1) * SPAN)
@@ -75,11 +70,12 @@
 
 
 def spread_table():
-    table = np.zeros((HALF, LANES), np.float32)
+    table = np.zeros((BINS, LANES), np.float32)
     for m in range(8):
-        for place, (s, b) in enumerate(INNER):
-            for quarter in range(4):
-                table[low_bin(m, s, b), quarter * HALF + m * 4 + place] = 1.0
+        for place, (a, s, b) in enumerate(INNER):
+            row = HALF * a + low_bin(m, s, b)
+            table[row, m * 8 + place] = 1.0
+            table[row, BINS + m * 8 + place] = 1.0
     return table.astype(bf16)
 
 
@@ -195,21 +191,22 @@
     others = split_dot(jnp.concatenate(rows, axis=0), high[1], low[1])
     real = [first[:, :LANES]] + [others[WX * m : WX * m + WX, :LANES] for m in range(7)]
     imag = [first[:, LANES:]] + [others[WX * m : WX * m + WX, LANES:] for m in range(7)]
-    real, imag = swap_blocks(real, lane, 4), swap_blocks(imag, lane, 4)
-    for k in range(8):
-        pieces = [real[k][:16], real[k][16:], imag[k][:16], imag[k][16:]]
-        for top, tile in enumerate(swap_blocks(pieces, lanes_of(16), HALF)):
-            out[top * 8 + k] = tile
+    real, imag = swap_blocks(real, lane, 8), swap_blocks(imag, lane, 8)
+    left = lane < BINS
+    for part in range(8):
+        out[part, 0] = jnp.where(left, real[part], pltpu.roll(imag[part], BINS, 1))
+        out[part, 1] = jnp.where(left, pltpu.roll(real[part], BINS, 1), imag[part])
 
 
 def inverse_kernel(blocks, high, low, turns, out):
     lane = lanes_of(WX)
+    left = lane < BINS
     real, imag = [], []
-    for k in range(8):
-        pieces = swap_blocks([blocks[top * 8 + k] for top in range(4)], lanes_of(16), HALF)
-        real.append(jnp.concatenate(pieces[:2], axis=0))
-        imag.append(jnp.concatenate(pieces[2:], axis=0))
-    real, imag = swap_blocks(real, lane, 4), swap_blocks(imag, lane, 4)
+    for part in range(8):
+        first, second = blocks[part, 0], blocks[part, 1]
+        real.append(jnp.where(left, first, pltpu.roll(second, BINS, 1)))
+        imag.append(jnp.where(left, pltpu.roll(first, BINS, 1), second))
+    real, imag = swap_blocks(real, lane, 8), swap_blocks(imag, lane, 8)
     first = split_dot(jnp.concatenate([real[0], imag[0]], axis=1), high[0], low[0])
     rows = [jnp.concatenate([real[m], imag[m]], axis=1) for m in range(1, 8)]
     others = split_dot(jnp.concatenate(rows, axis=0), high[1], low[1])
@@ -268,40 +265,58 @@
 SUMS = len(PAIRS) + len(OFF) + 2 * FILT
 
 
-def prepare_kernel(weights, live, got, spread, omega):
-    own = lax.axis_index("zh")
+def windows_kernel(weights, live, got, here, across, beside, held):
+    own, x = lax.axis_index("zh"), lax.axis_index("x")
     alive = live[...].astype(f32)
+    for n in range(ITERS):
+        mine, other = [], []
+        for i in range(FILT):
+            start = n * BINS * FILT + own * HALF * FILT + i
+            mine.append(weights[pl.ds(start, HALF, stride=FILT), :] * alive[i : i + 1])
+            other.append(got[n, pl.ds(i, HALF, stride=FILT), :])
+        for rows, beta in ((mine, own), (other, 1 - own)):
+            for w, block in enumerate(swap_blocks(rows, lanes_of(HALF), WX)):
+                held[w, beta, n] = block
+    pair = x + 1 - 2 * lax.rem(x, 2)
+    here[...] = held[x]
+    across[...] = held[WINDOWS - 1 - x]
+    beside[0] = held[pair]
+    beside[1] = held[WINDOWS - 1 - pair]
+
+
+def prepare_kernel(here, beside, across, spread, omega, held):
+    x = lax.axis_index("x")
+    pair = x + 1 - 2 * lax.rem(x, 2)
+    held[x] = here[...]
+    held[pair] = beside[0]
+    held[WINDOWS - 1 - x] = across[0]
+    held[WINDOWS - 1 - pair] = across[1]
     table = spread[...]
     over = (((0,), (0,)), ((), ()))
-    upper = (lanes_of(ROWS) & HALF) != 0
     for n in range(ITERS):
-        for i in range(FILT):
-            start = n * BINS * FILT + own * HALF * FILT + i
-            mine = weights[pl.ds(start, HALF, stride=FILT), :] * alive[i : i + 1]
-            for rows, beta in ((mine, own), (got[n, pl.ds(i, HALF, stride=FILT), :], 1 - own)):
+        for beta in range(2):
+            for kappa in range(2):
+                rows = jnp.concatenate([held[2 * kappa + a, beta, n] for a in range(2)], axis=0)
                 top = rows.astype(bf16)
                 rest = (rows - top.astype(f32)).astype(bf16)
-                wide = lax.dot_general(top, table, over, preferred_element_type=f32) + lax.dot_general(
-                    rest, table, over, preferred_element_type=f32
-                )
-                for w in range(WINDOWS):
-                    first, second = wide[w * WX : w * WX + ROWS], wide[w * WX + ROWS : (w + 1) * WX]
-                    omega[n, beta * WINDOWS + w, i * ROWS : (i + 1) * ROWS] = jnp.where(upper, second, first)
+                omega[n, beta * 2 + kappa] = lax.dot_general(
+                    top, table, over, preferred_element_type=f32
+                ) + lax.dot_general(rest, table, over, preferred_element_type=f32)
 
 
 def predictions(jobs, omega, turned, sums, coefs, store):
-    slots = WINDOWS * len(jobs)
+    slots = TWO * len(jobs)
     blocks = []
     for own, side, _, _ in jobs:
         blocks += [ref for ref in (own, side) if all(ref is not other for other in blocks)]
     for place, ref in enumerate(blocks):
-        for k in range(4 * FILT):
+        for k in range(TWO * FILT):
             turned[place, k] = pltpu.roll(ref[k], BINS, 1)
     places = [[next(p for p, other in enumerate(blocks) if other is ref) for ref in job[:2]] for job in jobs]
 
     def tile_of(row, w, flip):
         row = row % FILT
-        return w * FILT + row + flip * (FILT - 1 - 2 * row)
+        return (row + flip * (FILT - 1 - 2 * row)) * TWO + w
 
     def rows_of(job, w, lines):
         own, side, _, flip = jobs[job]
@@ -314,8 +329,8 @@
 
     def weight_of(job, i, w, sub):
         _, _, beta, flip = jobs[job]
-        start = tile_of(i, 0, flip) * ROWS + sub * 8
-        return omega[beta * WINDOWS + w, pl.ds(pl.multiple_of(start, 8), 8), :]
+        start = tile_of(i, 0, flip) // TWO * ROWS + sub * 8
+        return omega[beta * TWO + w, pl.ds(pl.multiple_of(start, 8), 8), :]
 
     def gather(w, carry):
         for job in range(len(jobs)):
@@ -340,12 +355,12 @@
                         add(place, weighted[k] * rows[i])
                         add(place + 1, weighted[k] * turns[i])
                         place += 2
-            start = pl.multiple_of((job * WINDOWS + w) * 8, 8)
+            start = pl.multiple_of((job * TWO + w) * 8, 8)
             for place in range(SUMS):
                 sums[place, pl.ds(start, 8), :] = acc[place]
         return carry
 
-    lax.fori_loop(0, WINDOWS, gather, 0)
+    lax.fori_loop(0, TWO, gather, 0)
 
     sign = jnp.where(lanes_of(slots) < BINS, 1.0, -1.0).astype(f32)
 
@@ -355,16 +370,13 @@
             value = value + sums[place, pl.ds(s, slots, stride=8), :]
         return value
 
-    def both_halves(value):
-        return value + pltpu.roll(value, HALF, 1)
-
     def real_sum(place):
         value = total(place)
-        return both_halves(value + pltpu.roll(value, BINS, 1))
+        return value + pltpu.roll(value, BINS, 1)
 
     def imag_sum(place):
         value = total(place)
-        return both_halves((value - pltpu.roll(value, BINS, 1)) * sign)
+        return (value - pltpu.roll(value, BINS, 1)) * sign
 
     matrix = [[None] * FILT for _ in range(FILT)]
     for place, (k, l) in enumerate(PAIRS):
@@ -384,8 +396,8 @@
                 rows, turns = rows_of(job, w, lines)
                 acc = [None] * FILT
                 for k in range(FILT):
-                    one = coefs[2 * k, pl.ds(job * WINDOWS + w, 1), :]
-                    two = coefs[2 * k + 1, pl.ds(job * WINDOWS + w, 1), :]
+                    one = coefs[2 * k, pl.ds(job * TWO + w, 1), :]
+                    two = coefs[2 * k + 1, pl.ds(job * TWO + w, 1), :]
                     for i in range(FILT):
                         value = one * rows[i + k + 1] + two * turns[i + k + 1]
                         acc[i] = value if acc[i] is None else acc[i] + value
@@ -393,7 +405,11 @@
                     store(job, tile_of(i, w, jobs[job][3]), lines, acc[i], weight_of(job, i, w, sub))
         return carry
 
-    lax.fori_loop(0, WINDOWS, predict, 0)
+    lax.fori_loop(0, TWO, predict, 0)
+
+
+def pick_kernel(block, out):
+    out[...] = block[lax.axis_index("c")]
 
 
 def beyond_kernel(n, beyond, edge, omegas, out, turned, sums, coefs):
@@ -442,8 +458,11 @@
 
 
 TRACES = (RADIX, WX, LANES)
-TILES = (8 * FILT, ROWS, LANES)
-EDGE = (4 * FILT, ROWS, LANES)
+TWO = 2
+ROWS = WX
+TILES = (2 * FILT, TWO, ROWS, LANES)
+EDGE = (TWO * FILT, ROWS, LANES)
+PART = (2, ITERS, HALF, LANES)
 GIVE = (ITERS, HALF * FILT, LANES)
 
 
@@ -469,18 +488,29 @@
     return kernel_call(inverse_kernel, [TRACES], name="inverse")(blocks, *tables)
 
 
-def prepare_call(weights, live, got, spread):
-    shape = (ITERS, UNITS, FILT * ROWS, LANES)
+def windows_call(weights, live, got):
     cost = pl.CostEstimate(flops=16_000_000_000, bytes_accessed=64_000_000, transcendentals=0)
-    return kernel_call(prepare_kernel, [shape], (), "prepare", cost)(weights, live, got, spread)
+    scratch = [pltpu.VMEM((WINDOWS,) + PART, f32)]
+    return kernel_call(windows_kernel, [PART, PART, (2,) + PART], scratch, "windows", cost)(weights, live, got)
+
+
+def prepare_call(*arrays):
+    shape = (ITERS, 2 * TWO, FILT * ROWS, LANES)
+    scratch = [pltpu.VMEM((WINDOWS,) + PART, f32)]
+    return kernel_call(prepare_kernel, [shape], scratch, "prepare")(*arrays)
 
 
 def filter_scratch(blocks, jobs):
     return [
         pltpu.VMEM((blocks,) + EDGE, f32),
-        pltpu.VMEM((SUMS, 8 * WINDOWS * jobs, LANES), f32),
-        pltpu.VMEM((2 * FILT, WINDOWS * jobs, LANES), f32),
+        pltpu.VMEM((SUMS, 8 * TWO * jobs, LANES), f32),
+        pltpu.VMEM((2 * FILT, TWO * jobs, LANES), f32),
     ]
+
+
+def pick_call(block):
+    cost = pl.CostEstimate(flops=16_000_000_000, bytes_accessed=64_000_000, transcendentals=0)
+    return kernel_call(pick_kernel, [EDGE], (), "pick", cost)(block)
 
 
 def beyond_call(n, edge, beyond, omegas):
@@ -515,19 +545,23 @@
     weights = reweights.reshape(ITERS * BINS * FILT, LANES)
     sent = send_call(traces_in)
     got = lax.ppermute(share(reweights, live_mask), "zh", swap)
-    omegas = prepare_call(weights, live_mask, got, spread)
-    core = lax.axis_index("c")
-    sent, omegas, core = lax.optimization_barrier((exchange(sent, ("x", "zl")), omegas, core))
-    block = exchange(forward_call(sent, live_mask, fh, fl, turns), ("zh", "x", "zl"))
-    block = block.reshape((2,) + EDGE)
-    edge = lax.dynamic_slice(block, (core, 0, 0, 0), (1,) + EDGE, allow_negative_indices=False).reshape(EDGE)
+    here, across, beside = windows_call(weights, live_mask, got)
+    beside = lax.ppermute(beside, "x", [(i, i ^ 1) for i in range(WINDOWS)])
+    sent, here, across, beside = lax.optimization_barrier((exchange(sent, ("x", "zl")), here, across, beside))
+    across = lax.ppermute(jnp.stack([across, beside[1]]), "x", [(i, WINDOWS - 1 - i) for i in range(WINDOWS)])
+    block = exchange(forward_call(sent, live_mask, fh, fl, turns), ("zh", "zl")).reshape((2,) + EDGE)
+    edge = pick_call(block)
+    omegas = None
     for n in range(ITERS):
         beyond = lax.ppermute(edge, ("y", "c"), shift)
         partner = lax.ppermute(block, "c", swap)
+        if omegas is None:
+            edge, across = lax.optimization_barrier((edge, across))
+            omegas = prepare_call(here, beside, across, spread)
         part = beyond_call(n, edge, beyond, omegas)
         found = filter_call(n, part, block, partner, omegas)
         block, edge = found if n + 1 < ITERS else (found, None)
-    back = exchange(block.reshape(TILES), ("zh", "x", "zl"))
+    back = exchange(block.reshape(TILES), ("zh", "zl"))
     return receive_call(exchange(inverse_call(back, ih, il, turns), ("x", "zl")))
 
 

time: 101 us -> 98.6 us (0.976)
  blocking collectives: 47.2 us -> 30.8 us
  starting transfers between devices: 32 us -> 42.7 us
  waiting for transfers between devices: 10.2 us -> 14 us
    all_to_all x3 -> x2, blocking collectives: 47.2 us -> 30.8 us  [exchange(): return lax.all_to_all(blocks, axes, 0, 0, tiled=True)]
    ppermute x0 -> x2, starting transfers between devices: none -> 7.4 us  [the longest x1 3.83 us: local(): beside = lax.ppermute(beside, 'x', [(i, i ^ 1) for i in range(WINDOWS)])]
    ppermute x0 -> x2, waiting for transfers between devices: none -> 4.37 us  [the longest x1 4.37 us: local(): beside = lax.ppermute(beside, 'x', [(i, i ^ 1) for i in range(WINDOWS)])]
    all_to_all x1 -> x2, starting transfers between devices: 7.26 us -> 10.7 us  [exchange(): return lax.all_to_all(blocks, axes, 0, 0, tiled=True)]
    all_to_all x1 -> x2, waiting for transfers between devices: 9.42 us -> 9.05 us  [exchange(): return lax.all_to_all(blocks, axes, 0, 0, tiled=True)]
  transfers between devices with their start and end apart: 6 -> 9, of which waited for: 3 -> 5; matrix products, arithmetic and copies ran while one was open for 0% -> 0% of each run, Pallas kernels for 2% -> 2%
where the time goes in v5:
time: 98.6 us; the launch traced here: 98 us
  starting transfers between devices  42.7 us (43%)
  blocking collectives  30.8 us (31%)
  waiting for transfers between devices  14 us (14%)
  Pallas kernels  8.44 us (9%)
  other arithmetic  1.67 us (2%)
    all_to_all x2, blocking collectives, exchange(): return lax.all_to_all(blocks, axes, 0, 0, tiled=True)  30.8 us
    ppermute x1, starting transfers between devices, local(): got = lax.ppermute(share(reweights, live_mask), 'zh', swap)  10.9 us
    all_to_all x2, starting transfers between devices, exchange(): return lax.all_to_all(blocks, axes, 0, 0, tiled=True)  10.7 us
    ppermute x2, starting transfers between devices, local(): partner = lax.ppermute(block, 'c', swap)  9.87 us
    all_to_all x2, waiting for transfers between devices, exchange(): return lax.all_to_all(blocks, axes, 0, 0, tiled=True)  9.05 us
    ppermute x1, waiting for transfers between devices, local(): beside = lax.ppermute(beside, 'x', [(i, i ^ 1) for i in range(WINDOWS)])  4.37 us
    ppermute x2, starting transfers between devices, local(): beyond = lax.ppermute(edge, ('y', 'c'), shift)  3.84 us
    ppermute x1, starting transfers between devices, local(): beside = lax.ppermute(beside, 'x', [(i, i ^ 1) for i in range(WINDOWS)])  3.83 us
  transfers between devices with their start and end apart: 9, of which 5 were waited for; matrix products, arithmetic and copies ran while one was open for 0% of the time, Pallas kernels for 2%

profile of v5, /device:TPU:24, one launch (start us, length us, event | category | flops | bytes accessed | tf_op | source)
XLA Modules:
  0.0 98.0 jit_solution(2055734971405018117)
XLA Ops:
  0.0 0.0 copy-start
  0.0 0.7 broadcast_compare_fusion
  0.7 0.9 dynamic-slice_select_fusion
  1.7 10.9 %collective-permute-start = (f32[2,128,128]{2,1,0:T(8,128)S(1)}, f32[2,128,128]{2,1,0:T(8,128)S(1)}, u32[]{:S(2)}, u32[]{:S(2)}) collective-permute-start(f32[2,128,128]{2,1,0:T(8,128)S(1)} %bitcast.14), channel_id=1, source_target_pairs={{0,32},{32,0},{1,33},{33,1},{2,34},{34,2},{3,35},{35,3},{4,36},{36... | collective-permute-start | bytes 393224 | tf_op jit(solution)/shard_map/ppermute | solution.py:547
  12.6 0.0 copy-done
  12.6 0.8 send.1
  13.4 0.0 copy-start.5
  13.4 7.3 %all-to-all-start = ((f32[16,32,128]{2,1,0:T(8,128)}), f32[16,32,128]{2,1,0:T(8,128)S(1)}, u32[]{:S(2)}, u32[]{:S(2)}) async-start(f32[16,32,128]{2,1,0:T(8,128)} %send.1), calls=%async_computation | async-start | bytes 524288 | tf_op jit(solution)/shard_map/all_to_all | solution.py:540
  20.7 0.0 collective-permute-done.got
  20.7 0.0 copy-done.5
  20.7 0.0 copy-done.8
  20.7 0.0 copy-start.3
  20.8 0.0 copy-start.4
  20.8 0.0 copy-start.6
  20.8 0.3 windows.1
  21.1 3.8 %collective-permute-start.1 = (f32[2,2,2,32,128]{4,3,2,1,0:T(8,128)S(1)}, f32[2,2,2,32,128]{4,3,2,1,0:T(8,128)S(1)}, u32[]{:S(2)}, u32[]{:S(2)}) collective-permute-start(f32[2,2,2,32,128]{4,3,2,1,0:T(8,128)S(1)} %get-tuple-element.18), channel_id=1, source_target_pairs={{0,4},{4,0},{8,12},{12,8},{1,5},{5,1},{9,13},{13,9},{2,6},{6,2},{1... | collective-permute-start | bytes 393224 | tf_op jit(solution)/shard_map/ppermute | solution.py:549
  24.9 4.4 %collective-permute-done.1.beside = f32[2,2,2,32,128]{4,3,2,1,0:T(8,128)S(1)} collective-permute-done((f32[2,2,2,32,128]{4,3,2,1,0:T(8,128)S(1)}, f32[2,2,2,32,128]{4,3,2,1,0:T(8,128)S(1)}, u32[]{:S(2)}, u32[]{:S(2)}) %collective-permute-start.1) | collective-permute-done | bytes 131104 | tf_op jit(solution)/shard_map/ppermute | solution.py:549
  29.3 2.0 %all-to-all-done.blocks = f32[16,32,128]{2,1,0:T(8,128)S(1)} async-done(((f32[16,32,128]{2,1,0:T(8,128)}), f32[16,32,128]{2,1,0:T(8,128)S(1)}, u32[]{:S(2)}, u32[]{:S(2)}) %all-to-all-start) | async-done | bytes 262176 | tf_op jit(solution)/shard_map/all_to_all | solution.py:540
  31.3 0.0 copy-done.3
  31.3 0.0 copy-done.4
  31.3 0.0 copy-done.6
  31.3 1.4 %forward.1 = f32[8,2,32,128]{3,2,1,0:T(8,128)} custom-call(f32[16,32,128]{2,1,0:T(8,128)S(1)} %all-to-all-done.blocks, s32[4,128]{1,0:T(4,128)S(1)} %copy-done.8, bf16[2,256,256]{2,1,0:T(8,128)(2,1)S(1)} %copy-done.3, bf16[2,256,256]{2,1,0:T(8,128)(2,1)S(1)} %copy-done.4, f32[2,8,128]{2,1,0:T(8,128)S(1)} %copy-done.6), custom_call_target="tpu_custom_call" | custom-call | tf_op jit(solution)/shard_map/forward/pallas_call | solution.py:484
  32.8 3.4 %all-to-all-start.1 = ((f32[8,2,32,128]{3,2,1,0:T(8,128)}), f32[8,2,32,128]{3,2,1,0:T(8,128)S(1)}, u32[]{:S(2)}, u32[]{:S(2)}) async-start(f32[8,2,32,128]{3,2,1,0:T(8,128)} %forward.1), calls=%async_computation.1 | async-start | bytes 524288 | tf_op jit(solution)/shard_map/all_to_all | solution.py:540
  36.2 3.6 %collective-permute-start.3 = (f32[2,2,2,32,128]{4,3,2,1,0:T(8,128)S(1)}, f32[2,2,2,32,128]{4,3,2,1,0:T(8,128)S(1)}, u32[]{:S(2)}, u32[]{:S(2)}) collective-permute-start(f32[2,2,2,32,128]{4,3,2,1,0:T(8,128)S(1)} %pad_maximum_fusion), channel_id=1, source_target_pairs={{0,12},{4,8},{8,4},{12,0},{1,13},{5,9},{9,5},{13,1},{2,14},{6,10},... | collective-permute-start | bytes 393224 | tf_op jit(solution)/shard_map/ppermute | solution.py:551
  39.8 7.0 %all-to-all-done.1 = f32[8,2,32,128]{3,2,1,0:T(8,128)S(1)} async-done(((f32[8,2,32,128]{3,2,1,0:T(8,128)}), f32[8,2,32,128]{3,2,1,0:T(8,128)S(1)}, u32[]{:S(2)}, u32[]{:S(2)}) %all-to-all-start.1) | async-done | bytes 262176 | tf_op jit(solution)/shard_map/all_to_all | solution.py:540
  46.8 1.9 %collective-permute-start.2 = (f32[8,32,128]{2,1,0:T(8,128)S(1)}, f32[8,32,128]{2,1,0:T(8,128)S(1)}, u32[]{:S(2)}, u32[]{:S(2)}) collective-permute-start(f32[8,32,128]{2,1,0:T(8,128)S(1)} %pick.1.edge), channel_id=1, source_target_pairs={{16,64},{80,128},{144,192},{208,256},{272,320},{336,384},{400,448}... | collective-permute-start | bytes 393224 | tf_op jit(solution)/shard_map/ppermute | solution.py:556
  48.8 4.8 %collective-permute-start.4 = (f32[2,8,32,128]{3,2,1,0:T(8,128)S(1)}, f32[2,8,32,128]{3,2,1,0:T(8,128)S(1)}, u32[]{:S(2)}, u32[]{:S(2)}) collective-permute-start(f32[2,8,32,128]{3,2,1,0:T(8,128)S(1)} %bitcast.8), channel_id=1, source_target_pairs={{0,16},{16,0},{1,17},{17,1},{2,18},{18,2},{3,19},{19,3},{4,20},{20... | collective-permute-start | bytes 786440 | tf_op jit(solution)/shard_map/ppermute | solution.py:557
  53.6 0.0 collective-permute-done.3.across
  53.6 0.0 copy-done.7
  53.6 0.4 prepare.1.omegas
  54.0 0.0 collective-permute-done.2.beyond
  54.0 0.6 beyond.2.part
  54.6 0.1 collective-permute-done.4.partner
  54.7 1.4 %filter.2 = (f32[2,8,32,128]{3,2,1,0:T(8,128)S(1)}, f32[8,32,128]{2,1,0:T(8,128)S(1)}) custom-call(f32[8,32,128]{2,1,0:T(8,128)S(1)} %beyond.2.part, f32[2,8,32,128]{3,2,1,0:T(8,128)S(1)} %bitcast.9, f32[2,8,32,128]{3,2,1,0:T(8,128)S(1)} %collective-permute-done.4.partner, f32[2,4,128,128]{3,2,1,0:T(8,128)S(1)} %prepare.1.omegas), custom_call_target="tpu_custom_call" | custom-call | tf_op jit(solution)/shard_map/filter/pallas_call | solution.py:526
  56.1 1.9 %collective-permute-start.5 = (f32[8,32,128]{2,1,0:T(8,128)S(1)}, f32[8,32,128]{2,1,0:T(8,128)S(1)}, u32[]{:S(2)}, u32[]{:S(2)}) collective-permute-start(f32[8,32,128]{2,1,0:T(8,128)S(1)} %get-tuple-element.25.edge), channel_id=1, source_target_pairs={{16,64},{80,128},{144,192},{208,256},{272,320},{336,384},{400,448}... | collective-permute-start | bytes 393224 | tf_op jit(solution)/shard_map/ppermute | solution.py:556
  58.0 5.1 %collective-permute-start.6 = (f32[2,8,32,128]{3,2,1,0:T(8,128)S(1)}, f32[2,8,32,128]{3,2,1,0:T(8,128)S(1)}, u32[]{:S(2)}, u32[]{:S(2)}) collective-permute-start(f32[2,8,32,128]{3,2,1,0:T(8,128)S(1)} %get-tuple-element.26.own), channel_id=1, source_target_pairs={{0,16},{16,0},{1,17},{17,1},{2,18},{18,2},{3,19},{19,3},{4,20},{20... | collective-permute-start | bytes 786440 | tf_op jit(solution)/shard_map/ppermute | solution.py:557
  63.1 0.0 collective-permute-done.5.beyond
  63.1 0.6 beyond.3.part
  63.8 0.5 collective-permute-done.6.partner
  64.3 1.4 %filter.3 = f32[2,8,32,128]{3,2,1,0:T(8,128)S(1)} custom-call(f32[8,32,128]{2,1,0:T(8,128)S(1)} %beyond.3.part, f32[2,8,32,128]{3,2,1,0:T(8,128)S(1)} %get-tuple-element.26.own, f32[2,8,32,128]{3,2,1,0:T(8,128)S(1)} %collective-permute-done.6.partner, f32[2,4,128,128]{3,2,1,0:T(8,128)S(1)} %prepare.1.omegas), custom_call_target="tpu_custom_call" | custom-call | tf_op jit(solution)/shard_map/filter/pallas_call | solution.py:526
  65.7 0.0 copy-start.1
  65.7 0.0 copy-start.2
  65.7 15.2 %all_to_all.20.blocks = f32[8,2,32,128]{3,2,1,0:T(8,128)S(1)} all-to-all(f32[8,2,32,128]{3,2,1,0:T(8,128)S(1)} %bitcast.10), channel_id=1, replica_groups=mesh['y'=8,'zh'=2,'c'=2,'x'=4,'zl'=4] {'zh','zl'}, dimensions={0} | all-to-all | bytes 524288 | tf_op jit(solution)/shard_map/all_to_all | solution.py:540
  80.9 0.0 copy-done.1
  80.9 0.0 copy-done.2
  80.9 0.6 inverse.1
  81.6 15.6 %all_to_all.21.blocks = f32[16,32,128]{2,1,0:T(8,128)S(1)} all-to-all(f32[16,32,128]{2,1,0:T(8,128)S(1)} %inverse.1), channel_id=1, replica_groups=mesh['y'=8,'zh'=2,'c'=2,'x'=4,'zl'=4] {'x','zl'}, dimensions={0} | all-to-all | bytes 524288 | tf_op jit(solution)/shard_map/all_to_all | solution.py:540
  97.1 0.8 receive.1
  (5 shorter events, 0.0 us)
Async XLA Ops:
  0.0 12.6 %copy-start = (f32[128,4,128]{2,1,0:T(4,128)S(1)}, f32[128,4,128]{2,1,0:T(4,128)}, u32[]{:S(2)}) copy-start(f32[128,4,128]{2,1,0:T(4,128)} %param.9) | copy-start | bytes 786436
  1.7 19.1 %collective-permute-start = (f32[2,128,128]{2,1,0:T(8,128)S(1)}, f32[2,128,128]{2,1,0:T(8,128)S(1)}, u32[]{:S(2)}, u32[]{:S(2)}) collective-permute-start(f32[2,128,128]{2,1,0:T(8,128)S(1)} %bitcast.14), channel_id=1, source_target_pairs={{0,32},{32,0},{1,33},{33,1},{2,34},{34,2},{3,35},{35,3},{4,36},{36... | collective-permute-start | bytes 393224 | tf_op jit(solution)/shard_map/ppermute | solution.py:547
  13.4 7.3 %copy-start.5 = (f32[2,64,4,128]{3,2,1,0:T(4,128)S(1)}, f32[2,64,4,128]{3,2,1,0:T(4,128)}, u32[]{:S(2)}) copy-start(f32[2,64,4,128]{3,2,1,0:T(4,128)} %param.10) | copy-start | bytes 786436
  13.4 7.3 %copy-start.8 = (s32[4,128]{1,0:T(4,128)S(1)}, s32[4,128]{1,0:T(4,128)}, u32[]{:S(2)}) copy-start(s32[4,128]{1,0:T(4,128)} %live.3) | copy-start | bytes 6148
  13.4 17.9 %all-to-all-start = ((f32[16,32,128]{2,1,0:T(8,128)}), f32[16,32,128]{2,1,0:T(8,128)S(1)}, u32[]{:S(2)}, u32[]{:S(2)}) async-start(f32[16,32,128]{2,1,0:T(8,128)} %send.1), calls=%async_computation | async-start | bytes 524288 | tf_op jit(solution)/shard_map/all_to_all | solution.py:540
  20.7 10.6 %copy-start.3 = (bf16[2,256,256]{2,1,0:T(8,128)(2,1)S(1)}, bf16[2,256,256]{2,1,0:T(8,128)(2,1)}, u32[]{:S(2)}) copy-start(bf16[2,256,256]{2,1,0:T(8,128)(2,1)} %constant.27.clone.high) | copy-start | bytes 786436
  20.8 10.6 %copy-start.4 = (bf16[2,256,256]{2,1,0:T(8,128)(2,1)S(1)}, bf16[2,256,256]{2,1,0:T(8,128)(2,1)}, u32[]{:S(2)}) copy-start(bf16[2,256,256]{2,1,0:T(8,128)(2,1)} %constant.28.clone.low) | copy-start | bytes 786436
  20.8 10.6 %copy-start.6 = (f32[2,8,128]{2,1,0:T(8,128)S(1)}, f32[2,8,128]{2,1,0:T(8,128)}, u32[]{:S(2)}) copy-start(f32[2,8,128]{2,1,0:T(8,128)} %constant.32.clone.turns) | copy-start | bytes 24580
  21.1 8.2 %collective-permute-start.1 = (f32[2,2,2,32,128]{4,3,2,1,0:T(8,128)S(1)}, f32[2,2,2,32,128]{4,3,2,1,0:T(8,128)S(1)}, u32[]{:S(2)}, u32[]{:S(2)}) collective-permute-start(f32[2,2,2,32,128]{4,3,2,1,0:T(8,128)S(1)} %get-tuple-element.18), channel_id=1, source_target_pairs={{0,4},{4,0},{8,12},{12,8},{1,5},{5,1},{9,13},{13,9},{2,6},{6,2},{1... | collective-permute-start | bytes 393224 | tf_op jit(solution)/shard_map/ppermute | solution.py:549
  32.8 14.1 %all-to-all-start.1 = ((f32[8,2,32,128]{3,2,1,0:T(8,128)}), f32[8,2,32,128]{3,2,1,0:T(8,128)S(1)}, u32[]{:S(2)}, u32[]{:S(2)}) async-start(f32[8,2,32,128]{3,2,1,0:T(8,128)} %forward.1), calls=%async_computation.1 | async-start | bytes 524288 | tf_op jit(solution)/shard_map/all_to_all | solution.py:540
  36.2 17.4 %collective-permute-start.3 = (f32[2,2,2,32,128]{4,3,2,1,0:T(8,128)S(1)}, f32[2,2,2,32,128]{4,3,2,1,0:T(8,128)S(1)}, u32[]{:S(2)}, u32[]{:S(2)}) collective-permute-start(f32[2,2,2,32,128]{4,3,2,1,0:T(8,128)S(1)} %pad_maximum_fusion), channel_id=1, source_target_pairs={{0,12},{4,8},{8,4},{12,0},{1,13},{5,9},{9,5},{13,1},{2,14},{6,10},... | collective-permute-start | bytes 393224 | tf_op jit(solution)/shard_map/ppermute | solution.py:551
  46.8 6.8 %copy-start.7 = (bf16[64,128]{1,0:T(8,128)(2,1)S(1)}, bf16[64,128]{1,0:T(8,128)(2,1)}, u32[]{:S(2)}) copy-start(bf16[64,128]{1,0:T(8,128)(2,1)} %constant.31.clone.spread) | copy-start | bytes 49156
  46.8 7.1 %collective-permute-start.2 = (f32[8,32,128]{2,1,0:T(8,128)S(1)}, f32[8,32,128]{2,1,0:T(8,128)S(1)}, u32[]{:S(2)}, u32[]{:S(2)}) collective-permute-start(f32[8,32,128]{2,1,0:T(8,128)S(1)} %pick.1.edge), channel_id=1, source_target_pairs={{16,64},{80,128},{144,192},{208,256},{272,320},{336,384},{400,448}... | collective-permute-start | bytes 393224 | tf_op jit(solution)/shard_map/ppermute | solution.py:556
  48.8 5.9 %collective-permute-start.4 = (f32[2,8,32,128]{3,2,1,0:T(8,128)S(1)}, f32[2,8,32,128]{3,2,1,0:T(8,128)S(1)}, u32[]{:S(2)}, u32[]{:S(2)}) collective-permute-start(f32[2,8,32,128]{3,2,1,0:T(8,128)S(1)} %bitcast.8), channel_id=1, source_target_pairs={{0,16},{16,0},{1,17},{17,1},{2,18},{18,2},{3,19},{19,3},{4,20},{20... | collective-permute-start | bytes 786440 | tf_op jit(solution)/shard_map/ppermute | solution.py:557
  56.1 7.0 %collective-permute-start.5 = (f32[8,32,128]{2,1,0:T(8,128)S(1)}, f32[8,32,128]{2,1,0:T(8,128)S(1)}, u32[]{:S(2)}, u32[]{:S(2)}) collective-permute-start(f32[8,32,128]{2,1,0:T(8,128)S(1)} %get-tuple-element.25.edge), channel_id=1, source_target_pairs={{16,64},{80,128},{144,192},{208,256},{272,320},{336,384},{400,448}... | collective-permute-start | bytes 393224 | tf_op jit(solution)/shard_map/ppermute | solution.py:556
  58.0 6.2 %collective-permute-start.6 = (f32[2,8,32,128]{3,2,1,0:T(8,128)S(1)}, f32[2,8,32,128]{3,2,1,0:T(8,128)S(1)}, u32[]{:S(2)}, u32[]{:S(2)}) collective-permute-start(f32[2,8,32,128]{3,2,1,0:T(8,128)S(1)} %get-tuple-element.26.own), channel_id=1, source_target_pairs={{0,16},{16,0},{1,17},{17,1},{2,18},{18,2},{3,19},{19,3},{4,20},{20... | collective-permute-start | bytes 786440 | tf_op jit(solution)/shard_map/ppermute | solution.py:557
  65.7 15.3 %copy-start.1 = (bf16[2,256,256]{2,1,0:T(8,128)(2,1)S(1)}, bf16[2,256,256]{2,1,0:T(8,128)(2,1)}, u32[]{:S(2)}) copy-start(bf16[2,256,256]{2,1,0:T(8,128)(2,1)} %constant.29.clone.high) | copy-start | bytes 786436
  65.7 15.2 %copy-start.2 = (bf16[2,256,256]{2,1,0:T(8,128)(2,1)S(1)}, bf16[2,256,256]{2,1,0:T(8,128)(2,1)}, u32[]{:S(2)}) copy-start(bf16[2,256,256]{2,1,0:T(8,128)(2,1)} %constant.30.clone.low) | copy-start | bytes 786436

commit v6 on v5

--- a/solution.py
+++ b/solution.py
@@ -265,38 +265,39 @@
 SUMS = len(PAIRS) + len(OFF) + 2 * FILT
 
 
-def windows_kernel(weights, live, got, here, across, beside, held):
-    own, x = lax.axis_index("zh"), lax.axis_index("x")
+def windows_kernel(weights, live, *refs):
+    *outs, held = refs
+    x = lax.axis_index("x")
     alive = live[...].astype(f32)
     for n in range(ITERS):
-        mine, other = [], []
+        rows = []
         for i in range(FILT):
-            start = n * BINS * FILT + own * HALF * FILT + i
-            mine.append(weights[pl.ds(start, HALF, stride=FILT), :] * alive[i : i + 1])
-            other.append(got[n, pl.ds(i, HALF, stride=FILT), :])
-        for rows, beta in ((mine, own), (other, 1 - own)):
-            for w, block in enumerate(swap_blocks(rows, lanes_of(HALF), WX)):
-                held[w, beta, n] = block
-    pair = x + 1 - 2 * lax.rem(x, 2)
-    here[...] = held[x]
-    across[...] = held[WINDOWS - 1 - x]
-    beside[0] = held[pair]
-    beside[1] = held[WINDOWS - 1 - pair]
-
-
-def prepare_kernel(here, beside, across, spread, omega, held):
-    x = lax.axis_index("x")
-    pair = x + 1 - 2 * lax.rem(x, 2)
-    held[x] = here[...]
-    held[pair] = beside[0]
-    held[WINDOWS - 1 - x] = across[0]
-    held[WINDOWS - 1 - pair] = across[1]
+            start = n * BINS * FILT + i
+            rows.append(weights[pl.ds(start, BINS, stride=FILT), :] * alive[i : i + 1])
+        for w, block in enumerate(swap_blocks(rows, lanes_of(BINS), WX)):
+            held[w, n] = block
+    for k, out in enumerate(outs):
+        out[...] = held[lax.rem(x + k, WINDOWS)]
+
+
+def halves_kernel(*refs):
+    *sources, keep, give = refs
+    x, own = lax.axis_index("x"), lax.axis_index("zh") * HALF
+    for k, source in enumerate(sources):
+        place = lax.rem(x + WINDOWS - k, WINDOWS)
+        for n in range(ITERS):
+            keep[place, n] = source[n, pl.ds(pl.multiple_of(own, HALF), HALF), :]
+            give[place, n] = source[n, pl.ds(pl.multiple_of(HALF - own, HALF), HALF), :]
+
+
+def prepare_kernel(keep, got, spread, omega):
+    own = lax.axis_index("zh")
     table = spread[...]
     over = (((0,), (0,)), ((), ()))
     for n in range(ITERS):
-        for beta in range(2):
+        for source, beta in ((keep, own), (got, 1 - own)):
             for kappa in range(2):
-                rows = jnp.concatenate([held[2 * kappa + a, beta, n] for a in range(2)], axis=0)
+                rows = jnp.concatenate([source[2 * kappa + a, n] for a in range(2)], axis=0)
                 top = rows.astype(bf16)
                 rest = (rows - top.astype(f32)).astype(bf16)
                 omega[n, beta * 2 + kappa] = lax.dot_general(
@@ -462,21 +463,12 @@
 ROWS = WX
 TILES = (2 * FILT, TWO, ROWS, LANES)
 EDGE = (TWO * FILT, ROWS, LANES)
-PART = (2, ITERS, HALF, LANES)
-GIVE = (ITERS, HALF * FILT, LANES)
+PART = (ITERS, BINS, LANES)
+HALVES = (WINDOWS, ITERS, HALF, LANES)
 
 
 def send_call(traces):
     return kernel_call(send_kernel, [TRACES], name="send")(traces.reshape(SPAN * FILT, LANES))
-
-
-def share(weights, live):
-    start = (1 - lax.axis_index("zh")) * HALF
-    zero = jnp.zeros_like(start)
-    mine = lax.dynamic_slice(
-        weights, (zero, start, zero, zero), (ITERS, HALF, FILT, LANES), allow_negative_indices=False
-    )
-    return jnp.where(live > 0, mine, 0.0).reshape(GIVE)
 
 
 def forward_call(blocks, live, *tables):
@@ -488,16 +480,21 @@
     return kernel_call(inverse_kernel, [TRACES], name="inverse")(blocks, *tables)
 
 
-def windows_call(weights, live, got):
-    cost = pl.CostEstimate(flops=16_000_000_000, bytes_accessed=64_000_000, transcendentals=0)
+LONG = pl.CostEstimate(flops=16_000_000_000, bytes_accessed=64_000_000, transcendentals=0)
+
+
+def windows_call(weights, live):
     scratch = [pltpu.VMEM((WINDOWS,) + PART, f32)]
-    return kernel_call(windows_kernel, [PART, PART, (2,) + PART], scratch, "windows", cost)(weights, live, got)
+    return kernel_call(windows_kernel, [PART] * WINDOWS, scratch, "windows")(weights, live)
+
+
+def halves_call(*arrays):
+    return kernel_call(halves_kernel, [HALVES, HALVES], (), "halves", LONG)(*arrays)
 
 
 def prepare_call(*arrays):
     shape = (ITERS, 2 * TWO, FILT * ROWS, LANES)
-    scratch = [pltpu.VMEM((WINDOWS,) + PART, f32)]
-    return kernel_call(prepare_kernel, [shape], scratch, "prepare")(*arrays)
+    return kernel_call(prepare_kernel, [shape], (), "prepare")(*arrays)
 
 
 def filter_scratch(blocks, jobs):
@@ -509,8 +506,7 @@
 
 
 def pick_call(block):
-    cost = pl.CostEstimate(flops=16_000_000_000, bytes_accessed=64_000_000, transcendentals=0)
-    return kernel_call(pick_kernel, [EDGE], (), "pick", cost)(block)
+    return kernel_call(pick_kernel, [EDGE], (), "pick", LONG)(block)
 
 
 def beyond_call(n, edge, beyond, omegas):
@@ -544,20 +540,21 @@
     shift = [(2 * y + 1, 2 * y + 2) for y in range(ys - 1)] + [(2 * y + 2, 2 * y + 1) for y in range(ys - 1)]
     weights = reweights.reshape(ITERS * BINS * FILT, LANES)
     sent = send_call(traces_in)
-    got = lax.ppermute(share(reweights, live_mask), "zh", swap)
-    here, across, beside = windows_call(weights, live_mask, got)
-    beside = lax.ppermute(beside, "x", [(i, i ^ 1) for i in range(WINDOWS)])
-    sent, here, across, beside = lax.optimization_barrier((exchange(sent, ("x", "zl")), here, across, beside))
-    across = lax.ppermute(jnp.stack([across, beside[1]]), "x", [(i, WINDOWS - 1 - i) for i in range(WINDOWS)])
-    block = exchange(forward_call(sent, live_mask, fh, fl, turns), ("zh", "zl")).reshape((2,) + EDGE)
+    shares = list(windows_call(weights, live_mask))
+    for k in range(1, WINDOWS):
+        shares[k] = lax.ppermute(shares[k], "x", [(i, (i + k) % WINDOWS) for i in range(WINDOWS)])
+    keep, give = halves_call(*shares)
+    got = lax.ppermute(give, "zh", swap)
+    spectra = forward_call(exchange(sent, ("x", "zl")), live_mask, fh, fl, turns)
+    block = exchange(spectra, ("zh", "zl")).reshape((2,) + EDGE)
     edge = pick_call(block)
     omegas = None
     for n in range(ITERS):
         beyond = lax.ppermute(edge, ("y", "c"), shift)
         partner = lax.ppermute(block, "c", swap)
         if omegas is None:
-            edge, across = lax.optimization_barrier((edge, across))
-            omegas = prepare_call(here, beside, across, spread)
+            edge, got = lax.optimization_barrier((edge, got))
+            omegas = prepare_call(keep, got, spread)
         part = beyond_call(n, edge, beyond, omegas)
         found = filter_call(n, part, block, partner, omegas)
         block, edge = found if n + 1 < ITERS else (found, None)

time: 98.6 us -> 96.6 us (0.980)
  starting transfers between devices: 42.7 us -> 50.9 us
  waiting for transfers between devices: 14 us -> 6.15 us
  other arithmetic: 1.67 us -> 0 us
  blocking collectives: 30.8 us -> 29.2 us
    all_to_all x2, starting transfers between devices: 10.7 us -> 17.5 us  [exchange(): return lax.all_to_all(blocks, axes, 0, 0, tiled=True)]
    ppermute x3 -> x4, waiting for transfers between devices: 4.38 us -> 0.01 us  [the longest x3 0.01 us: local(): lax.ppermute(shares[k], 'x', [(i, (i + k) % WINDOWS) for i in range(WINDO...]
    all_to_all x2, waiting for transfers between devices: 9.05 us -> 5.49 us  [exchange(): return lax.all_to_all(blocks, axes, 0, 0, tiled=True)]
    all_to_all x2, blocking collectives: 30.8 us -> 29.2 us  [exchange(): return lax.all_to_all(blocks, axes, 0, 0, tiled=True)]
    ppermute x3 -> x4, starting transfers between devices: 18.3 us -> 19.6 us  [the longest x3 11.8 us: local(): lax.ppermute(shares[k], 'x', [(i, (i + k) % WINDOWS) for i in range(WINDO...]
  transfers between devices with their start and end apart: 9 -> 10, of which waited for: 5 -> 3; matrix products, arithmetic and copies ran while one was open for 0% -> 0% of each run, Pallas kernels for 2% -> 4%
where the time goes in v6:
time: 96.6 us; the launch traced here: 95.9 us
  starting transfers between devices  50.9 us (53%)
  blocking collectives  29.2 us (30%)
  Pallas kernels  8.45 us (9%)
  waiting for transfers between devices  6.15 us (6%)
  local copies, waits for them, and re-layouts  0.99 us (1%)
    all_to_all x2, blocking collectives, exchange(): return lax.all_to_all(blocks, axes, 0, 0, tiled=True)  29.2 us
    all_to_all x2, starting transfers between devices, exchange(): return lax.all_to_all(blocks, axes, 0, 0, tiled=True)  17.5 us
    ppermute x3, starting transfers between devices, local(): lax.ppermute(shares[k], 'x', [(i, (i + k) % WINDOWS) for i in range(WINDO...  11.8 us
    ppermute x2, starting transfers between devices, local(): partner = lax.ppermute(block, 'c', swap)  9.87 us
    ppermute x1, starting transfers between devices, local(): got = lax.ppermute(give, 'zh', swap)  7.83 us
    all_to_all x2, waiting for transfers between devices, exchange(): return lax.all_to_all(blocks, axes, 0, 0, tiled=True)  5.49 us
    ppermute x2, starting transfers between devices, local(): beyond = lax.ppermute(edge, ('y', 'c'), shift)  3.84 us
    pallas_call x2, Pallas kernels, filter_call(): kernel_call(body, shapes, filter_scratch(4, 3), name='filter')  2.78 us
  transfers between devices with their start and end apart: 10, of which 3 were waited for; matrix products, arithmetic and copies ran while one was open for 0% of the time, Pallas kernels for 4%

profile of v6, /device:TPU:24, one launch (start us, length us, event | category | flops | bytes accessed | tf_op | source)
XLA Modules:
  0.0 95.9 jit_solution(1721283326265387745)
XLA Ops:
  0.0 0.0 copy-start
  0.0 0.9 copy-done
  1.0 0.0 copy-start.8
  1.0 0.8 send.1
  1.8 0.0 copy-start.1
  1.8 10.0 %all-to-all-start = ((f32[16,32,128]{2,1,0:T(8,128)}), f32[16,32,128]{2,1,0:T(8,128)S(1)}, u32[]{:S(2)}, u32[]{:S(2)}) async-start(f32[16,32,128]{2,1,0:T(8,128)} %send.1), calls=%async_computation | async-start | bytes 524288 | tf_op jit(solution)/shard_map/all_to_all | solution.py:536
  11.8 0.0 copy-start.4
  11.8 0.0 copy-done.8
  11.8 0.0 copy-done.1
  11.8 0.0 copy-start.6
  11.8 0.3 windows.1
  12.1 3.8 %collective-permute-start.1 = (f32[2,64,128]{2,1,0:T(8,128)S(1)}, f32[2,64,128]{2,1,0:T(8,128)S(1)}, u32[]{:S(2)}, u32[]{:S(2)}) collective-permute-start(f32[2,64,128]{2,1,0:T(8,128)S(1)} %get-tuple-element.16), channel_id=1, source_target_pairs={{0,4},{4,8},{8,12},{12,0},{1,5},{5,9},{9,13},{13,1},{2,6},{6,10},{... | collective-permute-start | bytes 196616 | tf_op jit(solution)/shard_map/ppermute | solution.py:545
  16.0 4.6 %collective-permute-start.2 = (f32[2,64,128]{2,1,0:T(8,128)S(1)}, f32[2,64,128]{2,1,0:T(8,128)S(1)}, u32[]{:S(2)}, u32[]{:S(2)}) collective-permute-start(f32[2,64,128]{2,1,0:T(8,128)S(1)} %get-tuple-element.17), channel_id=1, source_target_pairs={{0,8},{4,12},{8,0},{12,4},{1,9},{5,13},{9,1},{13,5},{2,10},{6,14},... | collective-permute-start | bytes 196616 | tf_op jit(solution)/shard_map/ppermute | solution.py:545
  20.5 3.4 %collective-permute-start.3 = (f32[2,64,128]{2,1,0:T(8,128)S(1)}, f32[2,64,128]{2,1,0:T(8,128)S(1)}, u32[]{:S(2)}, u32[]{:S(2)}) collective-permute-start(f32[2,64,128]{2,1,0:T(8,128)S(1)} %get-tuple-element.18), channel_id=1, source_target_pairs={{0,12},{4,0},{8,4},{12,8},{1,13},{5,1},{9,5},{13,9},{2,14},{6,2},{... | collective-permute-start | bytes 196616 | tf_op jit(solution)/shard_map/ppermute | solution.py:545
  23.9 0.0 all-to-all-done.blocks
  23.9 0.0 copy-done.5
  23.9 0.0 copy-done.4
  24.0 0.0 copy-done.6
  24.0 1.4 %forward.1 = f32[8,2,32,128]{3,2,1,0:T(8,128)} custom-call(f32[16,32,128]{2,1,0:T(8,128)S(1)} %all-to-all-done.blocks, s32[4,128]{1,0:T(4,128)S(1)} %copy-done.8, bf16[2,256,256]{2,1,0:T(8,128)(2,1)S(1)} %copy-done.5, bf16[2,256,256]{2,1,0:T(8,128)(2,1)S(1)} %copy-done.4, f32[2,8,128]{2,1,0:T(8,128)S(1)} %copy-done.6), custom_call_target="tpu_custom_call" | custom-call | tf_op jit(solution)/shard_map/forward/pallas_call | solution.py:476
  25.4 7.6 %all-to-all-start.1 = ((f32[8,2,32,128]{3,2,1,0:T(8,128)}), f32[8,2,32,128]{3,2,1,0:T(8,128)S(1)}, u32[]{:S(2)}, u32[]{:S(2)}) async-start(f32[8,2,32,128]{3,2,1,0:T(8,128)} %forward.1), calls=%async_computation.1 | async-start | bytes 524288 | tf_op jit(solution)/shard_map/all_to_all | solution.py:536
  33.0 0.0 collective-permute-done.1.refs_1_
  33.0 0.0 collective-permute-done.2.refs_2_
  33.0 0.0 collective-permute-done.3.refs_3_
  33.1 7.8 %collective-permute-start.4 = (f32[4,2,32,128]{3,2,1,0:T(8,128)S(1)}, f32[4,2,32,128]{3,2,1,0:T(8,128)S(1)}, u32[]{:S(2)}, u32[]{:S(2)}) collective-permute-start(f32[4,2,32,128]{3,2,1,0:T(8,128)S(1)} %get-tuple-element.19), channel_id=1, source_target_pairs={{0,32},{32,0},{1,33},{33,1},{2,34},{34,2},{3,35},{35,3},{4,36},{36... | collective-permute-start | bytes 393224 | tf_op jit(solution)/shard_map/ppermute | solution.py:547
  40.9 5.5 %all-to-all-done.1 = f32[8,2,32,128]{3,2,1,0:T(8,128)S(1)} async-done(((f32[8,2,32,128]{3,2,1,0:T(8,128)}), f32[8,2,32,128]{3,2,1,0:T(8,128)S(1)}, u32[]{:S(2)}, u32[]{:S(2)}) %all-to-all-start.1) | async-done | bytes 262176 | tf_op jit(solution)/shard_map/all_to_all | solution.py:536
  46.4 1.9 %collective-permute-start = (f32[8,32,128]{2,1,0:T(8,128)S(1)}, f32[8,32,128]{2,1,0:T(8,128)S(1)}, u32[]{:S(2)}, u32[]{:S(2)}) collective-permute-start(f32[8,32,128]{2,1,0:T(8,128)S(1)} %pick.1.edge), channel_id=1, source_target_pairs={{16,64},{80,128},{144,192},{208,256},{272,320},{336,384},{400,448}... | collective-permute-start | bytes 393224 | tf_op jit(solution)/shard_map/ppermute | solution.py:553
  48.3 4.8 %collective-permute-start.5 = (f32[2,8,32,128]{3,2,1,0:T(8,128)S(1)}, f32[2,8,32,128]{3,2,1,0:T(8,128)S(1)}, u32[]{:S(2)}, u32[]{:S(2)}) collective-permute-start(f32[2,8,32,128]{3,2,1,0:T(8,128)S(1)} %bitcast.6), channel_id=1, source_target_pairs={{0,16},{16,0},{1,17},{17,1},{2,18},{18,2},{3,19},{19,3},{4,20},{20... | collective-permute-start | bytes 786440 | tf_op jit(solution)/shard_map/ppermute | solution.py:554
  53.1 0.0 collective-permute-done.4.got
  53.1 0.0 copy-done.7
  53.2 0.3 prepare.1.omegas
  53.5 0.0 collective-permute-done.beyond
  53.5 0.6 beyond.2.part
  54.1 0.1 collective-permute-done.5.partner
  54.3 1.4 %filter.2 = (f32[2,8,32,128]{3,2,1,0:T(8,128)S(1)}, f32[8,32,128]{2,1,0:T(8,128)S(1)}) custom-call(f32[8,32,128]{2,1,0:T(8,128)S(1)} %beyond.2.part, f32[2,8,32,128]{3,2,1,0:T(8,128)S(1)} %bitcast.7, f32[2,8,32,128]{3,2,1,0:T(8,128)S(1)} %collective-permute-done.5.partner, f32[2,4,128,128]{3,2,1,0:T(8,128)S(1)} %prepare.1.omegas), custom_call_target="tpu_custom_call" | custom-call | tf_op jit(solution)/shard_map/filter/pallas_call | solution.py:522
  55.7 1.9 %collective-permute-start.6 = (f32[8,32,128]{2,1,0:T(8,128)S(1)}, f32[8,32,128]{2,1,0:T(8,128)S(1)}, u32[]{:S(2)}, u32[]{:S(2)}) collective-permute-start(f32[8,32,128]{2,1,0:T(8,128)S(1)} %get-tuple-element.23.edge), channel_id=1, source_target_pairs={{16,64},{80,128},{144,192},{208,256},{272,320},{336,384},{400,448}... | collective-permute-start | bytes 393224 | tf_op jit(solution)/shard_map/ppermute | solution.py:553
  57.6 5.1 %collective-permute-start.7 = (f32[2,8,32,128]{3,2,1,0:T(8,128)S(1)}, f32[2,8,32,128]{3,2,1,0:T(8,128)S(1)}, u32[]{:S(2)}, u32[]{:S(2)}) collective-permute-start(f32[2,8,32,128]{3,2,1,0:T(8,128)S(1)} %get-tuple-element.24.own), channel_id=1, source_target_pairs={{0,16},{16,0},{1,17},{17,1},{2,18},{18,2},{3,19},{19,3},{4,20},{20... | collective-permute-start | bytes 786440 | tf_op jit(solution)/shard_map/ppermute | solution.py:554
  62.7 0.0 collective-permute-done.6.beyond
  62.7 0.6 beyond.3.part
  63.3 0.5 collective-permute-done.7.partner
  63.8 1.4 %filter.3 = f32[2,8,32,128]{3,2,1,0:T(8,128)S(1)} custom-call(f32[8,32,128]{2,1,0:T(8,128)S(1)} %beyond.3.part, f32[2,8,32,128]{3,2,1,0:T(8,128)S(1)} %get-tuple-element.24.own, f32[2,8,32,128]{3,2,1,0:T(8,128)S(1)} %collective-permute-done.7.partner, f32[2,4,128,128]{3,2,1,0:T(8,128)S(1)} %prepare.1.omegas), custom_call_target="tpu_custom_call" | custom-call | tf_op jit(solution)/shard_map/filter/pallas_call | solution.py:522
  65.2 0.0 copy-start.2
  65.2 0.0 copy-start.3
  65.2 15.2 %all_to_all.20.blocks = f32[8,2,32,128]{3,2,1,0:T(8,128)S(1)} all-to-all(f32[8,2,32,128]{3,2,1,0:T(8,128)S(1)} %bitcast.8), channel_id=1, replica_groups=mesh['y'=8,'zh'=2,'c'=2,'x'=4,'zl'=4] {'zh','zl'}, dimensions={0} | all-to-all | bytes 524288 | tf_op jit(solution)/shard_map/all_to_all | solution.py:536
  80.5 0.0 copy-done.2
  80.5 0.0 copy-done.3
  80.5 0.6 inverse.1
  81.1 14.0 %all_to_all.21.blocks = f32[16,32,128]{2,1,0:T(8,128)S(1)} all-to-all(f32[16,32,128]{2,1,0:T(8,128)S(1)} %inverse.1), channel_id=1, replica_groups=mesh['y'=8,'zh'=2,'c'=2,'x'=4,'zl'=4] {'x','zl'}, dimensions={0} | all-to-all | bytes 524288 | tf_op jit(solution)/shard_map/all_to_all | solution.py:536
  95.1 0.8 receive.1
  (4 shorter events, 0.0 us)
Async XLA Ops:
  0.0 0.9 copy-start
  1.0 10.8 %copy-start.8 = (s32[4,128]{1,0:T(4,128)S(1)}, s32[4,128]{1,0:T(4,128)}, u32[]{:S(2)}) copy-start(s32[4,128]{1,0:T(4,128)} %live.3) | copy-start | bytes 6148
  1.8 10.0 %copy-start.1 = (f32[2,64,4,128]{3,2,1,0:T(4,128)S(1)}, f32[2,64,4,128]{3,2,1,0:T(4,128)}, u32[]{:S(2)}) copy-start(f32[2,64,4,128]{3,2,1,0:T(4,128)} %param.10) | copy-start | bytes 786436
  1.8 22.1 %copy-start.5 = (bf16[2,256,256]{2,1,0:T(8,128)(2,1)S(1)}, bf16[2,256,256]{2,1,0:T(8,128)(2,1)}, u32[]{:S(2)}) copy-start(bf16[2,256,256]{2,1,0:T(8,128)(2,1)} %constant.12.clone.high) | copy-start | bytes 786436
  1.8 22.1 %all-to-all-start = ((f32[16,32,128]{2,1,0:T(8,128)}), f32[16,32,128]{2,1,0:T(8,128)S(1)}, u32[]{:S(2)}, u32[]{:S(2)}) async-start(f32[16,32,128]{2,1,0:T(8,128)} %send.1), calls=%async_computation | async-start | bytes 524288 | tf_op jit(solution)/shard_map/all_to_all | solution.py:536
  11.8 12.2 %copy-start.4 = (bf16[2,256,256]{2,1,0:T(8,128)(2,1)S(1)}, bf16[2,256,256]{2,1,0:T(8,128)(2,1)}, u32[]{:S(2)}) copy-start(bf16[2,256,256]{2,1,0:T(8,128)(2,1)} %constant.13.clone.low) | copy-start | bytes 786436
  11.8 12.2 %copy-start.6 = (f32[2,8,128]{2,1,0:T(8,128)S(1)}, f32[2,8,128]{2,1,0:T(8,128)}, u32[]{:S(2)}) copy-start(f32[2,8,128]{2,1,0:T(8,128)} %constant.17.clone.turns) | copy-start | bytes 24580
  12.1 20.9 %collective-permute-start.1 = (f32[2,64,128]{2,1,0:T(8,128)S(1)}, f32[2,64,128]{2,1,0:T(8,128)S(1)}, u32[]{:S(2)}, u32[]{:S(2)}) collective-permute-start(f32[2,64,128]{2,1,0:T(8,128)S(1)} %get-tuple-element.16), channel_id=1, source_target_pairs={{0,4},{4,8},{8,12},{12,0},{1,5},{5,9},{9,13},{13,1},{2,6},{6,10},{... | collective-permute-start | bytes 196616 | tf_op jit(solution)/shard_map/ppermute | solution.py:545
  16.0 17.0 %collective-permute-start.2 = (f32[2,64,128]{2,1,0:T(8,128)S(1)}, f32[2,64,128]{2,1,0:T(8,128)S(1)}, u32[]{:S(2)}, u32[]{:S(2)}) collective-permute-start(f32[2,64,128]{2,1,0:T(8,128)S(1)} %get-tuple-element.17), channel_id=1, source_target_pairs={{0,8},{4,12},{8,0},{12,4},{1,9},{5,13},{9,1},{13,5},{2,10},{6,14},... | collective-permute-start | bytes 196616 | tf_op jit(solution)/shard_map/ppermute | solution.py:545
  20.5 12.5 %collective-permute-start.3 = (f32[2,64,128]{2,1,0:T(8,128)S(1)}, f32[2,64,128]{2,1,0:T(8,128)S(1)}, u32[]{:S(2)}, u32[]{:S(2)}) collective-permute-start(f32[2,64,128]{2,1,0:T(8,128)S(1)} %get-tuple-element.18), channel_id=1, source_target_pairs={{0,12},{4,0},{8,4},{12,8},{1,13},{5,1},{9,5},{13,9},{2,14},{6,2},{... | collective-permute-start | bytes 196616 | tf_op jit(solution)/shard_map/ppermute | solution.py:545
  25.4 21.0 %all-to-all-start.1 = ((f32[8,2,32,128]{3,2,1,0:T(8,128)}), f32[8,2,32,128]{3,2,1,0:T(8,128)S(1)}, u32[]{:S(2)}, u32[]{:S(2)}) async-start(f32[8,2,32,128]{3,2,1,0:T(8,128)} %forward.1), calls=%async_computation.1 | async-start | bytes 524288 | tf_op jit(solution)/shard_map/all_to_all | solution.py:536
  33.1 20.1 %collective-permute-start.4 = (f32[4,2,32,128]{3,2,1,0:T(8,128)S(1)}, f32[4,2,32,128]{3,2,1,0:T(8,128)S(1)}, u32[]{:S(2)}, u32[]{:S(2)}) collective-permute-start(f32[4,2,32,128]{3,2,1,0:T(8,128)S(1)} %get-tuple-element.19), channel_id=1, source_target_pairs={{0,32},{32,0},{1,33},{33,1},{2,34},{34,2},{3,35},{35,3},{4,36},{36... | collective-permute-start | bytes 393224 | tf_op jit(solution)/shard_map/ppermute | solution.py:547
  46.4 6.8 %copy-start.7 = (bf16[64,128]{1,0:T(8,128)(2,1)S(1)}, bf16[64,128]{1,0:T(8,128)(2,1)}, u32[]{:S(2)}) copy-start(bf16[64,128]{1,0:T(8,128)(2,1)} %constant.16.clone.spread) | copy-start | bytes 49156
  46.4 7.1 %collective-permute-start = (f32[8,32,128]{2,1,0:T(8,128)S(1)}, f32[8,32,128]{2,1,0:T(8,128)S(1)}, u32[]{:S(2)}, u32[]{:S(2)}) collective-permute-start(f32[8,32,128]{2,1,0:T(8,128)S(1)} %pick.1.edge), channel_id=1, source_target_pairs={{16,64},{80,128},{144,192},{208,256},{272,320},{336,384},{400,448}... | collective-permute-start | bytes 393224 | tf_op jit(solution)/shard_map/ppermute | solution.py:553
  48.3 5.9 %collective-permute-start.5 = (f32[2,8,32,128]{3,2,1,0:T(8,128)S(1)}, f32[2,8,32,128]{3,2,1,0:T(8,128)S(1)}, u32[]{:S(2)}, u32[]{:S(2)}) collective-permute-start(f32[2,8,32,128]{3,2,1,0:T(8,128)S(1)} %bitcast.6), channel_id=1, source_target_pairs={{0,16},{16,0},{1,17},{17,1},{2,18},{18,2},{3,19},{19,3},{4,20},{20... | collective-permute-start | bytes 786440 | tf_op jit(solution)/shard_map/ppermute | solution.py:554
  55.7 7.0 %collective-permute-start.6 = (f32[8,32,128]{2,1,0:T(8,128)S(1)}, f32[8,32,128]{2,1,0:T(8,128)S(1)}, u32[]{:S(2)}, u32[]{:S(2)}) collective-permute-start(f32[8,32,128]{2,1,0:T(8,128)S(1)} %get-tuple-element.23.edge), channel_id=1, source_target_pairs={{16,64},{80,128},{144,192},{208,256},{272,320},{336,384},{400,448}... | collective-permute-start | bytes 393224 | tf_op jit(solution)/shard_map/ppermute | solution.py:553
  57.6 6.2 %collective-permute-start.7 = (f32[2,8,32,128]{3,2,1,0:T(8,128)S(1)}, f32[2,8,32,128]{3,2,1,0:T(8,128)S(1)}, u32[]{:S(2)}, u32[]{:S(2)}) collective-permute-start(f32[2,8,32,128]{3,2,1,0:T(8,128)S(1)} %get-tuple-element.24.own), channel_id=1, source_target_pairs={{0,16},{16,0},{1,17},{17,1},{2,18},{18,2},{3,19},{19,3},{4,20},{20... | collective-permute-start | bytes 786440 | tf_op jit(solution)/shard_map/ppermute | solution.py:554
  65.2 15.3 %copy-start.2 = (bf16[2,256,256]{2,1,0:T(8,128)(2,1)S(1)}, bf16[2,256,256]{2,1,0:T(8,128)(2,1)}, u32[]{:S(2)}) copy-start(bf16[2,256,256]{2,1,0:T(8,128)(2,1)} %constant.15.clone.low) | copy-start | bytes 786436
  65.2 15.2 %copy-start.3 = (bf16[2,256,256]{2,1,0:T(8,128)(2,1)S(1)}, bf16[2,256,256]{2,1,0:T(8,128)(2,1)}, u32[]{:S(2)}) copy-start(bf16[2,256,256]{2,1,0:T(8,128)(2,1)} %constant.14.clone.high) | copy-start | bytes 786436

commit v7 on v6

--- a/solution.py
+++ b/solution.py
@@ -28,6 +28,7 @@
 
 INNER = [(a, s, b) for a in range(2) for s in range(2) for b in range(2)]
 HALF = BINS // 2
+SETS = ((0, 3), (1, 2))
 
 
 def split_table(table):
@@ -44,7 +45,7 @@
         kappa, part = divmod(spot, 8)
         zh, zl = divmod(part, 4)
         for place, (a, s, b) in enumerate(INNER):
-            base = BINS * (4 * (2 * kappa + a) + zl) + HALF * zh + 16 * b
+            base = BINS * (4 * SETS[kappa][a] + zl) + HALF * zh + 16 * b
             col = spot * 8 + place
             f = base + 8 * s
             angle = 2.0 * np.pi * ((f * r) % NT) / NT
@@ -170,6 +171,10 @@
     return lax.broadcasted_iota(jnp.int32, (rows, LANES), 1)
 
 
+def place_x():
+    return 2 * lax.axis_index("xq") + lax.axis_index("xr")
+
+
 def send_kernel(traces, out):
     for i in range(FILT):
         turned = traces[pl.ds(i, SPAN, stride=FILT), :].T
@@ -178,9 +183,10 @@
 
 
 def forward_kernel(blocks, live, high, low, turns, out, alive):
+    xq = lax.axis_index("xq")
     row = live[pl.ds(lax.axis_index("zl"), 1), :].astype(f32)
     alive[...] = jnp.broadcast_to(row, (LANES, LANES)).T
-    mask = alive[pl.ds(pl.multiple_of(lax.axis_index("x") * WX, WX), WX), :]
+    mask = alive[pl.ds(pl.multiple_of(place_x() * WX, WX), WX), :]
     lane = lanes_of(WX)
     bins = real_transform([blocks[j] * mask for j in range(RADIX)])
     first = split_dot(jnp.concatenate([bins[0][0], bins[8][0]], axis=1), high[0], low[0])
@@ -194,16 +200,19 @@
     real, imag = swap_blocks(real, lane, 8), swap_blocks(imag, lane, 8)
     left = lane < BINS
     for part in range(8):
-        out[part, 0] = jnp.where(left, real[part], pltpu.roll(imag[part], BINS, 1))
-        out[part, 1] = jnp.where(left, pltpu.roll(real[part], BINS, 1), imag[part])
+        place = part // 4 * 8 + part % 4
+        out[place + 4 * xq] = jnp.where(left, real[part], pltpu.roll(imag[part], BINS, 1))
+        out[place + 4 - 4 * xq] = jnp.where(left, pltpu.roll(real[part], BINS, 1), imag[part])
 
 
 def inverse_kernel(blocks, high, low, turns, out):
+    xq = lax.axis_index("xq")
     lane = lanes_of(WX)
     left = lane < BINS
     real, imag = [], []
     for part in range(8):
-        first, second = blocks[part, 0], blocks[part, 1]
+        place = part // 4 * 8 + part % 4
+        first, second = blocks[place + 4 * xq], blocks[place + 4 - 4 * xq]
         real.append(jnp.where(left, first, pltpu.roll(second, BINS, 1)))
         imag.append(jnp.where(left, pltpu.roll(first, BINS, 1), second))
     real, imag = swap_blocks(real, lane, 8), swap_blocks(imag, lane, 8)
@@ -265,9 +274,7 @@
 SUMS = len(PAIRS) + len(OFF) + 2 * FILT
 
 
-def windows_kernel(weights, live, *refs):
-    *outs, held = refs
-    x = lax.axis_index("x")
+def windows_kernel(weights, live, here, across, held):
     alive = live[...].astype(f32)
     for n in range(ITERS):
         rows = []
@@ -276,18 +283,19 @@
             rows.append(weights[pl.ds(start, BINS, stride=FILT), :] * alive[i : i + 1])
         for w, block in enumerate(swap_blocks(rows, lanes_of(BINS), WX)):
             held[w, n] = block
-    for k, out in enumerate(outs):
-        out[...] = held[lax.rem(x + k, WINDOWS)]
-
-
-def halves_kernel(*refs):
-    *sources, keep, give = refs
-    x, own = lax.axis_index("x"), lax.axis_index("zh") * HALF
-    for k, source in enumerate(sources):
-        place = lax.rem(x + WINDOWS - k, WINDOWS)
-        for n in range(ITERS):
-            keep[place, n] = source[n, pl.ds(pl.multiple_of(own, HALF), HALF), :]
-            give[place, n] = source[n, pl.ds(pl.multiple_of(HALF - own, HALF), HALF), :]
+    xq = lax.axis_index("xq")
+    for w in range(2):
+        here[w] = held[2 * xq + w]
+        across[w] = held[2 - 2 * xq + w]
+
+
+def halves_kernel(here, across, keep, give):
+    own, xq = lax.axis_index("zh") * HALF, lax.axis_index("xq")
+    for source, place in ((here, xq), (across, 1 - xq)):
+        for w in range(2):
+            for n in range(ITERS):
+                keep[place, w, n] = source[w, n, pl.ds(pl.multiple_of(own, HALF), HALF), :]
+                give[place, w, n] = source[w, n, pl.ds(pl.multiple_of(HALF - own, HALF), HALF), :]
 
 
 def prepare_kernel(keep, got, spread, omega):
@@ -296,11 +304,11 @@
     over = (((0,), (0,)), ((), ()))
     for n in range(ITERS):
         for source, beta in ((keep, own), (got, 1 - own)):
-            for kappa in range(2):
-                rows = jnp.concatenate([source[2 * kappa + a, n] for a in range(2)], axis=0)
+            for w in range(2):
+                rows = jnp.concatenate([source[a, w, n] for a in range(2)], axis=0)
                 top = rows.astype(bf16)
                 rest = (rows - top.astype(f32)).astype(bf16)
-                omega[n, beta * 2 + kappa] = lax.dot_general(
+                omega[n, beta * 2 + w] = lax.dot_general(
                     top, table, over, preferred_element_type=f32
                 ) + lax.dot_general(rest, table, over, preferred_element_type=f32)
 
@@ -317,7 +325,7 @@
 
     def tile_of(row, w, flip):
         row = row % FILT
-        return (row + flip * (FILT - 1 - 2 * row)) * TWO + w
+        return w * FILT + row + flip * (FILT - 1 - 2 * row)
 
     def rows_of(job, w, lines):
         own, side, _, flip = jobs[job]
@@ -330,7 +338,7 @@
 
     def weight_of(job, i, w, sub):
         _, _, beta, flip = jobs[job]
-        start = tile_of(i, 0, flip) // TWO * ROWS + sub * 8
+        start = tile_of(i, 0, flip) * ROWS + sub * 8
         return omega[beta * TWO + w, pl.ds(pl.multiple_of(start, 8), 8), :]
 
     def gather(w, carry):
@@ -461,10 +469,10 @@
 TRACES = (RADIX, WX, LANES)
 TWO = 2
 ROWS = WX
-TILES = (2 * FILT, TWO, ROWS, LANES)
+TILES = (2 * TWO * FILT, ROWS, LANES)
 EDGE = (TWO * FILT, ROWS, LANES)
-PART = (ITERS, BINS, LANES)
-HALVES = (WINDOWS, ITERS, HALF, LANES)
+PART = (2, ITERS, BINS, LANES)
+HALVES = (2, 2, ITERS, HALF, LANES)
 
 
 def send_call(traces):
@@ -484,8 +492,8 @@
 
 
 def windows_call(weights, live):
-    scratch = [pltpu.VMEM((WINDOWS,) + PART, f32)]
-    return kernel_call(windows_kernel, [PART] * WINDOWS, scratch, "windows")(weights, live)
+    scratch = [pltpu.VMEM((WINDOWS,) + PART[1:], f32)]
+    return kernel_call(windows_kernel, [PART, PART], scratch, "windows")(weights, live)
 
 
 def halves_call(*arrays):
@@ -540,13 +548,12 @@
     shift = [(2 * y + 1, 2 * y + 2) for y in range(ys - 1)] + [(2 * y + 2, 2 * y + 1) for y in range(ys - 1)]
     weights = reweights.reshape(ITERS * BINS * FILT, LANES)
     sent = send_call(traces_in)
-    shares = list(windows_call(weights, live_mask))
-    for k in range(1, WINDOWS):
-        shares[k] = lax.ppermute(shares[k], "x", [(i, (i + k) % WINDOWS) for i in range(WINDOWS)])
-    keep, give = halves_call(*shares)
+    here, across = windows_call(weights, live_mask)
+    across = lax.ppermute(across, ("xq", "xr"), [(i, WINDOWS - 1 - i) for i in range(WINDOWS)])
+    keep, give = halves_call(here, across)
     got = lax.ppermute(give, "zh", swap)
-    spectra = forward_call(exchange(sent, ("x", "zl")), live_mask, fh, fl, turns)
-    block = exchange(spectra, ("zh", "zl")).reshape((2,) + EDGE)
+    spectra = forward_call(exchange(sent, ("xq", "xr", "zl")), live_mask, fh, fl, turns)
+    block = exchange(spectra, ("zh", "xr", "zl")).reshape((2,) + EDGE)
     edge = pick_call(block)
     omegas = None
     for n in range(ITERS):
@@ -558,8 +565,8 @@
         part = beyond_call(n, edge, beyond, omegas)
         found = filter_call(n, part, block, partner, omegas)
         block, edge = found if n + 1 < ITERS else (found, None)
-    back = exchange(block.reshape(TILES), ("zh", "zl"))
-    return receive_call(exchange(inverse_call(back, ih, il, turns), ("x", "zl")))
+    back = exchange(block.reshape(TILES), ("zh", "xr", "zl"))
+    return receive_call(exchange(inverse_call(back, ih, il, turns), ("xq", "xr", "zl")))
 
 
 def solution(mesh):
@@ -568,8 +575,8 @@
     def run(traces_in, reweights, live_mask):
         return local(tables, traces_in, reweights, live_mask)
 
-    inner = jax.sharding.Mesh(mesh.devices.reshape(-1, 2, 2, 4, 4), ("y", "zh", "c", "x", "zl"))
-    inline, freq = ("y", "zh", "c"), ("x", "zl")
+    inner = jax.sharding.Mesh(mesh.devices.reshape(-1, 2, 2, 2, 2, 4), ("y", "zh", "c", "xq", "xr", "zl"))
+    inline, freq = ("y", "zh", "c"), ("xq", "xr", "zl")
     in_specs = (P(freq, inline, None), P(None, freq, inline, None), P(inline, None))
     out_specs = P(freq, inline, None)
     return jax.shard_map(run, mesh=inner, in_specs=in_specs, out_specs=out_specs, check_vma=False)

time: 96.6 us -> 95.1 us (0.984)
  starting transfers between devices: 50.9 us -> 44.1 us
  waiting for transfers between devices: 6.15 us -> 9.44 us
  blocking collectives: 29.2 us -> 31.4 us
    ppermute x3 -> x1, starting transfers between devices: 11.8 us -> 5.05 us  [local(): lax.ppermute(across, ('xq', 'xr'), [(i, WINDOWS - 1 - i) for i in range(W...]
    all_to_all x2, waiting for transfers between devices: 5.49 us -> 8.76 us  [exchange(): return lax.all_to_all(blocks, axes, 0, 0, tiled=True)]
    all_to_all x2, blocking collectives: 29.2 us -> 31.4 us  [exchange(): return lax.all_to_all(blocks, axes, 0, 0, tiled=True)]
  transfers between devices with their start and end apart: 10 -> 8, of which waited for: 3 -> 4; matrix products, arithmetic and copies ran while one was open for 0% -> 0% of each run, Pallas kernels for 4% -> 4%
where the time goes in v7:
time: 95.1 us; the launch traced here: 94.6 us
  starting transfers between devices  44.1 us (46%)
  blocking collectives  31.4 us (33%)
  waiting for transfers between devices  9.44 us (10%)
  Pallas kernels  8.41 us (9%)
  local copies, waits for them, and re-layouts  0.99 us (1%)
    all_to_all x2, blocking collectives, exchange(): return lax.all_to_all(blocks, axes, 0, 0, tiled=True)  31.4 us
    all_to_all x2, starting transfers between devices, exchange(): return lax.all_to_all(blocks, axes, 0, 0, tiled=True)  17.7 us
    ppermute x2, starting transfers between devices, local(): partner = lax.ppermute(block, 'c', swap)  9.85 us
    all_to_all x2, waiting for transfers between devices, exchange(): return lax.all_to_all(blocks, axes, 0, 0, tiled=True)  8.76 us
    ppermute x1, starting transfers between devices, local(): got = lax.ppermute(give, 'zh', swap)  7.74 us
    ppermute x1, starting transfers between devices, local(): lax.ppermute(across, ('xq', 'xr'), [(i, WINDOWS - 1 - i) for i in range(W...  5.05 us
    ppermute x2, starting transfers between devices, local(): beyond = lax.ppermute(edge, ('y', 'c'), shift)  3.84 us
    pallas_call x2, Pallas kernels, filter_call(): kernel_call(body, shapes, filter_scratch(4, 3), name='filter')  2.77 us
  transfers between devices with their start and end apart: 8, of which 4 were waited for; matrix products, arithmetic and copies ran while one was open for 0% of the time, Pallas kernels for 4%

profile of v7, /device:TPU:24, one launch (start us, length us, event | category | flops | bytes accessed | tf_op | source)
XLA Modules:
  0.0 94.6 jit_solution(13703533382054468555)
XLA Ops:
  0.0 0.0 copy-start
  0.0 0.9 %copy-done = f32[128,4,128]{2,1,0:T(4,128)S(1)} copy-done((f32[128,4,128]{2,1,0:T(4,128)S(1)}, f32[128,4,128]{2,1,0:T(4,128)}, u32[]{:S(2)}) %copy-start) | copy-done | bytes 262168
  1.0 0.0 copy-start.8
  1.0 0.0 copy-start.6
  1.0 0.8 send.1
  1.8 0.0 copy-start.1
  1.8 0.0 copy-start.5
  1.8 10.0 %all-to-all-start = ((f32[16,32,128]{2,1,0:T(8,128)}), f32[16,32,128]{2,1,0:T(8,128)S(1)}, u32[]{:S(2)}, u32[]{:S(2)}) async-start(f32[16,32,128]{2,1,0:T(8,128)} %send.1), calls=%async_computation | async-start | bytes 524288 | tf_op jit(solution)/shard_map/all_to_all | solution.py:544
  11.8 0.0 copy-start.4
  11.8 0.0 copy-done.8
  11.8 0.0 copy-done.1
  11.8 0.3 windows.1
  12.1 5.0 %collective-permute-start.1 = (f32[2,2,64,128]{3,2,1,0:T(8,128)S(1)}, f32[2,2,64,128]{3,2,1,0:T(8,128)S(1)}, u32[]{:S(2)}, u32[]{:S(2)}) collective-permute-start(f32[2,2,64,128]{3,2,1,0:T(8,128)S(1)} %get-tuple-element.14), channel_id=1, source_target_pairs={{0,12},{4,8},{8,4},{12,0},{1,13},{5,9},{9,5},{13,1},{2,14},{6,10},... | collective-permute-start | bytes 393224 | tf_op jit(solution)/shard_map/ppermute | solution.py:552
  17.2 5.5 %all-to-all-done.blocks = f32[16,32,128]{2,1,0:T(8,128)S(1)} async-done(((f32[16,32,128]{2,1,0:T(8,128)}), f32[16,32,128]{2,1,0:T(8,128)S(1)}, u32[]{:S(2)}, u32[]{:S(2)}) %all-to-all-start) | async-done | bytes 262176 | tf_op jit(solution)/shard_map/all_to_all | solution.py:544
  22.6 0.0 copy-done.6
  22.7 0.0 copy-done.5
  22.7 0.0 copy-done.4
  22.7 1.4 %forward.1 = f32[16,32,128]{2,1,0:T(8,128)} custom-call(f32[16,32,128]{2,1,0:T(8,128)S(1)} %all-to-all-done.blocks, s32[4,128]{1,0:T(4,128)S(1)} %copy-done.8, bf16[2,256,256]{2,1,0:T(8,128)(2,1)S(1)} %copy-done.5, bf16[2,256,256]{2,1,0:T(8,128)(2,1)S(1)} %copy-done.4, f32[2,8,128]{2,1,0:T(8,128)S(1)} %copy-done.6), custom_call_target="tpu_custom_call" | custom-call | tf_op jit(solution)/shard_map/forward/pallas_call | solution.py:484
  24.1 7.7 %all-to-all-start.1 = ((f32[16,32,128]{2,1,0:T(8,128)}), f32[16,32,128]{2,1,0:T(8,128)S(1)}, u32[]{:S(2)}, u32[]{:S(2)}) async-start(f32[16,32,128]{2,1,0:T(8,128)} %forward.1), calls=%async_computation.1 | async-start | bytes 524288 | tf_op jit(solution)/shard_map/all_to_all | solution.py:544
  31.8 0.0 collective-permute-done.1.across
  31.8 7.7 %collective-permute-start.2 = (f32[2,2,2,32,128]{4,3,2,1,0:T(8,128)S(1)}, f32[2,2,2,32,128]{4,3,2,1,0:T(8,128)S(1)}, u32[]{:S(2)}, u32[]{:S(2)}) collective-permute-start(f32[2,2,2,32,128]{4,3,2,1,0:T(8,128)S(1)} %get-tuple-element.15), channel_id=1, source_target_pairs={{0,32},{32,0},{1,33},{33,1},{2,34},{34,2},{3,35},{35,3},{4,36},{36... | collective-permute-start | bytes 393224 | tf_op jit(solution)/shard_map/ppermute | solution.py:554
  39.6 3.3 %all-to-all-done.1 = f32[16,32,128]{2,1,0:T(8,128)S(1)} async-done(((f32[16,32,128]{2,1,0:T(8,128)}), f32[16,32,128]{2,1,0:T(8,128)S(1)}, u32[]{:S(2)}, u32[]{:S(2)}) %all-to-all-start.1) | async-done | bytes 262176 | tf_op jit(solution)/shard_map/all_to_all | solution.py:544
  42.9 0.0 copy-start.7
  42.9 1.9 %collective-permute-start = (f32[8,32,128]{2,1,0:T(8,128)S(1)}, f32[8,32,128]{2,1,0:T(8,128)S(1)}, u32[]{:S(2)}, u32[]{:S(2)}) collective-permute-start(f32[8,32,128]{2,1,0:T(8,128)S(1)} %pick.1.edge), channel_id=1, source_target_pairs={{16,64},{80,128},{144,192},{208,256},{272,320},{336,384},{400,448}... | collective-permute-start | bytes 393224 | tf_op jit(solution)/shard_map/ppermute | solution.py:560
  44.8 4.8 %collective-permute-start.3 = (f32[2,8,32,128]{3,2,1,0:T(8,128)S(1)}, f32[2,8,32,128]{3,2,1,0:T(8,128)S(1)}, u32[]{:S(2)}, u32[]{:S(2)}) collective-permute-start(f32[2,8,32,128]{3,2,1,0:T(8,128)S(1)} %bitcast.6), channel_id=1, source_target_pairs={{0,16},{16,0},{1,17},{17,1},{2,18},{18,2},{3,19},{19,3},{4,20},{20... | collective-permute-start | bytes 786440 | tf_op jit(solution)/shard_map/ppermute | solution.py:561
  49.6 0.0 collective-permute-done.2.got
  49.6 0.0 copy-done.7
  49.6 0.3 prepare.1.omegas
  50.0 0.0 collective-permute-done.beyond
  50.0 0.6 beyond.2.part
  50.6 0.2 collective-permute-done.3.partner
  50.8 1.4 %filter.2 = (f32[2,8,32,128]{3,2,1,0:T(8,128)S(1)}, f32[8,32,128]{2,1,0:T(8,128)S(1)}) custom-call(f32[8,32,128]{2,1,0:T(8,128)S(1)} %beyond.2.part, f32[2,8,32,128]{3,2,1,0:T(8,128)S(1)} %bitcast.7, f32[2,8,32,128]{3,2,1,0:T(8,128)S(1)} %collective-permute-done.3.partner, f32[2,4,128,128]{3,2,1,0:T(8,128)S(1)} %prepare.1.omegas), custom_call_target="tpu_custom_call" | custom-call | tf_op jit(solution)/shard_map/filter/pallas_call | solution.py:530
  52.1 1.9 %collective-permute-start.4 = (f32[8,32,128]{2,1,0:T(8,128)S(1)}, f32[8,32,128]{2,1,0:T(8,128)S(1)}, u32[]{:S(2)}, u32[]{:S(2)}) collective-permute-start(f32[8,32,128]{2,1,0:T(8,128)S(1)} %get-tuple-element.19.edge), channel_id=1, source_target_pairs={{16,64},{80,128},{144,192},{208,256},{272,320},{336,384},{400,448}... | collective-permute-start | bytes 393224 | tf_op jit(solution)/shard_map/ppermute | solution.py:560
  54.1 5.1 %collective-permute-start.5 = (f32[2,8,32,128]{3,2,1,0:T(8,128)S(1)}, f32[2,8,32,128]{3,2,1,0:T(8,128)S(1)}, u32[]{:S(2)}, u32[]{:S(2)}) collective-permute-start(f32[2,8,32,128]{3,2,1,0:T(8,128)S(1)} %get-tuple-element.20.own), channel_id=1, source_target_pairs={{0,16},{16,0},{1,17},{17,1},{2,18},{18,2},{3,19},{19,3},{4,20},{20... | collective-permute-start | bytes 786440 | tf_op jit(solution)/shard_map/ppermute | solution.py:561
  59.1 0.0 collective-permute-done.4.beyond
  59.1 0.6 beyond.3.part
  59.8 0.5 collective-permute-done.5.partner
  60.3 1.4 %filter.3 = f32[2,8,32,128]{3,2,1,0:T(8,128)S(1)} custom-call(f32[8,32,128]{2,1,0:T(8,128)S(1)} %beyond.3.part, f32[2,8,32,128]{3,2,1,0:T(8,128)S(1)} %get-tuple-element.20.own, f32[2,8,32,128]{3,2,1,0:T(8,128)S(1)} %collective-permute-done.5.partner, f32[2,4,128,128]{3,2,1,0:T(8,128)S(1)} %prepare.1.omegas), custom_call_target="tpu_custom_call" | custom-call | tf_op jit(solution)/shard_map/filter/pallas_call | solution.py:530
  61.7 0.0 copy-start.2
  61.7 0.0 copy-start.3
  61.7 16.2 %all_to_all.20.blocks = f32[16,32,128]{2,1,0:T(8,128)S(1)} all-to-all(f32[16,32,128]{2,1,0:T(8,128)S(1)} %bitcast.8), channel_id=1, replica_groups=mesh['y'=8,'zh'=2,'c'=2,'xq'=2,'xr'=2,'zl'=4] {'zh','xr','zl'}, dimensions={0} | all-to-all | bytes 524288 | tf_op jit(solution)/shard_map/all_to_all | solution.py:544
  77.8 0.0 copy-done.2
  77.8 0.0 copy-done.3
  77.8 0.7 inverse.1
  78.5 15.2 %all_to_all.21.blocks = f32[16,32,128]{2,1,0:T(8,128)S(1)} all-to-all(f32[16,32,128]{2,1,0:T(8,128)S(1)} %inverse.1), channel_id=1, replica_groups=mesh['y'=8,'zh'=2,'c'=2,'xq'=2,'xr'=2,'zl'=4] {'xq','xr','zl'}, dimensions={0} | all-to-all | bytes 524288 | tf_op jit(solution)/shard_map/all_to_all | solution.py:544
  93.7 0.8 receive.1
  (2 shorter events, 0.0 us)
Async XLA Ops:
  0.0 0.9 %copy-start = (f32[128,4,128]{2,1,0:T(4,128)S(1)}, f32[128,4,128]{2,1,0:T(4,128)}, u32[]{:S(2)}) copy-start(f32[128,4,128]{2,1,0:T(4,128)} %param.9) | copy-start | bytes 786436
  1.0 10.8 %copy-start.8 = (s32[4,128]{1,0:T(4,128)S(1)}, s32[4,128]{1,0:T(4,128)}, u32[]{:S(2)}) copy-start(s32[4,128]{1,0:T(4,128)} %live.3) | copy-start | bytes 6148
  1.0 21.7 %copy-start.6 = (f32[2,8,128]{2,1,0:T(8,128)S(1)}, f32[2,8,128]{2,1,0:T(8,128)}, u32[]{:S(2)}) copy-start(f32[2,8,128]{2,1,0:T(8,128)} %constant.17.clone.turns) | copy-start | bytes 24580
  1.8 10.0 %copy-start.1 = (f32[2,64,4,128]{3,2,1,0:T(4,128)S(1)}, f32[2,64,4,128]{3,2,1,0:T(4,128)}, u32[]{:S(2)}) copy-start(f32[2,64,4,128]{3,2,1,0:T(4,128)} %param.10) | copy-start | bytes 786436
  1.8 20.9 %copy-start.5 = (bf16[2,256,256]{2,1,0:T(8,128)(2,1)S(1)}, bf16[2,256,256]{2,1,0:T(8,128)(2,1)}, u32[]{:S(2)}) copy-start(bf16[2,256,256]{2,1,0:T(8,128)(2,1)} %constant.12.clone.high) | copy-start | bytes 786436
  1.8 20.9 %all-to-all-start = ((f32[16,32,128]{2,1,0:T(8,128)}), f32[16,32,128]{2,1,0:T(8,128)S(1)}, u32[]{:S(2)}, u32[]{:S(2)}) async-start(f32[16,32,128]{2,1,0:T(8,128)} %send.1), calls=%async_computation | async-start | bytes 524288 | tf_op jit(solution)/shard_map/all_to_all | solution.py:544
  11.8 10.9 %copy-start.4 = (bf16[2,256,256]{2,1,0:T(8,128)(2,1)S(1)}, bf16[2,256,256]{2,1,0:T(8,128)(2,1)}, u32[]{:S(2)}) copy-start(bf16[2,256,256]{2,1,0:T(8,128)(2,1)} %constant.13.clone.low) | copy-start | bytes 786436
  12.1 19.7 %collective-permute-start.1 = (f32[2,2,64,128]{3,2,1,0:T(8,128)S(1)}, f32[2,2,64,128]{3,2,1,0:T(8,128)S(1)}, u32[]{:S(2)}, u32[]{:S(2)}) collective-permute-start(f32[2,2,64,128]{3,2,1,0:T(8,128)S(1)} %get-tuple-element.14), channel_id=1, source_target_pairs={{0,12},{4,8},{8,4},{12,0},{1,13},{5,9},{9,5},{13,1},{2,14},{6,10},... | collective-permute-start | bytes 393224 | tf_op jit(solution)/shard_map/ppermute | solution.py:552
  24.1 18.8 %all-to-all-start.1 = ((f32[16,32,128]{2,1,0:T(8,128)}), f32[16,32,128]{2,1,0:T(8,128)S(1)}, u32[]{:S(2)}, u32[]{:S(2)}) async-start(f32[16,32,128]{2,1,0:T(8,128)} %forward.1), calls=%async_computation.1 | async-start | bytes 524288 | tf_op jit(solution)/shard_map/all_to_all | solution.py:544
  31.8 17.8 %collective-permute-start.2 = (f32[2,2,2,32,128]{4,3,2,1,0:T(8,128)S(1)}, f32[2,2,2,32,128]{4,3,2,1,0:T(8,128)S(1)}, u32[]{:S(2)}, u32[]{:S(2)}) collective-permute-start(f32[2,2,2,32,128]{4,3,2,1,0:T(8,128)S(1)} %get-tuple-element.15), channel_id=1, source_target_pairs={{0,32},{32,0},{1,33},{33,1},{2,34},{34,2},{3,35},{35,3},{4,36},{36... | collective-permute-start | bytes 393224 | tf_op jit(solution)/shard_map/ppermute | solution.py:554
  42.9 6.8 %copy-start.7 = (bf16[64,128]{1,0:T(8,128)(2,1)S(1)}, bf16[64,128]{1,0:T(8,128)(2,1)}, u32[]{:S(2)}) copy-start(bf16[64,128]{1,0:T(8,128)(2,1)} %constant.16.clone.spread) | copy-start | bytes 49156
  42.9 7.1 %collective-permute-start = (f32[8,32,128]{2,1,0:T(8,128)S(1)}, f32[8,32,128]{2,1,0:T(8,128)S(1)}, u32[]{:S(2)}, u32[]{:S(2)}) collective-permute-start(f32[8,32,128]{2,1,0:T(8,128)S(1)} %pick.1.edge), channel_id=1, source_target_pairs={{16,64},{80,128},{144,192},{208,256},{272,320},{336,384},{400,448}... | collective-permute-start | bytes 393224 | tf_op jit(solution)/shard_map/ppermute | solution.py:560
  44.8 5.9 %collective-permute-start.3 = (f32[2,8,32,128]{3,2,1,0:T(8,128)S(1)}, f32[2,8,32,128]{3,2,1,0:T(8,128)S(1)}, u32[]{:S(2)}, u32[]{:S(2)}) collective-permute-start(f32[2,8,32,128]{3,2,1,0:T(8,128)S(1)} %bitcast.6), channel_id=1, source_target_pairs={{0,16},{16,0},{1,17},{17,1},{2,18},{18,2},{3,19},{19,3},{4,20},{20... | collective-permute-start | bytes 786440 | tf_op jit(solution)/shard_map/ppermute | solution.py:561
  52.1 7.0 %collective-permute-start.4 = (f32[8,32,128]{2,1,0:T(8,128)S(1)}, f32[8,32,128]{2,1,0:T(8,128)S(1)}, u32[]{:S(2)}, u32[]{:S(2)}) collective-permute-start(f32[8,32,128]{2,1,0:T(8,128)S(1)} %get-tuple-element.19.edge), channel_id=1, source_target_pairs={{16,64},{80,128},{144,192},{208,256},{272,320},{336,384},{400,448}... | collective-permute-start | bytes 393224 | tf_op jit(solution)/shard_map/ppermute | solution.py:560
  54.1 6.2 %collective-permute-start.5 = (f32[2,8,32,128]{3,2,1,0:T(8,128)S(1)}, f32[2,8,32,128]{3,2,1,0:T(8,128)S(1)}, u32[]{:S(2)}, u32[]{:S(2)}) collective-permute-start(f32[2,8,32,128]{3,2,1,0:T(8,128)S(1)} %get-tuple-element.20.own), channel_id=1, source_target_pairs={{0,16},{16,0},{1,17},{17,1},{2,18},{18,2},{3,19},{19,3},{4,20},{20... | collective-permute-start | bytes 786440 | tf_op jit(solution)/shard_map/ppermute | solution.py:561
  61.7 16.2 %copy-start.2 = (bf16[2,256,256]{2,1,0:T(8,128)(2,1)S(1)}, bf16[2,256,256]{2,1,0:T(8,128)(2,1)}, u32[]{:S(2)}) copy-start(bf16[2,256,256]{2,1,0:T(8,128)(2,1)} %constant.15.clone.low) | copy-start | bytes 786436
  61.7 16.2 %copy-start.3 = (bf16[2,256,256]{2,1,0:T(8,128)(2,1)S(1)}, bf16[2,256,256]{2,1,0:T(8,128)(2,1)}, u32[]{:S(2)}) copy-start(bf16[2,256,256]{2,1,0:T(8,128)(2,1)} %constant.14.clone.high) | copy-start | bytes 786436

commit v8 on v7

--- a/solution.py
+++ b/solution.py
@@ -31,6 +31,11 @@
 SETS = ((0, 3), (1, 2))
 
 
+def held_bins(zh, zl):
+    z = 4 * zh + zl
+    return (0, z - 2) if 2 <= z <= 5 else (1, (z + 2) % 8)
+
+
 def split_table(table):
     high = table.astype(np.float32).astype(bf16)
     low = (table - high.astype(np.float64)).astype(np.float32).astype(bf16)
@@ -43,9 +48,9 @@
     r = np.arange(SPAN)
     for spot in range(2 * 8):
         kappa, part = divmod(spot, 8)
-        zh, zl = divmod(part, 4)
+        half, source = held_bins(*divmod(part, 4))
         for place, (a, s, b) in enumerate(INNER):
-            base = BINS * (4 * SETS[kappa][a] + zl) + HALF * zh + 16 * b
+            base = BINS * (4 * SETS[kappa][a] + source) + HALF * half + 16 * b
             col = spot * 8 + place
             f = base + 8 * s
             angle = 2.0 * np.pi * ((f * r) % NT) / NT
@@ -289,21 +294,22 @@
         across[w] = held[2 - 2 * xq + w]
 
 
-def halves_kernel(here, across, keep, give):
+def halves_kernel(here, across, plus, minus):
     own, xq = lax.axis_index("zh") * HALF, lax.axis_index("xq")
     for source, place in ((here, xq), (across, 1 - xq)):
         for w in range(2):
             for n in range(ITERS):
-                keep[place, w, n] = source[w, n, pl.ds(pl.multiple_of(own, HALF), HALF), :]
-                give[place, w, n] = source[w, n, pl.ds(pl.multiple_of(HALF - own, HALF), HALF), :]
-
-
-def prepare_kernel(keep, got, spread, omega):
-    own = lax.axis_index("zh")
+                plus[place, w, n] = source[w, n, pl.ds(pl.multiple_of(own, HALF), HALF), :]
+                minus[place, w, n] = source[w, n, pl.ds(pl.multiple_of(HALF - own, HALF), HALF), :]
+
+
+def prepare_kernel(plus, minus, spread, omega):
+    z = 4 * lax.axis_index("zh") + lax.axis_index("zl")
+    beta_plus = jnp.where((z >= 2) & (z <= 5), 0, 1)
     table = spread[...]
     over = (((0,), (0,)), ((), ()))
     for n in range(ITERS):
-        for source, beta in ((keep, own), (got, 1 - own)):
+        for source, beta in ((plus, beta_plus), (minus, 1 - beta_plus)):
             for w in range(2):
                 rows = jnp.concatenate([source[a, w, n] for a in range(2)], axis=0)
                 top = rows.astype(bf16)
@@ -315,14 +321,6 @@
 
 def predictions(jobs, omega, turned, sums, coefs, store):
     slots = TWO * len(jobs)
-    blocks = []
-    for own, side, _, _ in jobs:
-        blocks += [ref for ref in (own, side) if all(ref is not other for other in blocks)]
-    for place, ref in enumerate(blocks):
-        for k in range(TWO * FILT):
-            turned[place, k] = pltpu.roll(ref[k], BINS, 1)
-    places = [[next(p for p, other in enumerate(blocks) if other is ref) for ref in job[:2]] for job in jobs]
-
     def tile_of(row, w, flip):
         row = row % FILT
         return w * FILT + row + flip * (FILT - 1 - 2 * row)
@@ -333,7 +331,7 @@
         for row in range(2 * FILT):
             which, tile = row // FILT, tile_of(row, w, flip)
             plain.append((own, side)[which][tile, lines, :])
-            quarter.append(turned[places[job][which], tile, lines, :])
+            quarter.append(pltpu.roll(plain[-1], BINS, 1))
         return plain, quarter
 
     def weight_of(job, i, w, sub):
@@ -364,12 +362,13 @@
                         add(place, weighted[k] * rows[i])
                         add(place + 1, weighted[k] * turns[i])
                         place += 2
-            start = pl.multiple_of((job * TWO + w) * 8, 8)
+            start = (job * TWO + w) * 8
             for place in range(SUMS):
                 sums[place, pl.ds(start, 8), :] = acc[place]
         return carry
 
-    lax.fori_loop(0, TWO, gather, 0)
+    for w in range(TWO):
+        gather(w, 0)
 
     sign = jnp.where(lanes_of(slots) < BINS, 1.0, -1.0).astype(f32)
 
@@ -414,7 +413,8 @@
                     store(job, tile_of(i, w, jobs[job][3]), lines, acc[i], weight_of(job, i, w, sub))
         return carry
 
-    lax.fori_loop(0, TWO, predict, 0)
+    for w in range(TWO):
+        predict(w, 0)
 
 
 def pick_kernel(block, out):
@@ -550,8 +550,9 @@
     sent = send_call(traces_in)
     here, across = windows_call(weights, live_mask)
     across = lax.ppermute(across, ("xq", "xr"), [(i, WINDOWS - 1 - i) for i in range(WINDOWS)])
-    keep, give = halves_call(here, across)
-    got = lax.ppermute(give, "zh", swap)
+    plus, minus = halves_call(here, across)
+    plus = lax.ppermute(plus, ("zh", "zl"), [(z, (z + 2) % 8) for z in range(8)])
+    minus = lax.ppermute(minus, ("zh", "zl"), [(z, (z - 2) % 8) for z in range(8)])
     spectra = forward_call(exchange(sent, ("xq", "xr", "zl")), live_mask, fh, fl, turns)
     block = exchange(spectra, ("zh", "xr", "zl")).reshape((2,) + EDGE)
     edge = pick_call(block)
@@ -560,8 +561,8 @@
         beyond = lax.ppermute(edge, ("y", "c"), shift)
         partner = lax.ppermute(block, "c", swap)
         if omegas is None:
-            edge, got = lax.optimization_barrier((edge, got))
-            omegas = prepare_call(keep, got, spread)
+            edge, plus, minus = lax.optimization_barrier((edge, plus, minus))
+            omegas = prepare_call(plus, minus, spread)
         part = beyond_call(n, edge, beyond, omegas)
         found = filter_call(n, part, block, partner, omegas)
         block, edge = found if n + 1 < ITERS else (found, None)

time: 95.1 us -> 94.4 us (level)
    ppermute x1 -> x2, starting transfers between devices: 7.74 us -> 7.95 us  [the longest x1 4.73 us: local(): lax.ppermute(plus, ('zh', 'zl'), [(z, (z + 2) % 8) for z in range(8)])]
  transfers between devices with their start and end apart: 8 -> 9, of which waited for: 4 -> 4; matrix products, arithmetic and copies ran while one was open for 0% -> 0% of each run, Pallas kernels for 4% -> 3%
where the time goes in v8:
time: 94.4 us; the launch traced here: 93.8 us
  starting transfers between devices  44.2 us (47%)
  blocking collectives  31 us (33%)
  waiting for transfers between devices  9.62 us (10%)
  Pallas kernels  7.73 us (8%)
  local copies, waits for them, and re-layouts  0.99 us (1%)
    all_to_all x2, blocking collectives, exchange(): return lax.all_to_all(blocks, axes, 0, 0, tiled=True)  31 us
    all_to_all x2, starting transfers between devices, exchange(): return lax.all_to_all(blocks, axes, 0, 0, tiled=True)  17.7 us
    ppermute x2, starting transfers between devices, local(): partner = lax.ppermute(block, 'c', swap)  9.7 us
    all_to_all x2, waiting for transfers between devices, exchange(): return lax.all_to_all(blocks, axes, 0, 0, tiled=True)  8.65 us
    ppermute x1, starting transfers between devices, local(): lax.ppermute(across, ('xq', 'xr'), [(i, WINDOWS - 1 - i) for i in range(W...  5.05 us
    ppermute x1, starting transfers between devices, local(): lax.ppermute(plus, ('zh', 'zl'), [(z, (z + 2) % 8) for z in range(8)])  4.73 us
    ppermute x2, starting transfers between devices, local(): beyond = lax.ppermute(edge, ('y', 'c'), shift)  3.84 us
    ppermute x1, starting transfers between devices, local(): lax.ppermute(minus, ('zh', 'zl'), [(z, (z - 2) % 8) for z in range(8)])  3.22 us
  transfers between devices with their start and end apart: 9, of which 4 were waited for; matrix products, arithmetic and copies ran while one was open for 0% of the time, Pallas kernels for 3%

profile of v8, /device:TPU:24, one launch (start us, length us, event | category | flops | bytes accessed | tf_op | source)
XLA Modules:
  0.0 93.8 jit_solution(17305093586966783240)
XLA Ops:
  0.0 0.0 copy-start
  0.0 0.9 %copy-done = f32[128,4,128]{2,1,0:T(4,128)S(1)} copy-done((f32[128,4,128]{2,1,0:T(4,128)S(1)}, f32[128,4,128]{2,1,0:T(4,128)}, u32[]{:S(2)}) %copy-start) | copy-done | bytes 262168
  1.0 0.0 copy-start.8
  1.0 0.0 copy-start.6
  1.0 0.8 send.1
  1.8 0.0 copy-start.1
  1.8 0.0 copy-start.5
  1.8 10.0 %all-to-all-start = ((f32[16,32,128]{2,1,0:T(8,128)}), f32[16,32,128]{2,1,0:T(8,128)S(1)}, u32[]{:S(2)}, u32[]{:S(2)}) async-start(f32[16,32,128]{2,1,0:T(8,128)} %send.1), calls=%async_computation | async-start | bytes 524288 | tf_op jit(solution)/shard_map/all_to_all | solution.py:544
  11.8 0.0 copy-start.4
  11.8 0.0 copy-done.8
  11.8 0.0 copy-done.1
  11.8 0.3 windows.1
  12.1 5.0 %collective-permute-start.1 = (f32[2,2,64,128]{3,2,1,0:T(8,128)S(1)}, f32[2,2,64,128]{3,2,1,0:T(8,128)S(1)}, u32[]{:S(2)}, u32[]{:S(2)}) collective-permute-start(f32[2,2,64,128]{3,2,1,0:T(8,128)S(1)} %get-tuple-element.15), channel_id=1, source_target_pairs={{0,12},{4,8},{8,4},{12,0},{1,13},{5,9},{9,5},{13,1},{2,14},{6,10},... | collective-permute-start | bytes 393224 | tf_op jit(solution)/shard_map/ppermute | solution.py:552
  17.2 5.5 %all-to-all-done.blocks = f32[16,32,128]{2,1,0:T(8,128)S(1)} async-done(((f32[16,32,128]{2,1,0:T(8,128)}), f32[16,32,128]{2,1,0:T(8,128)S(1)}, u32[]{:S(2)}, u32[]{:S(2)}) %all-to-all-start) | async-done | bytes 262176 | tf_op jit(solution)/shard_map/all_to_all | solution.py:544
  22.6 0.0 copy-done.6
  22.7 0.0 copy-done.5
  22.7 0.0 copy-done.4
  22.7 1.4 %forward.1 = f32[16,32,128]{2,1,0:T(8,128)} custom-call(f32[16,32,128]{2,1,0:T(8,128)S(1)} %all-to-all-done.blocks, s32[4,128]{1,0:T(4,128)S(1)} %copy-done.8, bf16[2,256,256]{2,1,0:T(8,128)(2,1)S(1)} %copy-done.5, bf16[2,256,256]{2,1,0:T(8,128)(2,1)S(1)} %copy-done.4, f32[2,8,128]{2,1,0:T(8,128)S(1)} %copy-done.6), custom_call_target="tpu_custom_call" | custom-call | tf_op jit(solution)/shard_map/forward/pallas_call | solution.py:484
  24.1 7.7 %all-to-all-start.1 = ((f32[16,32,128]{2,1,0:T(8,128)}), f32[16,32,128]{2,1,0:T(8,128)S(1)}, u32[]{:S(2)}, u32[]{:S(2)}) async-start(f32[16,32,128]{2,1,0:T(8,128)} %forward.1), calls=%async_computation.1 | async-start | bytes 524288 | tf_op jit(solution)/shard_map/all_to_all | solution.py:544
  31.8 0.0 collective-permute-done.1.across
  31.8 4.7 %collective-permute-start.2 = (f32[2,2,2,32,128]{4,3,2,1,0:T(8,128)S(1)}, f32[2,2,2,32,128]{4,3,2,1,0:T(8,128)S(1)}, u32[]{:S(2)}, u32[]{:S(2)}) collective-permute-start(f32[2,2,2,32,128]{4,3,2,1,0:T(8,128)S(1)} %get-tuple-element.16), channel_id=1, source_target_pairs={{0,2},{1,3},{2,32},{3,33},{32,34},{33,35},{34,0},{35,1},{4,6},{5,7... | collective-permute-start | bytes 393224 | tf_op jit(solution)/shard_map/ppermute | solution.py:554
  36.6 3.2 %collective-permute-start.3 = (f32[2,2,2,32,128]{4,3,2,1,0:T(8,128)S(1)}, f32[2,2,2,32,128]{4,3,2,1,0:T(8,128)S(1)}, u32[]{:S(2)}, u32[]{:S(2)}) collective-permute-start(f32[2,2,2,32,128]{4,3,2,1,0:T(8,128)S(1)} %get-tuple-element.17), channel_id=1, source_target_pairs={{0,34},{1,35},{2,0},{3,1},{32,2},{33,3},{34,32},{35,33},{4,38},{5,... | collective-permute-start | bytes 393224 | tf_op jit(solution)/shard_map/ppermute | solution.py:555
  39.8 3.2 %all-to-all-done.1 = f32[16,32,128]{2,1,0:T(8,128)S(1)} async-done(((f32[16,32,128]{2,1,0:T(8,128)}), f32[16,32,128]{2,1,0:T(8,128)S(1)}, u32[]{:S(2)}, u32[]{:S(2)}) %all-to-all-start.1) | async-done | bytes 262176 | tf_op jit(solution)/shard_map/all_to_all | solution.py:544
  43.0 0.0 copy-start.7
  43.0 1.9 %collective-permute-start = (f32[8,32,128]{2,1,0:T(8,128)S(1)}, f32[8,32,128]{2,1,0:T(8,128)S(1)}, u32[]{:S(2)}, u32[]{:S(2)}) collective-permute-start(f32[8,32,128]{2,1,0:T(8,128)S(1)} %pick.1.edge), channel_id=1, source_target_pairs={{16,64},{80,128},{144,192},{208,256},{272,320},{336,384},{400,448}... | collective-permute-start | bytes 393224 | tf_op jit(solution)/shard_map/ppermute | solution.py:561
  44.9 4.8 %collective-permute-start.4 = (f32[2,8,32,128]{3,2,1,0:T(8,128)S(1)}, f32[2,8,32,128]{3,2,1,0:T(8,128)S(1)}, u32[]{:S(2)}, u32[]{:S(2)}) collective-permute-start(f32[2,8,32,128]{3,2,1,0:T(8,128)S(1)} %bitcast.6), channel_id=1, source_target_pairs={{0,16},{16,0},{1,17},{17,1},{2,18},{18,2},{3,19},{19,3},{4,20},{20... | collective-permute-start | bytes 786440 | tf_op jit(solution)/shard_map/ppermute | solution.py:562
  49.7 0.0 collective-permute-done.2.plus
  49.7 0.0 collective-permute-done.3.minus
  49.7 0.0 copy-done.7
  49.8 0.3 prepare.1.omegas
  50.1 0.0 collective-permute-done.beyond
  50.1 0.5 beyond.2.part
  50.6 0.3 collective-permute-done.4.partner
  50.9 1.1 %filter.2 = (f32[2,8,32,128]{3,2,1,0:T(8,128)S(1)}, f32[8,32,128]{2,1,0:T(8,128)S(1)}) custom-call(f32[8,32,128]{2,1,0:T(8,128)S(1)} %beyond.2.part, f32[2,8,32,128]{3,2,1,0:T(8,128)S(1)} %bitcast.7, f32[2,8,32,128]{3,2,1,0:T(8,128)S(1)} %collective-permute-done.4.partner, f32[2,4,128,128]{3,2,1,0:T(8,128)S(1)} %prepare.1.omegas), custom_call_target="tpu_custom_call" | custom-call | tf_op jit(solution)/shard_map/filter/pallas_call | solution.py:530
  52.0 1.9 %collective-permute-start.5 = (f32[8,32,128]{2,1,0:T(8,128)S(1)}, f32[8,32,128]{2,1,0:T(8,128)S(1)}, u32[]{:S(2)}, u32[]{:S(2)}) collective-permute-start(f32[8,32,128]{2,1,0:T(8,128)S(1)} %get-tuple-element.21.edge), channel_id=1, source_target_pairs={{16,64},{80,128},{144,192},{208,256},{272,320},{336,384},{400,448}... | collective-permute-start | bytes 393224 | tf_op jit(solution)/shard_map/ppermute | solution.py:561
  53.9 4.9 %collective-permute-start.6 = (f32[2,8,32,128]{3,2,1,0:T(8,128)S(1)}, f32[2,8,32,128]{3,2,1,0:T(8,128)S(1)}, u32[]{:S(2)}, u32[]{:S(2)}) collective-permute-start(f32[2,8,32,128]{3,2,1,0:T(8,128)S(1)} %get-tuple-element.22.own), channel_id=1, source_target_pairs={{0,16},{16,0},{1,17},{17,1},{2,18},{18,2},{3,19},{19,3},{4,20},{20... | collective-permute-start | bytes 786440 | tf_op jit(solution)/shard_map/ppermute | solution.py:562
  58.8 0.0 collective-permute-done.5.beyond
  58.9 0.5 beyond.3.part
  59.3 0.7 collective-permute-done.6.partner
  60.0 1.2 %filter.3 = f32[2,8,32,128]{3,2,1,0:T(8,128)S(1)} custom-call(f32[8,32,128]{2,1,0:T(8,128)S(1)} %beyond.3.part, f32[2,8,32,128]{3,2,1,0:T(8,128)S(1)} %get-tuple-element.22.own, f32[2,8,32,128]{3,2,1,0:T(8,128)S(1)} %collective-permute-done.6.partner, f32[2,4,128,128]{3,2,1,0:T(8,128)S(1)} %prepare.1.omegas), custom_call_target="tpu_custom_call" | custom-call | tf_op jit(solution)/shard_map/filter/pallas_call | solution.py:530
  61.2 0.0 copy-start.2
  61.2 0.0 copy-start.3
  61.3 15.8 %all_to_all.20.blocks = f32[16,32,128]{2,1,0:T(8,128)S(1)} all-to-all(f32[16,32,128]{2,1,0:T(8,128)S(1)} %bitcast.8), channel_id=1, replica_groups=mesh['y'=8,'zh'=2,'c'=2,'xq'=2,'xr'=2,'zl'=4] {'zh','xr','zl'}, dimensions={0} | all-to-all | bytes 524288 | tf_op jit(solution)/shard_map/all_to_all | solution.py:544
  77.1 0.0 copy-done.2
  77.1 0.0 copy-done.3
  77.1 0.6 inverse.1
  77.7 15.2 %all_to_all.21.blocks = f32[16,32,128]{2,1,0:T(8,128)S(1)} all-to-all(f32[16,32,128]{2,1,0:T(8,128)S(1)} %inverse.1), channel_id=1, replica_groups=mesh['y'=8,'zh'=2,'c'=2,'xq'=2,'xr'=2,'zl'=4] {'xq','xr','zl'}, dimensions={0} | all-to-all | bytes 524288 | tf_op jit(solution)/shard_map/all_to_all | solution.py:544
  92.9 0.8 receive.1
  (2 shorter events, 0.0 us)
Async XLA Ops:
  0.0 0.9 %copy-start = (f32[128,4,128]{2,1,0:T(4,128)S(1)}, f32[128,4,128]{2,1,0:T(4,128)}, u32[]{:S(2)}) copy-start(f32[128,4,128]{2,1,0:T(4,128)} %param.9) | copy-start | bytes 786436
  1.0 10.8 %copy-start.8 = (s32[4,128]{1,0:T(4,128)S(1)}, s32[4,128]{1,0:T(4,128)}, u32[]{:S(2)}) copy-start(s32[4,128]{1,0:T(4,128)} %live.3) | copy-start | bytes 6148
  1.0 21.7 %copy-start.6 = (f32[2,8,128]{2,1,0:T(8,128)S(1)}, f32[2,8,128]{2,1,0:T(8,128)}, u32[]{:S(2)}) copy-start(f32[2,8,128]{2,1,0:T(8,128)} %constant.17.clone.turns) | copy-start | bytes 24580
  1.8 10.0 %copy-start.1 = (f32[2,64,4,128]{3,2,1,0:T(4,128)S(1)}, f32[2,64,4,128]{3,2,1,0:T(4,128)}, u32[]{:S(2)}) copy-start(f32[2,64,4,128]{3,2,1,0:T(4,128)} %param.10) | copy-start | bytes 786436
  1.8 20.9 %copy-start.5 = (bf16[2,256,256]{2,1,0:T(8,128)(2,1)S(1)}, bf16[2,256,256]{2,1,0:T(8,128)(2,1)}, u32[]{:S(2)}) copy-start(bf16[2,256,256]{2,1,0:T(8,128)(2,1)} %constant.12.clone.high) | copy-start | bytes 786436
  1.8 20.9 %all-to-all-start = ((f32[16,32,128]{2,1,0:T(8,128)}), f32[16,32,128]{2,1,0:T(8,128)S(1)}, u32[]{:S(2)}, u32[]{:S(2)}) async-start(f32[16,32,128]{2,1,0:T(8,128)} %send.1), calls=%async_computation | async-start | bytes 524288 | tf_op jit(solution)/shard_map/all_to_all | solution.py:544
  11.8 10.9 %copy-start.4 = (bf16[2,256,256]{2,1,0:T(8,128)(2,1)S(1)}, bf16[2,256,256]{2,1,0:T(8,128)(2,1)}, u32[]{:S(2)}) copy-start(bf16[2,256,256]{2,1,0:T(8,128)(2,1)} %constant.13.clone.low) | copy-start | bytes 786436
  12.1 19.7 %collective-permute-start.1 = (f32[2,2,64,128]{3,2,1,0:T(8,128)S(1)}, f32[2,2,64,128]{3,2,1,0:T(8,128)S(1)}, u32[]{:S(2)}, u32[]{:S(2)}) collective-permute-start(f32[2,2,64,128]{3,2,1,0:T(8,128)S(1)} %get-tuple-element.15), channel_id=1, source_target_pairs={{0,12},{4,8},{8,4},{12,0},{1,13},{5,9},{9,5},{13,1},{2,14},{6,10},... | collective-permute-start | bytes 393224 | tf_op jit(solution)/shard_map/ppermute | solution.py:552
  24.1 18.9 %all-to-all-start.1 = ((f32[16,32,128]{2,1,0:T(8,128)}), f32[16,32,128]{2,1,0:T(8,128)S(1)}, u32[]{:S(2)}, u32[]{:S(2)}) async-start(f32[16,32,128]{2,1,0:T(8,128)} %forward.1), calls=%async_computation.1 | async-start | bytes 524288 | tf_op jit(solution)/shard_map/all_to_all | solution.py:544
  31.8 17.9 %collective-permute-start.2 = (f32[2,2,2,32,128]{4,3,2,1,0:T(8,128)S(1)}, f32[2,2,2,32,128]{4,3,2,1,0:T(8,128)S(1)}, u32[]{:S(2)}, u32[]{:S(2)}) collective-permute-start(f32[2,2,2,32,128]{4,3,2,1,0:T(8,128)S(1)} %get-tuple-element.16), channel_id=1, source_target_pairs={{0,2},{1,3},{2,32},{3,33},{32,34},{33,35},{34,0},{35,1},{4,6},{5,7... | collective-permute-start | bytes 393224 | tf_op jit(solution)/shard_map/ppermute | solution.py:554
  36.6 13.2 %collective-permute-start.3 = (f32[2,2,2,32,128]{4,3,2,1,0:T(8,128)S(1)}, f32[2,2,2,32,128]{4,3,2,1,0:T(8,128)S(1)}, u32[]{:S(2)}, u32[]{:S(2)}) collective-permute-start(f32[2,2,2,32,128]{4,3,2,1,0:T(8,128)S(1)} %get-tuple-element.17), channel_id=1, source_target_pairs={{0,34},{1,35},{2,0},{3,1},{32,2},{33,3},{34,32},{35,33},{4,38},{5,... | collective-permute-start | bytes 393224 | tf_op jit(solution)/shard_map/ppermute | solution.py:555
  43.0 6.8 %copy-start.7 = (bf16[64,128]{1,0:T(8,128)(2,1)S(1)}, bf16[64,128]{1,0:T(8,128)(2,1)}, u32[]{:S(2)}) copy-start(bf16[64,128]{1,0:T(8,128)(2,1)} %constant.16.clone.spread) | copy-start | bytes 49156
  43.0 7.1 %collective-permute-start = (f32[8,32,128]{2,1,0:T(8,128)S(1)}, f32[8,32,128]{2,1,0:T(8,128)S(1)}, u32[]{:S(2)}, u32[]{:S(2)}) collective-permute-start(f32[8,32,128]{2,1,0:T(8,128)S(1)} %pick.1.edge), channel_id=1, source_target_pairs={{16,64},{80,128},{144,192},{208,256},{272,320},{336,384},{400,448}... | collective-permute-start | bytes 393224 | tf_op jit(solution)/shard_map/ppermute | solution.py:561
  44.9 5.9 %collective-permute-start.4 = (f32[2,8,32,128]{3,2,1,0:T(8,128)S(1)}, f32[2,8,32,128]{3,2,1,0:T(8,128)S(1)}, u32[]{:S(2)}, u32[]{:S(2)}) collective-permute-start(f32[2,8,32,128]{3,2,1,0:T(8,128)S(1)} %bitcast.6), channel_id=1, source_target_pairs={{0,16},{16,0},{1,17},{17,1},{2,18},{18,2},{3,19},{19,3},{4,20},{20... | collective-permute-start | bytes 786440 | tf_op jit(solution)/shard_map/ppermute | solution.py:562
  52.0 6.8 %collective-permute-start.5 = (f32[8,32,128]{2,1,0:T(8,128)S(1)}, f32[8,32,128]{2,1,0:T(8,128)S(1)}, u32[]{:S(2)}, u32[]{:S(2)}) collective-permute-start(f32[8,32,128]{2,1,0:T(8,128)S(1)} %get-tuple-element.21.edge), channel_id=1, source_target_pairs={{16,64},{80,128},{144,192},{208,256},{272,320},{336,384},{400,448}... | collective-permute-start | bytes 393224 | tf_op jit(solution)/shard_map/ppermute | solution.py:561
  53.9 6.0 %collective-permute-start.6 = (f32[2,8,32,128]{3,2,1,0:T(8,128)S(1)}, f32[2,8,32,128]{3,2,1,0:T(8,128)S(1)}, u32[]{:S(2)}, u32[]{:S(2)}) collective-permute-start(f32[2,8,32,128]{3,2,1,0:T(8,128)S(1)} %get-tuple-element.22.own), channel_id=1, source_target_pairs={{0,16},{16,0},{1,17},{17,1},{2,18},{18,2},{3,19},{19,3},{4,20},{20... | collective-permute-start | bytes 786440 | tf_op jit(solution)/shard_map/ppermute | solution.py:562
  61.2 15.8 %copy-start.2 = (bf16[2,256,256]{2,1,0:T(8,128)(2,1)S(1)}, bf16[2,256,256]{2,1,0:T(8,128)(2,1)}, u32[]{:S(2)}) copy-start(bf16[2,256,256]{2,1,0:T(8,128)(2,1)} %constant.15.clone.low) | copy-start | bytes 786436
  61.2 15.8 %copy-start.3 = (bf16[2,256,256]{2,1,0:T(8,128)(2,1)S(1)}, bf16[2,256,256]{2,1,0:T(8,128)(2,1)}, u32[]{:S(2)}) copy-start(bf16[2,256,256]{2,1,0:T(8,128)(2,1)} %constant.14.clone.high) | copy-start | bytes 786436

commit v9 on v8

--- a/solution.py
+++ b/solution.py
@@ -430,28 +430,46 @@
     predictions([(edge, beyond, core, 1 - core)], omegas.at[n], turned, sums, coefs, store)
 
 
-def filter_kernel(n, part, own, partner, omegas, *refs):
-    *outs, turned, sums, coefs = refs
+def filter_kernel(part, own, partner, omegas, out, turned, sums, coefs):
     core = lax.axis_index("c")
-    rest_at, edge_at = (1 - core, core) if n == 0 else (0, 1)
-    rest, edge = own.at[rest_at], own.at[edge_at]
-    near, far = (partner.at[core], partner.at[1 - core]) if n == 0 else (partner.at[0], partner.at[1])
-    new_rest, new_edge = (outs[0].at[0], outs[0].at[1]) if n + 1 < ITERS else (outs[0].at[1 - core], outs[0].at[core])
+    rest, edge, near, far = own.at[0], own.at[1], partner.at[0], partner.at[1]
 
     def store(job, tile, lines, value, weight):
         half = jnp.where(weight > 0.0, 0.5, 0.0)
         if job == 0:
-            value = (value + part[tile, lines, :]) * half
-            new_edge[tile, lines, :] = value
-            if n + 1 < ITERS:
-                outs[1][tile, lines, :] = value
+            out[core, tile, lines, :] = (value + part[tile, lines, :]) * half
         elif job == 1:
-            new_rest[tile, lines, :] = value
+            out[1 - core, tile, lines, :] = value
         else:
-            new_rest[tile, lines, :] = (new_rest[tile, lines, :] + value) * half
+            out[1 - core, tile, lines, :] = (out[1 - core, tile, lines, :] + value) * half
 
     jobs = [(edge, near, core, core), (rest, near, 1 - core, 1 - core), (rest, far, 1 - core, core)]
-    predictions(jobs, omegas.at[n], turned, sums, coefs, store)
+    predictions(jobs, omegas.at[ITERS - 1], turned, sums, coefs, store)
+
+
+def near_kernel(part, own, partner, omegas, out, turned, sums, coefs):
+    core = lax.axis_index("c")
+
+    def store(job, tile, lines, value, weight):
+        out[tile, lines, :] = (value + part[tile, lines, :]) * jnp.where(weight > 0.0, 0.5, 0.0)
+
+    predictions([(own.at[core], partner.at[core], core, core)], omegas.at[0], turned, sums, coefs, store)
+
+
+def rest_kernel(edge, own, partner, omegas, out, turned, sums, coefs):
+    core = lax.axis_index("c")
+
+    def store(job, tile, lines, value, weight):
+        if job == 0:
+            out[0, tile, lines, :] = value
+        else:
+            out[0, tile, lines, :] = (out[0, tile, lines, :] + value) * jnp.where(weight > 0.0, 0.5, 0.0)
+
+    rest, near, far = own.at[1 - core], partner.at[core], partner.at[1 - core]
+    jobs = [(rest, near, 1 - core, 1 - core), (rest, far, 1 - core, core)]
+    predictions(jobs, omegas.at[0], turned, sums, coefs, store)
+    for k in range(TWO * FILT):
+        out[1, k] = edge[k]
 
 
 def kernel_call(body, shapes, scratch=(), name=None, cost=None):
@@ -523,11 +541,16 @@
     return kernel_call(body, [EDGE], filter_scratch(2, 1), "beyond", cost)(beyond, edge, omegas)
 
 
-def filter_call(n, part, own, partner, omegas):
-    both = (2,) + EDGE
-    shapes = [both, EDGE] if n + 1 < ITERS else [both]
-    body = functools.partial(filter_kernel, n)
-    return kernel_call(body, shapes, filter_scratch(4, 3), name="filter")(part, own, partner, omegas)
+def near_call(*arrays):
+    return kernel_call(near_kernel, [EDGE], filter_scratch(2, 1), "near")(*arrays)
+
+
+def rest_call(*arrays):
+    return kernel_call(rest_kernel, [(2,) + EDGE], filter_scratch(3, 2), "rest")(*arrays)
+
+
+def filter_call(*arrays):
+    return kernel_call(filter_kernel, [(2,) + EDGE], filter_scratch(4, 3), "filter")(*arrays)
 
 
 def receive_call(blocks):
@@ -564,8 +587,11 @@
             edge, plus, minus = lax.optimization_barrier((edge, plus, minus))
             omegas = prepare_call(plus, minus, spread)
         part = beyond_call(n, edge, beyond, omegas)
-        found = filter_call(n, part, block, partner, omegas)
-        block, edge = found if n + 1 < ITERS else (found, None)
+        if n + 1 < ITERS:
+            edge = near_call(part, block, partner, omegas)
+            block = rest_call(edge, block, partner, omegas)
+        else:
+            block = filter_call(part, block, partner, omegas)
     back = exchange(block.reshape(TILES), ("zh", "xr", "zl"))
     return receive_call(exchange(inverse_call(back, ih, il, turns), ("xq", "xr", "zl")))
 

time: 94.4 us -> 94.5 us (level)
    pallas_call x2 -> x3, Pallas kernels: 2.39 us -> 2.5 us  [the longest x1 1.24 us: filter_call(): kernel_call(filter_kernel, [(2,) + EDGE], filter_scratch(4, 3), 'filter')]
  transfers between devices with their start and end apart: 9 -> 9, of which waited for: 4 -> 4; matrix products, arithmetic and copies ran while one was open for 0% -> 0% of each run, Pallas kernels for 3% -> 4%
where the time goes in v9:
time: 94.5 us; the launch traced here: 93.9 us
  starting transfers between devices  44.2 us (47%)
  blocking collectives  31 us (33%)
  waiting for transfers between devices  9.62 us (10%)
  Pallas kernels  7.84 us (8%)
  local copies, waits for them, and re-layouts  0.99 us (1%)
    all_to_all x2, blocking collectives, exchange(): return lax.all_to_all(blocks, axes, 0, 0, tiled=True)  31 us
    all_to_all x2, starting transfers between devices, exchange(): return lax.all_to_all(blocks, axes, 0, 0, tiled=True)  17.7 us
    ppermute x2, starting transfers between devices, local(): partner = lax.ppermute(block, 'c', swap)  9.7 us
    all_to_all x2, waiting for transfers between devices, exchange(): return lax.all_to_all(blocks, axes, 0, 0, tiled=True)  8.65 us
    ppermute x1, starting transfers between devices, local(): lax.ppermute(across, ('xq', 'xr'), [(i, WINDOWS - 1 - i) for i in range(W...  5.05 us
    ppermute x1, starting transfers between devices, local(): lax.ppermute(plus, ('zh', 'zl'), [(z, (z + 2) % 8) for z in range(8)])  4.73 us
    ppermute x2, starting transfers between devices, local(): beyond = lax.ppermute(edge, ('y', 'c'), shift)  3.84 us
    ppermute x1, starting transfers between devices, local(): lax.ppermute(minus, ('zh', 'zl'), [(z, (z - 2) % 8) for z in range(8)])  3.22 us
  transfers between devices with their start and end apart: 9, of which 4 were waited for; matrix products, arithmetic and copies ran while one was open for 0% of the time, Pallas kernels for 4%

profile of v9, /device:TPU:24, one launch (start us, length us, event | category | flops | bytes accessed | tf_op | source)
XLA Modules:
  0.0 93.9 jit_solution(8169414019816169969)
XLA Ops:
  0.0 0.0 copy-start
  0.0 0.9 %copy-done = f32[128,4,128]{2,1,0:T(4,128)S(1)} copy-done((f32[128,4,128]{2,1,0:T(4,128)S(1)}, f32[128,4,128]{2,1,0:T(4,128)}, u32[]{:S(2)}) %copy-start) | copy-done | bytes 262168
  1.0 0.0 copy-start.8
  1.0 0.0 copy-start.6
  1.0 0.8 send.1
  1.8 0.0 copy-start.1
  1.8 0.0 copy-start.5
  1.8 10.0 %all-to-all-start = ((f32[16,32,128]{2,1,0:T(8,128)}), f32[16,32,128]{2,1,0:T(8,128)S(1)}, u32[]{:S(2)}, u32[]{:S(2)}) async-start(f32[16,32,128]{2,1,0:T(8,128)} %send.1), calls=%async_computation | async-start | bytes 524288 | tf_op jit(solution)/shard_map/all_to_all | solution.py:567
  11.8 0.0 copy-start.4
  11.8 0.0 copy-done.8
  11.8 0.0 copy-done.1
  11.8 0.3 windows.1
  12.1 5.0 %collective-permute-start.1 = (f32[2,2,64,128]{3,2,1,0:T(8,128)S(1)}, f32[2,2,64,128]{3,2,1,0:T(8,128)S(1)}, u32[]{:S(2)}, u32[]{:S(2)}) collective-permute-start(f32[2,2,64,128]{3,2,1,0:T(8,128)S(1)} %get-tuple-element.13), channel_id=1, source_target_pairs={{0,12},{4,8},{8,4},{12,0},{1,13},{5,9},{9,5},{13,1},{2,14},{6,10},... | collective-permute-start | bytes 393224 | tf_op jit(solution)/shard_map/ppermute | solution.py:575
  17.2 5.5 %all-to-all-done.blocks = f32[16,32,128]{2,1,0:T(8,128)S(1)} async-done(((f32[16,32,128]{2,1,0:T(8,128)}), f32[16,32,128]{2,1,0:T(8,128)S(1)}, u32[]{:S(2)}, u32[]{:S(2)}) %all-to-all-start) | async-done | bytes 262176 | tf_op jit(solution)/shard_map/all_to_all | solution.py:567
  22.6 0.0 copy-done.6
  22.7 0.0 copy-done.5
  22.7 0.0 copy-done.4
  22.7 1.4 %forward.1 = f32[16,32,128]{2,1,0:T(8,128)} custom-call(f32[16,32,128]{2,1,0:T(8,128)S(1)} %all-to-all-done.blocks, s32[4,128]{1,0:T(4,128)S(1)} %copy-done.8, bf16[2,256,256]{2,1,0:T(8,128)(2,1)S(1)} %copy-done.4, bf16[2,256,256]{2,1,0:T(8,128)(2,1)S(1)} %copy-done.5, f32[2,8,128]{2,1,0:T(8,128)S(1)} %copy-done.6), custom_call_target="tpu_custom_call" | custom-call | tf_op jit(solution)/shard_map/forward/pallas_call | solution.py:502
  24.1 7.7 %all-to-all-start.1 = ((f32[16,32,128]{2,1,0:T(8,128)}), f32[16,32,128]{2,1,0:T(8,128)S(1)}, u32[]{:S(2)}, u32[]{:S(2)}) async-start(f32[16,32,128]{2,1,0:T(8,128)} %forward.1), calls=%async_computation.1 | async-start | bytes 524288 | tf_op jit(solution)/shard_map/all_to_all | solution.py:567
  31.8 0.0 collective-permute-done.1.across
  31.8 4.7 %collective-permute-start.2 = (f32[2,2,2,32,128]{4,3,2,1,0:T(8,128)S(1)}, f32[2,2,2,32,128]{4,3,2,1,0:T(8,128)S(1)}, u32[]{:S(2)}, u32[]{:S(2)}) collective-permute-start(f32[2,2,2,32,128]{4,3,2,1,0:T(8,128)S(1)} %get-tuple-element.14), channel_id=1, source_target_pairs={{0,2},{1,3},{2,32},{3,33},{32,34},{33,35},{34,0},{35,1},{4,6},{5,7... | collective-permute-start | bytes 393224 | tf_op jit(solution)/shard_map/ppermute | solution.py:577
  36.6 3.2 %collective-permute-start.3 = (f32[2,2,2,32,128]{4,3,2,1,0:T(8,128)S(1)}, f32[2,2,2,32,128]{4,3,2,1,0:T(8,128)S(1)}, u32[]{:S(2)}, u32[]{:S(2)}) collective-permute-start(f32[2,2,2,32,128]{4,3,2,1,0:T(8,128)S(1)} %get-tuple-element.15), channel_id=1, source_target_pairs={{0,34},{1,35},{2,0},{3,1},{32,2},{33,3},{34,32},{35,33},{4,38},{5,... | collective-permute-start | bytes 393224 | tf_op jit(solution)/shard_map/ppermute | solution.py:578
  39.8 3.2 %all-to-all-done.1 = f32[16,32,128]{2,1,0:T(8,128)S(1)} async-done(((f32[16,32,128]{2,1,0:T(8,128)}), f32[16,32,128]{2,1,0:T(8,128)S(1)}, u32[]{:S(2)}, u32[]{:S(2)}) %all-to-all-start.1) | async-done | bytes 262176 | tf_op jit(solution)/shard_map/all_to_all | solution.py:567
  43.0 1.9 %collective-permute-start = (f32[8,32,128]{2,1,0:T(8,128)S(1)}, f32[8,32,128]{2,1,0:T(8,128)S(1)}, u32[]{:S(2)}, u32[]{:S(2)}) collective-permute-start(f32[8,32,128]{2,1,0:T(8,128)S(1)} %pick.1.edge), channel_id=1, source_target_pairs={{16,64},{80,128},{144,192},{208,256},{272,320},{336,384},{400,448}... | collective-permute-start | bytes 393224 | tf_op jit(solution)/shard_map/ppermute | solution.py:584
  44.9 4.8 %collective-permute-start.4 = (f32[2,8,32,128]{3,2,1,0:T(8,128)S(1)}, f32[2,8,32,128]{3,2,1,0:T(8,128)S(1)}, u32[]{:S(2)}, u32[]{:S(2)}) collective-permute-start(f32[2,8,32,128]{3,2,1,0:T(8,128)S(1)} %bitcast.6), channel_id=1, source_target_pairs={{0,16},{16,0},{1,17},{17,1},{2,18},{18,2},{3,19},{19,3},{4,20},{20... | collective-permute-start | bytes 786440 | tf_op jit(solution)/shard_map/ppermute | solution.py:585
  49.7 0.0 collective-permute-done.2.plus
  49.7 0.0 collective-permute-done.3.minus
  49.7 0.0 copy-done.7
  49.8 0.3 prepare.1.omegas
  50.1 0.0 collective-permute-done.beyond
  50.1 0.5 beyond.2.part
  50.6 0.3 collective-permute-done.4.partner
  50.9 0.5 near.1.edge
  51.3 1.9 %collective-permute-start.5 = (f32[8,32,128]{2,1,0:T(8,128)S(1)}, f32[8,32,128]{2,1,0:T(8,128)S(1)}, u32[]{:S(2)}, u32[]{:S(2)}) collective-permute-start(f32[8,32,128]{2,1,0:T(8,128)S(1)} %near.1.edge), channel_id=1, source_target_pairs={{16,64},{80,128},{144,192},{208,256},{272,320},{336,384},{400,448}... | collective-permute-start | bytes 393224 | tf_op jit(solution)/shard_map/ppermute | solution.py:584
  53.3 0.8 rest.1.own
  54.1 4.9 %collective-permute-start.6 = (f32[2,8,32,128]{3,2,1,0:T(8,128)S(1)}, f32[2,8,32,128]{3,2,1,0:T(8,128)S(1)}, u32[]{:S(2)}, u32[]{:S(2)}) collective-permute-start(f32[2,8,32,128]{3,2,1,0:T(8,128)S(1)} %rest.1.own), channel_id=1, source_target_pairs={{0,16},{16,0},{1,17},{17,1},{2,18},{18,2},{3,19},{19,3},{4,20},{20... | collective-permute-start | bytes 786440 | tf_op jit(solution)/shard_map/ppermute | solution.py:585
  59.0 0.0 collective-permute-done.5.beyond
  59.0 0.5 beyond.3.part
  59.4 0.7 collective-permute-done.6.partner
  60.1 1.2 %filter.1 = f32[2,8,32,128]{3,2,1,0:T(8,128)S(1)} custom-call(f32[8,32,128]{2,1,0:T(8,128)S(1)} %beyond.3.part, f32[2,8,32,128]{3,2,1,0:T(8,128)S(1)} %rest.1.own, f32[2,8,32,128]{3,2,1,0:T(8,128)S(1)} %collective-permute-done.6.partner, f32[2,4,128,128]{3,2,1,0:T(8,128)S(1)} %prepare.1.omegas), custom_call_target="tpu_custom_call" | custom-call | tf_op jit(solution)/shard_map/filter/pallas_call | solution.py:553
  61.4 0.0 copy-start.2
  61.4 0.0 copy-start.3
  61.4 15.8 %all_to_all.20.blocks = f32[16,32,128]{2,1,0:T(8,128)S(1)} all-to-all(f32[16,32,128]{2,1,0:T(8,128)S(1)} %bitcast.9), channel_id=1, replica_groups=mesh['y'=8,'zh'=2,'c'=2,'xq'=2,'xr'=2,'zl'=4] {'zh','xr','zl'}, dimensions={0} | all-to-all | bytes 524288 | tf_op jit(solution)/shard_map/all_to_all | solution.py:567
  77.2 0.0 copy-done.2
  77.2 0.0 copy-done.3
  77.2 0.6 inverse.1
  77.8 15.2 %all_to_all.21.blocks = f32[16,32,128]{2,1,0:T(8,128)S(1)} all-to-all(f32[16,32,128]{2,1,0:T(8,128)S(1)} %inverse.1), channel_id=1, replica_groups=mesh['y'=8,'zh'=2,'c'=2,'xq'=2,'xr'=2,'zl'=4] {'xq','xr','zl'}, dimensions={0} | all-to-all | bytes 524288 | tf_op jit(solution)/shard_map/all_to_all | solution.py:567
  93.1 0.8 receive.1
  (3 shorter events, 0.0 us)
Async XLA Ops:
  0.0 0.9 %copy-start = (f32[128,4,128]{2,1,0:T(4,128)S(1)}, f32[128,4,128]{2,1,0:T(4,128)}, u32[]{:S(2)}) copy-start(f32[128,4,128]{2,1,0:T(4,128)} %param.9) | copy-start | bytes 786436
  1.0 10.8 %copy-start.8 = (s32[4,128]{1,0:T(4,128)S(1)}, s32[4,128]{1,0:T(4,128)}, u32[]{:S(2)}) copy-start(s32[4,128]{1,0:T(4,128)} %live.3) | copy-start | bytes 6148
  1.0 21.7 %copy-start.6 = (f32[2,8,128]{2,1,0:T(8,128)S(1)}, f32[2,8,128]{2,1,0:T(8,128)}, u32[]{:S(2)}) copy-start(f32[2,8,128]{2,1,0:T(8,128)} %constant.17.clone.turns) | copy-start | bytes 24580
  1.8 10.0 %copy-start.1 = (f32[2,64,4,128]{3,2,1,0:T(4,128)S(1)}, f32[2,64,4,128]{3,2,1,0:T(4,128)}, u32[]{:S(2)}) copy-start(f32[2,64,4,128]{3,2,1,0:T(4,128)} %param.10) | copy-start | bytes 786436
  1.8 20.9 %copy-start.5 = (bf16[2,256,256]{2,1,0:T(8,128)(2,1)S(1)}, bf16[2,256,256]{2,1,0:T(8,128)(2,1)}, u32[]{:S(2)}) copy-start(bf16[2,256,256]{2,1,0:T(8,128)(2,1)} %constant.13.clone.low) | copy-start | bytes 786436
  1.8 20.9 %all-to-all-start = ((f32[16,32,128]{2,1,0:T(8,128)}), f32[16,32,128]{2,1,0:T(8,128)S(1)}, u32[]{:S(2)}, u32[]{:S(2)}) async-start(f32[16,32,128]{2,1,0:T(8,128)} %send.1), calls=%async_computation | async-start | bytes 524288 | tf_op jit(solution)/shard_map/all_to_all | solution.py:567
  11.8 10.9 %copy-start.4 = (bf16[2,256,256]{2,1,0:T(8,128)(2,1)S(1)}, bf16[2,256,256]{2,1,0:T(8,128)(2,1)}, u32[]{:S(2)}) copy-start(bf16[2,256,256]{2,1,0:T(8,128)(2,1)} %constant.12.clone.high) | copy-start | bytes 786436
  12.1 19.7 %collective-permute-start.1 = (f32[2,2,64,128]{3,2,1,0:T(8,128)S(1)}, f32[2,2,64,128]{3,2,1,0:T(8,128)S(1)}, u32[]{:S(2)}, u32[]{:S(2)}) collective-permute-start(f32[2,2,64,128]{3,2,1,0:T(8,128)S(1)} %get-tuple-element.13), channel_id=1, source_target_pairs={{0,12},{4,8},{8,4},{12,0},{1,13},{5,9},{9,5},{13,1},{2,14},{6,10},... | collective-permute-start | bytes 393224 | tf_op jit(solution)/shard_map/ppermute | solution.py:575
  24.1 18.9 %all-to-all-start.1 = ((f32[16,32,128]{2,1,0:T(8,128)}), f32[16,32,128]{2,1,0:T(8,128)S(1)}, u32[]{:S(2)}, u32[]{:S(2)}) async-start(f32[16,32,128]{2,1,0:T(8,128)} %forward.1), calls=%async_computation.1 | async-start | bytes 524288 | tf_op jit(solution)/shard_map/all_to_all | solution.py:567
  31.8 17.9 %collective-permute-start.2 = (f32[2,2,2,32,128]{4,3,2,1,0:T(8,128)S(1)}, f32[2,2,2,32,128]{4,3,2,1,0:T(8,128)S(1)}, u32[]{:S(2)}, u32[]{:S(2)}) collective-permute-start(f32[2,2,2,32,128]{4,3,2,1,0:T(8,128)S(1)} %get-tuple-element.14), channel_id=1, source_target_pairs={{0,2},{1,3},{2,32},{3,33},{32,34},{33,35},{34,0},{35,1},{4,6},{5,7... | collective-permute-start | bytes 393224 | tf_op jit(solution)/shard_map/ppermute | solution.py:577
  36.6 13.2 %collective-permute-start.3 = (f32[2,2,2,32,128]{4,3,2,1,0:T(8,128)S(1)}, f32[2,2,2,32,128]{4,3,2,1,0:T(8,128)S(1)}, u32[]{:S(2)}, u32[]{:S(2)}) collective-permute-start(f32[2,2,2,32,128]{4,3,2,1,0:T(8,128)S(1)} %get-tuple-element.15), channel_id=1, source_target_pairs={{0,34},{1,35},{2,0},{3,1},{32,2},{33,3},{34,32},{35,33},{4,38},{5,... | collective-permute-start | bytes 393224 | tf_op jit(solution)/shard_map/ppermute | solution.py:578
  43.0 6.8 %copy-start.7 = (bf16[64,128]{1,0:T(8,128)(2,1)S(1)}, bf16[64,128]{1,0:T(8,128)(2,1)}, u32[]{:S(2)}) copy-start(bf16[64,128]{1,0:T(8,128)(2,1)} %constant.16.clone.spread) | copy-start | bytes 49156
  43.0 7.1 %collective-permute-start = (f32[8,32,128]{2,1,0:T(8,128)S(1)}, f32[8,32,128]{2,1,0:T(8,128)S(1)}, u32[]{:S(2)}, u32[]{:S(2)}) collective-permute-start(f32[8,32,128]{2,1,0:T(8,128)S(1)} %pick.1.edge), channel_id=1, source_target_pairs={{16,64},{80,128},{144,192},{208,256},{272,320},{336,384},{400,448}... | collective-permute-start | bytes 393224 | tf_op jit(solution)/shard_map/ppermute | solution.py:584
  44.9 5.9 %collective-permute-start.4 = (f32[2,8,32,128]{3,2,1,0:T(8,128)S(1)}, f32[2,8,32,128]{3,2,1,0:T(8,128)S(1)}, u32[]{:S(2)}, u32[]{:S(2)}) collective-permute-start(f32[2,8,32,128]{3,2,1,0:T(8,128)S(1)} %bitcast.6), channel_id=1, source_target_pairs={{0,16},{16,0},{1,17},{17,1},{2,18},{18,2},{3,19},{19,3},{4,20},{20... | collective-permute-start | bytes 786440 | tf_op jit(solution)/shard_map/ppermute | solution.py:585
  51.3 7.6 %collective-permute-start.5 = (f32[8,32,128]{2,1,0:T(8,128)S(1)}, f32[8,32,128]{2,1,0:T(8,128)S(1)}, u32[]{:S(2)}, u32[]{:S(2)}) collective-permute-start(f32[8,32,128]{2,1,0:T(8,128)S(1)} %near.1.edge), channel_id=1, source_target_pairs={{16,64},{80,128},{144,192},{208,256},{272,320},{336,384},{400,448}... | collective-permute-start | bytes 393224 | tf_op jit(solution)/shard_map/ppermute | solution.py:584
  54.1 6.0 %collective-permute-start.6 = (f32[2,8,32,128]{3,2,1,0:T(8,128)S(1)}, f32[2,8,32,128]{3,2,1,0:T(8,128)S(1)}, u32[]{:S(2)}, u32[]{:S(2)}) collective-permute-start(f32[2,8,32,128]{3,2,1,0:T(8,128)S(1)} %rest.1.own), channel_id=1, source_target_pairs={{0,16},{16,0},{1,17},{17,1},{2,18},{18,2},{3,19},{19,3},{4,20},{20... | collective-permute-start | bytes 786440 | tf_op jit(solution)/shard_map/ppermute | solution.py:585
  61.4 15.8 %copy-start.2 = (bf16[2,256,256]{2,1,0:T(8,128)(2,1)S(1)}, bf16[2,256,256]{2,1,0:T(8,128)(2,1)}, u32[]{:S(2)}) copy-start(bf16[2,256,256]{2,1,0:T(8,128)(2,1)} %constant.14.clone.high) | copy-start | bytes 786436
  61.4 15.8 %copy-start.3 = (bf16[2,256,256]{2,1,0:T(8,128)(2,1)S(1)}, bf16[2,256,256]{2,1,0:T(8,128)(2,1)}, u32[]{:S(2)}) copy-start(bf16[2,256,256]{2,1,0:T(8,128)(2,1)} %constant.15.clone.low) | copy-start | bytes 786436

commit v10 on v8

--- a/solution.py
+++ b/solution.py
@@ -149,11 +149,10 @@
 
 
 def split_dot(lhs, high, low):
-    rows = lhs.shape[0]
     top = lhs.astype(bf16)
     rest = (lhs - top.astype(f32)).astype(bf16)
-    both = jnp.dot(jnp.concatenate([top, rest], axis=0), high, preferred_element_type=f32)
-    return both[:rows] + both[rows:] + jnp.dot(top, low, preferred_element_type=f32)
+    table = jnp.concatenate([high, high, low], axis=0)
+    return jnp.dot(jnp.concatenate([top, rest, top], axis=1), table, preferred_element_type=f32)
 
 
 def swap_blocks(arrays, lane, width):

time: 94.4 us -> 94.4 us (level)
  no operation moved by 1% of the time
where the time goes in v10:
time: 94.4 us; the launch traced here: 93.8 us
  starting transfers between devices  44.2 us (47%)
  blocking collectives  31 us (33%)
  waiting for transfers between devices  9.62 us (10%)
  Pallas kernels  7.76 us (8%)
  local copies, waits for them, and re-layouts  0.99 us (1%)
    all_to_all x2, blocking collectives, exchange(): return lax.all_to_all(blocks, axes, 0, 0, tiled=True)  31 us
    all_to_all x2, starting transfers between devices, exchange(): return lax.all_to_all(blocks, axes, 0, 0, tiled=True)  17.7 us
    ppermute x2, starting transfers between devices, local(): partner = lax.ppermute(block, 'c', swap)  9.7 us
    all_to_all x2, waiting for transfers between devices, exchange(): return lax.all_to_all(blocks, axes, 0, 0, tiled=True)  8.65 us
    ppermute x1, starting transfers between devices, local(): lax.ppermute(across, ('xq', 'xr'), [(i, WINDOWS - 1 - i) for i in range(W...  5.05 us
    ppermute x1, starting transfers between devices, local(): lax.ppermute(plus, ('zh', 'zl'), [(z, (z + 2) % 8) for z in range(8)])  4.73 us
    ppermute x2, starting transfers between devices, local(): beyond = lax.ppermute(edge, ('y', 'c'), shift)  3.84 us
    ppermute x1, starting transfers between devices, local(): lax.ppermute(minus, ('zh', 'zl'), [(z, (z - 2) % 8) for z in range(8)])  3.22 us
  transfers between devices with their start and end apart: 9, of which 4 were waited for; matrix products, arithmetic and copies ran while one was open for 0% of the time, Pallas kernels for 3%

profile of v10, /device:TPU:24, one launch (start us, length us, event | category | flops | bytes accessed | tf_op | source)
XLA Modules:
  0.0 93.8 jit_solution(9805130191785065168)
XLA Ops:
  0.0 0.0 copy-start
  0.0 0.9 %copy-done = f32[128,4,128]{2,1,0:T(4,128)S(1)} copy-done((f32[128,4,128]{2,1,0:T(4,128)S(1)}, f32[128,4,128]{2,1,0:T(4,128)}, u32[]{:S(2)}) %copy-start) | copy-done | bytes 262168
  1.0 0.0 copy-start.8
  1.0 0.0 copy-start.6
  1.0 0.8 send.1
  1.8 0.0 copy-start.1
  1.8 0.0 copy-start.5
  1.8 10.0 %all-to-all-start = ((f32[16,32,128]{2,1,0:T(8,128)}), f32[16,32,128]{2,1,0:T(8,128)S(1)}, u32[]{:S(2)}, u32[]{:S(2)}) async-start(f32[16,32,128]{2,1,0:T(8,128)} %send.1), calls=%async_computation | async-start | bytes 524288 | tf_op jit(solution)/shard_map/all_to_all | solution.py:543
  11.8 0.0 copy-start.4
  11.8 0.0 copy-done.8
  11.8 0.0 copy-done.1
  11.8 0.3 windows.1
  12.1 5.0 %collective-permute-start.1 = (f32[2,2,64,128]{3,2,1,0:T(8,128)S(1)}, f32[2,2,64,128]{3,2,1,0:T(8,128)S(1)}, u32[]{:S(2)}, u32[]{:S(2)}) collective-permute-start(f32[2,2,64,128]{3,2,1,0:T(8,128)S(1)} %get-tuple-element.15), channel_id=1, source_target_pairs={{0,12},{4,8},{8,4},{12,0},{1,13},{5,9},{9,5},{13,1},{2,14},{6,10},... | collective-permute-start | bytes 393224 | tf_op jit(solution)/shard_map/ppermute | solution.py:551
  17.2 5.5 %all-to-all-done.blocks = f32[16,32,128]{2,1,0:T(8,128)S(1)} async-done(((f32[16,32,128]{2,1,0:T(8,128)}), f32[16,32,128]{2,1,0:T(8,128)S(1)}, u32[]{:S(2)}, u32[]{:S(2)}) %all-to-all-start) | async-done | bytes 262176 | tf_op jit(solution)/shard_map/all_to_all | solution.py:543
  22.6 0.0 copy-done.6
  22.7 0.0 copy-done.5
  22.7 0.0 copy-done.4
  22.7 1.4 %forward.1 = f32[16,32,128]{2,1,0:T(8,128)} custom-call(f32[16,32,128]{2,1,0:T(8,128)S(1)} %all-to-all-done.blocks, s32[4,128]{1,0:T(4,128)S(1)} %copy-done.8, bf16[2,256,256]{2,1,0:T(8,128)(2,1)S(1)} %copy-done.5, bf16[2,256,256]{2,1,0:T(8,128)(2,1)S(1)} %copy-done.4, f32[2,8,128]{2,1,0:T(8,128)S(1)} %copy-done.6), custom_call_target="tpu_custom_call" | custom-call | tf_op jit(solution)/shard_map/forward/pallas_call | solution.py:483
  24.1 7.7 %all-to-all-start.1 = ((f32[16,32,128]{2,1,0:T(8,128)}), f32[16,32,128]{2,1,0:T(8,128)S(1)}, u32[]{:S(2)}, u32[]{:S(2)}) async-start(f32[16,32,128]{2,1,0:T(8,128)} %forward.1), calls=%async_computation.1 | async-start | bytes 524288 | tf_op jit(solution)/shard_map/all_to_all | solution.py:543
  31.8 0.0 collective-permute-done.1.across
  31.8 4.7 %collective-permute-start.2 = (f32[2,2,2,32,128]{4,3,2,1,0:T(8,128)S(1)}, f32[2,2,2,32,128]{4,3,2,1,0:T(8,128)S(1)}, u32[]{:S(2)}, u32[]{:S(2)}) collective-permute-start(f32[2,2,2,32,128]{4,3,2,1,0:T(8,128)S(1)} %get-tuple-element.16), channel_id=1, source_target_pairs={{0,2},{1,3},{2,32},{3,33},{32,34},{33,35},{34,0},{35,1},{4,6},{5,7... | collective-permute-start | bytes 393224 | tf_op jit(solution)/shard_map/ppermute | solution.py:553
  36.6 3.2 %collective-permute-start.3 = (f32[2,2,2,32,128]{4,3,2,1,0:T(8,128)S(1)}, f32[2,2,2,32,128]{4,3,2,1,0:T(8,128)S(1)}, u32[]{:S(2)}, u32[]{:S(2)}) collective-permute-start(f32[2,2,2,32,128]{4,3,2,1,0:T(8,128)S(1)} %get-tuple-element.17), channel_id=1, source_target_pairs={{0,34},{1,35},{2,0},{3,1},{32,2},{33,3},{34,32},{35,33},{4,38},{5,... | collective-permute-start | bytes 393224 | tf_op jit(solution)/shard_map/ppermute | solution.py:554
  39.8 3.2 %all-to-all-done.1 = f32[16,32,128]{2,1,0:T(8,128)S(1)} async-done(((f32[16,32,128]{2,1,0:T(8,128)}), f32[16,32,128]{2,1,0:T(8,128)S(1)}, u32[]{:S(2)}, u32[]{:S(2)}) %all-to-all-start.1) | async-done | bytes 262176 | tf_op jit(solution)/shard_map/all_to_all | solution.py:543
  43.0 0.0 copy-start.7
  43.0 1.9 %collective-permute-start = (f32[8,32,128]{2,1,0:T(8,128)S(1)}, f32[8,32,128]{2,1,0:T(8,128)S(1)}, u32[]{:S(2)}, u32[]{:S(2)}) collective-permute-start(f32[8,32,128]{2,1,0:T(8,128)S(1)} %pick.1.edge), channel_id=1, source_target_pairs={{16,64},{80,128},{144,192},{208,256},{272,320},{336,384},{400,448}... | collective-permute-start | bytes 393224 | tf_op jit(solution)/shard_map/ppermute | solution.py:560
  44.9 4.8 %collective-permute-start.4 = (f32[2,8,32,128]{3,2,1,0:T(8,128)S(1)}, f32[2,8,32,128]{3,2,1,0:T(8,128)S(1)}, u32[]{:S(2)}, u32[]{:S(2)}) collective-permute-start(f32[2,8,32,128]{3,2,1,0:T(8,128)S(1)} %bitcast.6), channel_id=1, source_target_pairs={{0,16},{16,0},{1,17},{17,1},{2,18},{18,2},{3,19},{19,3},{4,20},{20... | collective-permute-start | bytes 786440 | tf_op jit(solution)/shard_map/ppermute | solution.py:561
  49.7 0.0 collective-permute-done.2.plus
  49.7 0.0 collective-permute-done.3.minus
  49.7 0.0 copy-done.7
  49.8 0.3 prepare.1.omegas
  50.1 0.0 collective-permute-done.beyond
  50.1 0.5 beyond.2.part
  50.6 0.3 collective-permute-done.4.partner
  50.9 1.1 %filter.2 = (f32[2,8,32,128]{3,2,1,0:T(8,128)S(1)}, f32[8,32,128]{2,1,0:T(8,128)S(1)}) custom-call(f32[8,32,128]{2,1,0:T(8,128)S(1)} %beyond.2.part, f32[2,8,32,128]{3,2,1,0:T(8,128)S(1)} %bitcast.7, f32[2,8,32,128]{3,2,1,0:T(8,128)S(1)} %collective-permute-done.4.partner, f32[2,4,128,128]{3,2,1,0:T(8,128)S(1)} %prepare.1.omegas), custom_call_target="tpu_custom_call" | custom-call | tf_op jit(solution)/shard_map/filter/pallas_call | solution.py:529
  52.0 1.9 %collective-permute-start.5 = (f32[8,32,128]{2,1,0:T(8,128)S(1)}, f32[8,32,128]{2,1,0:T(8,128)S(1)}, u32[]{:S(2)}, u32[]{:S(2)}) collective-permute-start(f32[8,32,128]{2,1,0:T(8,128)S(1)} %get-tuple-element.21.edge), channel_id=1, source_target_pairs={{16,64},{80,128},{144,192},{208,256},{272,320},{336,384},{400,448}... | collective-permute-start | bytes 393224 | tf_op jit(solution)/shard_map/ppermute | solution.py:560
  53.9 4.9 %collective-permute-start.6 = (f32[2,8,32,128]{3,2,1,0:T(8,128)S(1)}, f32[2,8,32,128]{3,2,1,0:T(8,128)S(1)}, u32[]{:S(2)}, u32[]{:S(2)}) collective-permute-start(f32[2,8,32,128]{3,2,1,0:T(8,128)S(1)} %get-tuple-element.22.own), channel_id=1, source_target_pairs={{0,16},{16,0},{1,17},{17,1},{2,18},{18,2},{3,19},{19,3},{4,20},{20... | collective-permute-start | bytes 786440 | tf_op jit(solution)/shard_map/ppermute | solution.py:561
  58.9 0.0 collective-permute-done.5.beyond
  58.9 0.5 beyond.3.part
  59.3 0.7 collective-permute-done.6.partner
  60.0 1.2 %filter.3 = f32[2,8,32,128]{3,2,1,0:T(8,128)S(1)} custom-call(f32[8,32,128]{2,1,0:T(8,128)S(1)} %beyond.3.part, f32[2,8,32,128]{3,2,1,0:T(8,128)S(1)} %get-tuple-element.22.own, f32[2,8,32,128]{3,2,1,0:T(8,128)S(1)} %collective-permute-done.6.partner, f32[2,4,128,128]{3,2,1,0:T(8,128)S(1)} %prepare.1.omegas), custom_call_target="tpu_custom_call" | custom-call | tf_op jit(solution)/shard_map/filter/pallas_call | solution.py:529
  61.2 0.0 copy-start.2
  61.2 0.0 copy-start.3
  61.3 15.8 %all_to_all.20.blocks = f32[16,32,128]{2,1,0:T(8,128)S(1)} all-to-all(f32[16,32,128]{2,1,0:T(8,128)S(1)} %bitcast.8), channel_id=1, replica_groups=mesh['y'=8,'zh'=2,'c'=2,'xq'=2,'xr'=2,'zl'=4] {'zh','xr','zl'}, dimensions={0} | all-to-all | bytes 524288 | tf_op jit(solution)/shard_map/all_to_all | solution.py:543
  77.1 0.0 copy-done.2
  77.1 0.0 copy-done.3
  77.1 0.7 inverse.1
  77.7 15.2 %all_to_all.21.blocks = f32[16,32,128]{2,1,0:T(8,128)S(1)} all-to-all(f32[16,32,128]{2,1,0:T(8,128)S(1)} %inverse.1), channel_id=1, replica_groups=mesh['y'=8,'zh'=2,'c'=2,'xq'=2,'xr'=2,'zl'=4] {'xq','xr','zl'}, dimensions={0} | all-to-all | bytes 524288 | tf_op jit(solution)/shard_map/all_to_all | solution.py:543
  93.0 0.8 receive.1
  (2 shorter events, 0.0 us)
Async XLA Ops:
  0.0 0.9 %copy-start = (f32[128,4,128]{2,1,0:T(4,128)S(1)}, f32[128,4,128]{2,1,0:T(4,128)}, u32[]{:S(2)}) copy-start(f32[128,4,128]{2,1,0:T(4,128)} %param.9) | copy-start | bytes 786436
  1.0 10.8 %copy-start.8 = (s32[4,128]{1,0:T(4,128)S(1)}, s32[4,128]{1,0:T(4,128)}, u32[]{:S(2)}) copy-start(s32[4,128]{1,0:T(4,128)} %live.3) | copy-start | bytes 6148
  1.0 21.7 %copy-start.6 = (f32[2,8,128]{2,1,0:T(8,128)S(1)}, f32[2,8,128]{2,1,0:T(8,128)}, u32[]{:S(2)}) copy-start(f32[2,8,128]{2,1,0:T(8,128)} %constant.17.clone.turns) | copy-start | bytes 24580
  1.8 10.0 %copy-start.1 = (f32[2,64,4,128]{3,2,1,0:T(4,128)S(1)}, f32[2,64,4,128]{3,2,1,0:T(4,128)}, u32[]{:S(2)}) copy-start(f32[2,64,4,128]{3,2,1,0:T(4,128)} %param.10) | copy-start | bytes 786436
  1.8 20.9 %copy-start.5 = (bf16[2,256,256]{2,1,0:T(8,128)(2,1)S(1)}, bf16[2,256,256]{2,1,0:T(8,128)(2,1)}, u32[]{:S(2)}) copy-start(bf16[2,256,256]{2,1,0:T(8,128)(2,1)} %constant.12.clone.high) | copy-start | bytes 786436
  1.8 20.9 %all-to-all-start = ((f32[16,32,128]{2,1,0:T(8,128)}), f32[16,32,128]{2,1,0:T(8,128)S(1)}, u32[]{:S(2)}, u32[]{:S(2)}) async-start(f32[16,32,128]{2,1,0:T(8,128)} %send.1), calls=%async_computation | async-start | bytes 524288 | tf_op jit(solution)/shard_map/all_to_all | solution.py:543
  11.8 10.9 %copy-start.4 = (bf16[2,256,256]{2,1,0:T(8,128)(2,1)S(1)}, bf16[2,256,256]{2,1,0:T(8,128)(2,1)}, u32[]{:S(2)}) copy-start(bf16[2,256,256]{2,1,0:T(8,128)(2,1)} %constant.13.clone.low) | copy-start | bytes 786436
  12.1 19.7 %collective-permute-start.1 = (f32[2,2,64,128]{3,2,1,0:T(8,128)S(1)}, f32[2,2,64,128]{3,2,1,0:T(8,128)S(1)}, u32[]{:S(2)}, u32[]{:S(2)}) collective-permute-start(f32[2,2,64,128]{3,2,1,0:T(8,128)S(1)} %get-tuple-element.15), channel_id=1, source_target_pairs={{0,12},{4,8},{8,4},{12,0},{1,13},{5,9},{9,5},{13,1},{2,14},{6,10},... | collective-permute-start | bytes 393224 | tf_op jit(solution)/shard_map/ppermute | solution.py:551
  24.1 18.9 %all-to-all-start.1 = ((f32[16,32,128]{2,1,0:T(8,128)}), f32[16,32,128]{2,1,0:T(8,128)S(1)}, u32[]{:S(2)}, u32[]{:S(2)}) async-start(f32[16,32,128]{2,1,0:T(8,128)} %forward.1), calls=%async_computation.1 | async-start | bytes 524288 | tf_op jit(solution)/shard_map/all_to_all | solution.py:543
  31.8 17.9 %collective-permute-start.2 = (f32[2,2,2,32,128]{4,3,2,1,0:T(8,128)S(1)}, f32[2,2,2,32,128]{4,3,2,1,0:T(8,128)S(1)}, u32[]{:S(2)}, u32[]{:S(2)}) collective-permute-start(f32[2,2,2,32,128]{4,3,2,1,0:T(8,128)S(1)} %get-tuple-element.16), channel_id=1, source_target_pairs={{0,2},{1,3},{2,32},{3,33},{32,34},{33,35},{34,0},{35,1},{4,6},{5,7... | collective-permute-start | bytes 393224 | tf_op jit(solution)/shard_map/ppermute | solution.py:553
  36.6 13.2 %collective-permute-start.3 = (f32[2,2,2,32,128]{4,3,2,1,0:T(8,128)S(1)}, f32[2,2,2,32,128]{4,3,2,1,0:T(8,128)S(1)}, u32[]{:S(2)}, u32[]{:S(2)}) collective-permute-start(f32[2,2,2,32,128]{4,3,2,1,0:T(8,128)S(1)} %get-tuple-element.17), channel_id=1, source_target_pairs={{0,34},{1,35},{2,0},{3,1},{32,2},{33,3},{34,32},{35,33},{4,38},{5,... | collective-permute-start | bytes 393224 | tf_op jit(solution)/shard_map/ppermute | solution.py:554
  43.0 6.8 %copy-start.7 = (bf16[64,128]{1,0:T(8,128)(2,1)S(1)}, bf16[64,128]{1,0:T(8,128)(2,1)}, u32[]{:S(2)}) copy-start(bf16[64,128]{1,0:T(8,128)(2,1)} %constant.16.clone.spread) | copy-start | bytes 49156
  43.0 7.1 %collective-permute-start = (f32[8,32,128]{2,1,0:T(8,128)S(1)}, f32[8,32,128]{2,1,0:T(8,128)S(1)}, u32[]{:S(2)}, u32[]{:S(2)}) collective-permute-start(f32[8,32,128]{2,1,0:T(8,128)S(1)} %pick.1.edge), channel_id=1, source_target_pairs={{16,64},{80,128},{144,192},{208,256},{272,320},{336,384},{400,448}... | collective-permute-start | bytes 393224 | tf_op jit(solution)/shard_map/ppermute | solution.py:560
  44.9 5.9 %collective-permute-start.4 = (f32[2,8,32,128]{3,2,1,0:T(8,128)S(1)}, f32[2,8,32,128]{3,2,1,0:T(8,128)S(1)}, u32[]{:S(2)}, u32[]{:S(2)}) collective-permute-start(f32[2,8,32,128]{3,2,1,0:T(8,128)S(1)} %bitcast.6), channel_id=1, source_target_pairs={{0,16},{16,0},{1,17},{17,1},{2,18},{18,2},{3,19},{19,3},{4,20},{20... | collective-permute-start | bytes 786440 | tf_op jit(solution)/shard_map/ppermute | solution.py:561
  52.0 6.8 %collective-permute-start.5 = (f32[8,32,128]{2,1,0:T(8,128)S(1)}, f32[8,32,128]{2,1,0:T(8,128)S(1)}, u32[]{:S(2)}, u32[]{:S(2)}) collective-permute-start(f32[8,32,128]{2,1,0:T(8,128)S(1)} %get-tuple-element.21.edge), channel_id=1, source_target_pairs={{16,64},{80,128},{144,192},{208,256},{272,320},{336,384},{400,448}... | collective-permute-start | bytes 393224 | tf_op jit(solution)/shard_map/ppermute | solution.py:560
  53.9 6.0 %collective-permute-start.6 = (f32[2,8,32,128]{3,2,1,0:T(8,128)S(1)}, f32[2,8,32,128]{3,2,1,0:T(8,128)S(1)}, u32[]{:S(2)}, u32[]{:S(2)}) collective-permute-start(f32[2,8,32,128]{3,2,1,0:T(8,128)S(1)} %get-tuple-element.22.own), channel_id=1, source_target_pairs={{0,16},{16,0},{1,17},{17,1},{2,18},{18,2},{3,19},{19,3},{4,20},{20... | collective-permute-start | bytes 786440 | tf_op jit(solution)/shard_map/ppermute | solution.py:561
  61.2 15.8 %copy-start.2 = (bf16[2,256,256]{2,1,0:T(8,128)(2,1)S(1)}, bf16[2,256,256]{2,1,0:T(8,128)(2,1)}, u32[]{:S(2)}) copy-start(bf16[2,256,256]{2,1,0:T(8,128)(2,1)} %constant.15.clone.low) | copy-start | bytes 786436
  61.2 15.8 %copy-start.3 = (bf16[2,256,256]{2,1,0:T(8,128)(2,1)S(1)}, bf16[2,256,256]{2,1,0:T(8,128)(2,1)}, u32[]{:S(2)}) copy-start(bf16[2,256,256]{2,1,0:T(8,128)(2,1)} %constant.14.clone.high) | copy-start | bytes 786436
